TPU v7x, 32 devices: a whole 2x2x4 slice. The times are simulated.
32 devices in a mesh: groups: 2 (over x), span: 16 (over z, y, core).
Axes of the slice: x: 2, y: 2, z: 4, core: 2. Of those that a mesh axis runs over, the one named last changes fastest.
Arguments:
- queries: bfloat16 [8192, 2560], P(('groups', 'span')), parts along dimension 0, may hold values from -100 to 100
- cross_queries: bfloat16 [8192, 2560], P(('groups', 'span')), parts along dimension 0, may hold values from -100 to 100
- frame_kv: bfloat16 [8192, 5120], P(('groups', 'span')), parts along dimension 0, may hold values from -7 to 7
- sink_kv: bfloat16 [32, 64, 5120], P(('groups', 'span')), parts along dimension 0, may hold values from -5 to 5
- prompt_kv: bfloat16 [4, 512, 5120], P('groups', 'span'), parts along dimension 0, may hold values from -7 to 7
- switch: int32 [8], P('groups'), parts along dimension 0, may hold values from 0 to 4
Outputs:
- self_out: bfloat16 [8192, 2560], P(('groups', 'span')), parts along dimension 0
- cross_out: bfloat16 [8192, 2560], P(('groups', 'span')), parts along dimension 0
There are 2 independent parts, one for each index of `groups`. A program takes and returns all parts, laid end to end along the dimension named above; each array names one. Nothing has to cross between parts.
All inputs are finite; a program needn't handle non-finite values.
Results may differ from a plain program's by a relative error of at most 0.006.
Values may be sent and summed in bfloat16 or wider, within the bound.
No kernel may reach another device: no remote copies, remote signals or barrier semaphores. Data moves between devices by JAX's collectives and lax.ppermute only.
A program may use at most 128 MiB of HBM per device.

v0:
```python
import math

import jax
import jax.numpy as jnp
from jax import lax
from jax.experimental import pallas as pl
from jax.experimental.pallas import tpu as pltpu
from jax.sharding import PartitionSpec as P

HEADS = 20
HDIM = 128
WIN = 4
CHUNKS = 4
PER = HEADS // CHUNKS
CW = PER * HDIM
WIDTH = HEADS * HDIM
STAT = 16
LOG_SCALE = math.log2(math.e) / math.sqrt(HDIM)
VMEM = 48 * 1024 * 1024
ANYWHERE = pl.BlockSpec(memory_space=pl.ANY)
SCALAR = pl.BlockSpec(memory_space=pltpu.SMEM)
INSIDE = pl.BlockSpec(memory_space=pltpu.VMEM)


def diagonal():
    rows = lax.broadcasted_iota(jnp.int32, (HDIM, HDIM), 0)
    cols = lax.broadcasted_iota(jnp.int32, (HDIM, HDIM), 1)
    return rows == cols


def stat_rows(column):
    eye = diagonal()
    groups = column.shape[0] // HDIM
    tops, mids, lows = [], [], []
    for group in range(groups):
        part = column[group * HDIM : (group + 1) * HDIM]
        row = jnp.sum(jnp.where(eye, part, 0.0), axis=0, keepdims=True)
        top = row.astype(jnp.bfloat16).astype(jnp.float32)
        mid = (row - top).astype(jnp.bfloat16).astype(jnp.float32)
        tops.append(top)
        mids.append(mid)
        lows.append(row - top - mid)
    used = tops + mids + lows
    used.append(jnp.zeros((STAT - len(used), HDIM), jnp.float32))
    return jnp.concatenate(used, axis=0).astype(jnp.bfloat16)


def stat_column(tile, groups):
    eye = diagonal()
    tile = tile.astype(jnp.float32)
    columns = []
    for group in range(groups):
        row = (
            tile[group : group + 1]
            + tile[groups + group : groups + group + 1]
            + tile[2 * groups + group : 2 * groups + group + 1]
        )
        columns.append(jnp.sum(jnp.where(eye, row, 0.0), axis=1, keepdims=True))
    return jnp.concatenate(columns, axis=0)


def fresh_state(query, keys, values):
    scores = lax.dot_general(
        query, keys, (((1,), (1,)), ((), ())), preferred_element_type=jnp.float32
    )
    top = jnp.max(scores, axis=1, keepdims=True)
    weights = jnp.exp2((scores - top) * LOG_SCALE).astype(jnp.bfloat16)
    beside = jnp.concatenate([values, jnp.ones_like(values)], axis=1)
    both = jnp.dot(weights, beside, preferred_element_type=jnp.float32)
    return top * LOG_SCALE, both[:, HDIM:], both[:, :HDIM]


def merge_states(states):
    if len(states) == 1:
        return states[0]
    top = states[0][0]
    for state in states[1:]:
        top = jnp.maximum(top, state[0])
    total, blended = 0.0, 0.0
    for state in states:
        factor = jnp.exp2(state[0] - top)
        total = total + state[1] * factor
        blended = blended + state[2] * factor
    return top, total, blended


def stacked(pieces):
    return pieces[0] if len(pieces) == 1 else jnp.concatenate(pieces, axis=0)


class Block:
    def __init__(self, array, row, rows, col=0):
        self.array, self.row, self.rows, self.col = array, row, rows, col


class Operands:
    def __init__(self):
        self.arrays = []

    def index(self, array):
        for at, each in enumerate(self.arrays):
            if each is array:
                return at
        self.arrays.append(array)
        return len(self.arrays) - 1


def attend(jobs, out_shape, name, after=()):
    operands = Operands()

    def located(block):
        return (operands.index(block.array), block.row, block.rows, block.col)

    plan = [
        (
            [located(q) for q in queries],
            [(located(k), located(v)) for k, v in pairs],
            [located(p) for p in parts],
            out_col,
        )
        for queries, pairs, parts, out_col in jobs
    ]
    count = len(operands.arrays)

    def kernel(*refs):
        out = refs[-1]

        def read(where, head):
            at, row, rows, col = where
            left = pl.multiple_of(col + head * HDIM, HDIM)
            return refs[at][row : row + rows, pl.ds(left, HDIM)]

        def one_job(queries, pairs, parts, out_col):
            def one_head(head, carry):
                if pairs:
                    keys = stacked([read(k, head) for k, _ in pairs])
                    values = stacked([read(v, head) for _, v in pairs])
                cols = pl.ds(pl.multiple_of((out_col or 0) + head * HDIM, HDIM), HDIM)
                for at, query in enumerate(queries):
                    frame = query[2]
                    states = []
                    if pairs:
                        states.append(fresh_state(read(query, head), keys, values))
                    for part in parts:
                        rows = read(part, head)
                        states.append(
                            (
                                stat_column(rows[frame : frame + STAT], frame // HDIM),
                                1.0,
                                rows[:frame].astype(jnp.float32),
                            )
                        )
                    top, total, blended = merge_states(states)
                    done = (blended / total).astype(jnp.bfloat16)
                    if out_col is None:
                        start = at * (frame + STAT)
                        out[start : start + frame, cols] = done
                        out[start + frame : start + frame + STAT, cols] = stat_rows(
                            top + jnp.log2(total)
                        )
                    else:
                        out[:, cols] = done
                return carry

            lax.fori_loop(0, PER, one_head, 0)

        for job in plan:
            one_job(*job)

    work = sum(
        PER * len(queries) * queries[0].rows * sum(k.rows for k, _ in pairs)
        for queries, pairs, _, _ in jobs
    )
    return pl.pallas_call(
        kernel,
        out_shape=jax.ShapeDtypeStruct(out_shape, jnp.bfloat16),
        in_specs=[INSIDE] * count + [ANYWHERE] * len(after),
        out_specs=INSIDE,
        compiler_params=pltpu.CompilerParams(vmem_limit_bytes=VMEM),
        cost_estimate=pl.CostEstimate(
            flops=4 * work * HDIM, bytes_accessed=4_000_000, transcendentals=work
        ),
        name=name,
    )(*operands.arrays, *after)


def home(queries, frame_kv, sink, after):
    frame = queries.shape[0]

    def kernel(query, key, value, sink_key, sink_value, _, out):
        for head in range(PER):
            cols = slice(head * HDIM, (head + 1) * HDIM)
            keys = jnp.concatenate([key[:, cols], sink_key[:, cols]], axis=0)
            values = jnp.concatenate([value[:, cols], sink_value[:, cols]], axis=0)
            top, total, blended = fresh_state(query[:, cols], keys, values)
            out[:frame, cols] = (blended / total).astype(jnp.bfloat16)
            out[frame:, cols] = stat_rows(top + jnp.log2(total))

    def block(array, first):
        return pl.BlockSpec((array.shape[0], CW), lambda at: (0, first + at))

    return pl.pallas_call(
        kernel,
        out_shape=jax.ShapeDtypeStruct((frame + STAT, WIDTH), jnp.bfloat16),
        grid=(CHUNKS,),
        in_specs=[
            block(queries, 0),
            block(frame_kv, 0),
            block(frame_kv, CHUNKS),
            block(sink, 0),
            block(sink, CHUNKS),
            ANYWHERE,
        ],
        out_specs=pl.BlockSpec((frame + STAT, CW), lambda at: (0, at)),
        compiler_params=pltpu.CompilerParams(vmem_limit_bytes=VMEM),
        cost_estimate=pl.CostEstimate(
            flops=4 * WIDTH * frame * (frame + sink.shape[0]),
            bytes_accessed=6_000_000,
            transcendentals=HEADS * frame * (frame + sink.shape[0]),
        ),
        name="home",
    )(queries, frame_kv, frame_kv, sink, sink, after)


def finish(queries, at_home, sinks, came, extra, sink_rows):
    frame = queries.shape[0]
    as_keys = bool(came) and len(came) == CHUNKS and bool(sinks)
    rows = 2 * frame + 2 * sink_rows
    came_rows = rows if as_keys else frame + STAT
    moved = [(each, came_rows) for each in came] + [(each, rows) for each in extra]

    def kernel(*refs):
        query, home_ref = refs[:2]
        sink_refs = refs[2 : 2 + 2 * len(sinks)]
        sources = refs[2 + 2 * len(sinks) : 2 + 2 * len(sinks) + len(moved)]
        out = refs[2 + 2 * len(sinks) + len(moved)]
        held = refs[3 + 2 * len(sinks) + len(moved) : -1]
        sems = refs[-1]
        step = pl.program_id(0)

        def copy(at):
            return pltpu.make_async_copy(
                sources[at].at[pl.ds(0, moved[at][1])],
                held[0].at[at] if at < len(came) else held[-1].at[at - len(came)],
                sems.at[at],
            )

        if moved:

            @pl.when(step == 0)
            def _():
                for at in range(len(moved)):
                    copy(at).start()

        for at in range(len(came)):

            @pl.when(step == at)
            def _():
                copy(at).wait()

        def chunk(key_places, part_place):
            for head in range(PER):
                cols = slice(head * HDIM, (head + 1) * HDIM)
                keys = [ref[:, cols] for ref in sink_refs[::2]]
                values = [ref[:, cols] for ref in sink_refs[1::2]]
                for buffer, which in key_places:
                    keys += [buffer[which, :frame, cols], buffer[which, 2 * frame : 2 * frame + sink_rows, cols]]
                    values += [buffer[which, frame : 2 * frame, cols], buffer[which, 2 * frame + sink_rows :, cols]]
                parts = [home_ref[:, cols]]
                if part_place is not None:
                    parts.append(part_place[0][part_place[1], :, cols])
                states = [fresh_state(query[:, cols], stacked(keys), stacked(values))] if keys else []
                for part in parts:
                    states.append(
                        (
                            stat_column(part[frame:], frame // HDIM),
                            1.0,
                            part[:frame].astype(jnp.float32),
                        )
                    )
                _, total, blended = merge_states(states)
                out[:, cols] = (blended / total).astype(jnp.bfloat16)

        if extra:

            @pl.when(step < len(came))
            def _():
                chunk([], (held[0], step))

            @pl.when(step == len(came))
            def _():
                for at in range(len(came), len(moved)):
                    copy(at).wait()
                chunk([(held[-1], at) for at in range(len(extra))], None)

        elif as_keys:
            chunk([(held[0], step)], None)
        elif came:
            chunk([], (held[0], step))
        else:
            chunk([], None)

    in_specs = [
        pl.BlockSpec((frame, CW), lambda at: (0, at)),
        pl.BlockSpec((frame + STAT, CW), lambda at: (0, at)),
    ]
    for _ in sinks:
        in_specs += [
            pl.BlockSpec((sink_rows, CW), lambda at: (at, 0)),
            pl.BlockSpec((sink_rows, CW), lambda at: (CHUNKS + at, 0)),
        ]
    scratch = []
    if came:
        scratch.append(pltpu.VMEM((len(came), came_rows, CW), jnp.bfloat16))
    if extra:
        scratch.append(pltpu.VMEM((len(extra), rows, CW), jnp.bfloat16))
    return pl.pallas_call(
        kernel,
        out_shape=jax.ShapeDtypeStruct(queries.shape, jnp.bfloat16),
        grid=(CHUNKS,),
        in_specs=in_specs + [ANYWHERE] * len(moved),
        out_specs=pl.BlockSpec((frame, CW), lambda at: (0, at)),
        scratch_shapes=scratch + [pltpu.SemaphoreType.DMA((max(len(moved), 1),))],
        compiler_params=pltpu.CompilerParams(vmem_limit_bytes=VMEM),
        name="finish",
    )(queries, at_home, *[each for sink in sinks for each in (sink, sink)], *[each for each, _ in moved])


def cross(queries, shards, pick, prompt_rows, after):
    frame = queries.shape[0]
    step = 2 * prompt_rows

    def kernel(pick_ref, query, *refs):
        out = refs[-1]
        picked = pick_ref[0] * prompt_rows

        def chunk(at, carry):
            def rows(ref, which):
                start = pl.multiple_of(which * step + picked, 8)
                return ref.at[pl.ds(start, prompt_rows)]

            first = pl.multiple_of(at * CW, HDIM)
            for head in range(PER):
                cols = pl.ds(head * HDIM, HDIM)
                keys = stacked([rows(ref, at)[:, cols] for ref in refs[:-2]])
                values = stacked([rows(ref, CHUNKS + at)[:, cols] for ref in refs[:-2]])
                here = pl.ds(first + head * HDIM, HDIM)
                _, total, blended = fresh_state(query[:, here], keys, values)
                out[:, here] = (blended / total).astype(jnp.bfloat16)
            return carry

        lax.fori_loop(0, CHUNKS, chunk, 0)

    work = HEADS * frame * prompt_rows * len(shards)
    return pl.pallas_call(
        kernel,
        out_shape=jax.ShapeDtypeStruct(queries.shape, jnp.bfloat16),
        in_specs=[SCALAR] + [INSIDE] * (1 + len(shards)) + [ANYWHERE],
        out_specs=INSIDE,
        compiler_params=pltpu.CompilerParams(vmem_limit_bytes=VMEM),
        cost_estimate=pl.CostEstimate(
            flops=4 * work * HDIM, bytes_accessed=12_000_000, transcendentals=work
        ),
        name="cross",
    )(pick, queries, *shards, after)


def pack(place, rows, plans, name="pack", after=()):
    operands = Operands()
    located = {
        at: [(operands.index(block.array), block, first) for block, first in items]
        for at, items in plans.items()
    }
    most = max(len(items) for items in located.values())

    def kernel(place_ref, *refs):
        out, sems = refs[-2:]
        for at, items in located.items():

            @pl.when(place_ref[0] == at)
            def _():
                copies = [
                    pltpu.make_async_copy(
                        refs[which].at[pl.ds(block.row, block.rows), pl.ds(block.col, CW)],
                        out.at[pl.ds(first, block.rows), :],
                        sems.at[n],
                    )
                    for n, (which, block, first) in enumerate(items)
                ]
                for copy in copies:
                    copy.start()
                for copy in copies:
                    copy.wait()

    return pl.pallas_call(
        kernel,
        out_shape=jax.ShapeDtypeStruct((rows, CW), jnp.bfloat16),
        in_specs=[SCALAR] + [ANYWHERE] * (len(operands.arrays) + len(after)),
        out_specs=INSIDE,
        scratch_shapes=[pltpu.SemaphoreType.DMA((most,))],
        cost_estimate=pl.CostEstimate(flops=0, bytes_accessed=2_000_000, transcendentals=0),
        name=name,
    )(place, *operands.arrays, *after)


def unused(rows, after):
    return pl.pallas_call(
        lambda _, out: None,
        out_shape=jax.ShapeDtypeStruct((rows, CW), jnp.bfloat16),
        in_specs=[ANYWHERE],
        out_specs=ANYWHERE,
        name="unused",
    )(after)


def shards(queries, cross_queries, frame_kv, sink_kv, prompt_kv, switch):
    streams = lax.axis_size("span") // WIN
    device = lax.axis_index("span")
    place = device // streams
    stream = device % streams
    frame = queries.shape[0]
    sink = sink_kv.reshape(sink_kv.shape[1], sink_kv.shape[2])
    sink_rows = sink.shape[0]
    prompt_rows = prompt_kv.shape[1]
    prompt_both = prompt_kv.reshape(2 * prompt_rows, prompt_kv.shape[2])
    part_rows = frame + STAT
    place_ref = place.reshape(1).astype(jnp.int32)

    def move(value, *pairs):
        both = [(a * streams + s, b * streams + s) for a, b in pairs for s in range(streams)]
        return lax.ppermute(value, "span", both)

    def across(value, flip):
        pairs = [(at, at - at % streams + ((at % streams) ^ flip)) for at in range(WIN * streams)]
        return lax.ppermute(value, "span", pairs)

    def choose(branches, *operands):
        return lax.switch(place, branches, *operands)

    def columns(array, height):
        count = array.shape[1] // CW
        return [(Block(array, 0, height, at * CW), at * height) for at in range(count)]

    def cut(row, rows, first, array, col=0):
        size = rows // 4 if rows % 64 == 0 else rows
        return [
            (Block(array, row + at, size, col), first + at) for at in range(0, rows, size)
        ]

    def query_chunks(array, *chunks):
        return [
            each
            for at, chunk in enumerate(chunks)
            for each in cut(0, frame, at * frame, array, chunk * CW)
        ]

    def kvs(frame_array, sink_array, chunk):
        low = chunk * CW
        return [
            (Block(frame_array, 0, frame, low), 0),
            (Block(frame_array, 0, frame, WIDTH + low), frame),
            (Block(sink_array, 0, sink_rows, low), 2 * frame),
            (Block(sink_array, 0, sink_rows, WIDTH + low), 2 * frame + sink_rows),
        ]

    def whole(array, rows):
        return cut(0, rows, 0, array)

    def own_pairs(frame_array, sink_array, chunk):
        low = chunk * CW
        return [
            (Block(frame_array, 0, frame, low), Block(frame_array, 0, frame, WIDTH + low)),
            (Block(sink_array, 0, sink_rows, low), Block(sink_array, 0, sink_rows, WIDTH + low)),
        ]

    def kvs_pairs(array):
        return [
            (Block(array, 0, frame), Block(array, frame, frame)),
            (
                Block(array, 2 * frame, sink_rows),
                Block(array, 2 * frame + sink_rows, sink_rows),
            ),
        ]

    def sink_pair(array, chunk):
        return (
            Block(array, chunk * sink_rows, sink_rows),
            Block(array, (CHUNKS + chunk) * sink_rows, sink_rows),
        )

    def part(array, index=0, col=0):
        return Block(array, index * part_rows, part_rows, col)

    def spread(shard):
        held = [shard]
        flip = streams // 2
        while flip > 0:
            held = held + [across(each, flip) for each in held]
            flip //= 2
        return held

    stream_ids = jnp.arange(switch.shape[0], dtype=jnp.int32)
    switch_at = jnp.sum(jnp.where(stream_ids == stream, switch, 0))
    pick = (place >= switch_at).astype(jnp.int32).reshape(1)

    prompt_size = 4 * CHUNKS * prompt_rows
    sink_size = 2 * CHUNKS * sink_rows
    same = max(prompt_size, 2 * frame, sink_size)
    kvs_rows = 2 * frame + 2 * sink_rows
    wide = max(kvs_rows, prompt_size, 2 * part_rows)
    two = 2 * part_rows

    prompt = pack(
        place_ref,
        prompt_size,
        {p: columns(prompt_both, 2 * prompt_rows) for p in range(WIN)},
        name="prompt",
    )
    up_a = move(prompt, (0, 1), (1, 2), (2, 3))
    send_b = pack(
        place_ref,
        same,
        {1: whole(prompt, prompt_size), 2: query_chunks(queries, 0, 1), 3: whole(prompt, prompt_size)},
        name="send_b",
    )
    down_b = move(send_b, (3, 2), (2, 1), (1, 0))
    send_c = pack(
        place_ref,
        kvs_rows,
        {0: kvs(frame_kv, sink, 3), 1: kvs(frame_kv, sink, 3)},
        name="send_c",
        after=(send_b,),
    )
    up_c = move(send_c, (0, 1), (1, 2))
    send_d = pack(
        place_ref,
        same,
        {1: columns(sink, sink_rows), 3: query_chunks(queries, 0, 1)},
        name="send_d",
        after=(send_c,),
    )
    down_d = move(send_d, (3, 1), (1, 0))
    stages = spread(prompt)
    at_home = home(queries, frame_kv, sink, send_d)

    send_e = pack(
        place_ref,
        wide,
        {
            0: kvs(frame_kv, sink, 0),
            1: whole(up_a, prompt_size),
            2: whole(up_a, prompt_size),
        },
        name="send_e",
        after=(at_home,),
    )
    up_e = move(send_e, (0, 1), (1, 2), (2, 3))
    send_f = pack(
        place_ref,
        same,
        {2: whole(prompt, prompt_size), 3: query_chunks(queries, 2, 3)},
        name="send_f",
        after=(send_e,),
    )
    down_f = move(send_f, (3, 2), (2, 1))
    second = pack(
        place_ref,
        prompt_size,
        {p: whole(down_b if p == 0 else up_a, prompt_size) for p in range(WIN)},
        name="second_shard",
        after=(send_f,),
    )
    stages += spread(second)
    send_g = pack(
        place_ref,
        kvs_rows,
        {0: kvs(frame_kv, sink, 1), 1: whole(up_c, kvs_rows)},
        name="send_g",
        after=(second,),
    )
    up_g = move(send_g, (0, 1), (1, 2))
    send_i = pack(
        place_ref,
        same,
        {2: whole(down_b, same), 3: query_chunks(queries, 0, 1)},
        name="send_i",
        after=(send_g,),
    )
    down_i = move(send_i, (3, 2), (2, 1))
    send_k = pack(
        place_ref,
        same,
        {
            1: whole(down_f, prompt_size),
            2: cut(0, frame, 0, queries, 2 * CW) + cut(0, frame, frame, down_f),
            3: columns(sink, sink_rows),
        },
        name="send_k",
        after=(send_i,),
    )
    down_k = move(send_k, (3, 2), (2, 1), (1, 0))

    def visit(q2, q3, came, frame_array, sink_array, chunk, rows):
        return attend(
            [([q2, q3], own_pairs(frame_array, sink_array, chunk) + kvs_pairs(came), [], None)],
            (rows, CW),
            "visit",
        )

    def join(query, came, frame_array, sink_array, chunk, rows):
        return attend(
            [([query], own_pairs(frame_array, sink_array, chunk), [part(came, 1)], None)],
            (rows, CW),
            "join",
        )

    def branch_pack(rows, items):
        return pack(jnp.zeros((1,), jnp.int32), rows, {0: items}, name="branch")

    send_h = choose(
        [
            lambda t, f, s, e, b, d: branch_pack(wide, kvs(f, s, 2)),
            lambda t, f, s, e, b, d: visit(
                Block(b, 0, frame), Block(d, 0, frame), e, f, s, 0, wide
            ),
            lambda t, f, s, e, b, d: branch_pack(wide, whole(e, prompt_size)),
            lambda t, f, s, e, b, d: unused(wide, t),
        ],
        send_k,
        frame_kv,
        sink,
        up_e,
        down_b,
        down_d,
    )
    up_h = move(send_h, (0, 1), (1, 2), (2, 3))
    send_l = pack(
        place_ref,
        same,
        {1: whole(down_i, same), 2: columns(sink, sink_rows)},
        name="send_l",
        after=(send_h,),
    )
    down_l = move(send_l, (2, 1), (1, 0))
    third = pack(
        place_ref,
        prompt_size,
        {
            0: whole(down_k, prompt_size),
            1: whole(down_f, prompt_size),
            2: whole(down_b, prompt_size),
            3: whole(up_e, prompt_size),
        },
        name="third_shard",
        after=(send_l,),
    )
    stages += spread(third)
    send_j = choose(
        [
            lambda t, f, s, c, g, b, d, fd: unused(two, t),
            lambda t, f, s, c, g, b, d, fd: visit(
                Block(b, frame, frame), Block(d, frame, frame), g, f, s, 1, two
            ),
            lambda t, f, s, c, g, b, d, fd: attend(
                [([Block(fd, frame, frame)], own_pairs(f, s, 3) + kvs_pairs(c) + kvs_pairs(g), [], None)],
                (two, CW),
                "all_d",
            ),
            lambda t, f, s, c, g, b, d, fd: unused(two, t),
        ],
        third,
        frame_kv,
        sink,
        up_c,
        up_g,
        down_b,
        down_d,
        down_f,
    )
    up_j = move(send_j, (1, 2), (2, 3))
    down_m = move(down_k, (2, 1))
    last = pack(
        place_ref,
        prompt_size,
        {
            0: whole(down_l, prompt_size),
            1: whole(down_i, prompt_size),
            2: whole(up_e, prompt_size),
            3: whole(up_h, prompt_size),
        },
        name="last_shard",
        after=(send_j,),
    )
    stages += spread(last)
    down_o = move(down_l, (1, 0))
    send_n = choose(
        [
            lambda t, f, s, h, k, i: unused(two, t),
            lambda t, f, s, h, k, i: visit(
                Block(k, 0, frame), Block(k, frame, frame), h, f, s, 2, two
            ),
            lambda t, f, s, h, k, i: join(Block(i, 0, frame), h, f, s, 0, two),
            lambda t, f, s, h, k, i: unused(two, t),
        ],
        last,
        frame_kv,
        sink,
        up_h,
        down_k,
        down_i,
    )
    up_n = move(send_n, (1, 2), (2, 3))
    send_o = choose(
        [
            lambda t, f, s, j, i: unused(part_rows, t),
            lambda t, f, s, j, i: unused(part_rows, t),
            lambda t, f, s, j, i: join(Block(i, frame, frame), j, f, s, 1, part_rows),
            lambda t, f, s, j, i: unused(part_rows, t),
        ],
        send_n,
        frame_kv,
        sink,
        up_j,
        down_i,
    )
    up_o = move(send_o, (2, 3))
    down_r = move(down_m, (1, 0))
    send_q = choose(
        [
            lambda t, f, s, n, d: unused(part_rows, t),
            lambda t, f, s, n, d: unused(part_rows, t),
            lambda t, f, s, n, d: join(Block(d, 0, frame), n, f, s, 2, part_rows),
            lambda t, f, s, n, d: unused(part_rows, t),
        ],
        send_o,
        frame_kv,
        sink,
        up_n,
        down_f,
    )
    up_q = move(send_q, (2, 3))

    cross_out = cross(cross_queries, stages, pick, prompt_rows, send_q)

    def finish0(q, h, x, u, d):
        return finish(q, h, [d["d"], d["o"], d["r"]], [], [], sink_rows)

    def finish1(q, h, x, u, d):
        return finish(q, h, [d["l"], d["m"]], [u["e"], u["g"], u["h"], u["c"]], [], sink_rows)

    def finish2(q, h, x, u, d):
        return finish(q, h, [d["k"]], [u["h"], u["j"], u["n"]], [u["c"], u["g"]], sink_rows)

    def finish3(q, h, x, u, d):
        return finish(q, h, [], [u["n"], u["o"], u["q"], u["j"]], [], sink_rows)

    ups = {"c": up_c, "e": up_e, "g": up_g, "h": up_h, "j": up_j, "n": up_n, "o": up_o, "q": up_q}
    downs = {"d": down_d, "k": down_k, "l": down_l, "m": down_m, "o": down_o, "r": down_r}
    self_out = choose(
        [finish0, finish1, finish2, finish3], queries, at_home, cross_out, ups, downs
    )
    return (self_out, cross_out)


def solution(mesh):
    in_specs = (
        P(("groups", "span"), None),
        P(("groups", "span"), None),
        P(("groups", "span"), None),
        P(("groups", "span"), None, None),
        P("groups", "span", None),
        P("groups"),
    )
    out_specs = (P(("groups", "span"), None), P(("groups", "span"), None))
    return jax.shard_map(shards, mesh=mesh, in_specs=in_specs, out_specs=out_specs, check_vma=False)
```

profile of v0, /device:TPU:0, one launch (start us, length us, event | category | flops | bytes accessed | tf_op | source)
XLA Modules:
  0.0 175.4 jit_solution(16271561056938065861)
XLA Ops:
  0.7 2.2 %prompt.1.refs_0_ = bf16[512,640]{1,0:T(8,128)(2,1)} custom-call(s32[1]{0:T(128)} %bitcast.1.place_ref, bf16[64,5120]{1,0:T(8,128)(2,1)} %bitcast.20), custom_call_target="tpu_custom_call" | custom-call | bytes 2000000 | tf_op jit(solution)/shard_map/prompt/pallas_call | solution.py:395
  2.9 6.0 %collective-permute-start.3 = (bf16[512,640]{1,0:T(8,128)(2,1)}, bf16[512,640]{1,0:T(8,128)(2,1)}, u32[]{:S(2)}, u32[]{:S(2)}) collective-permute-start(bf16[512,640]{1,0:T(8,128)(2,1)} %prompt.1.refs_0_), channel_id=1, source_target_pairs={{0,4},{1,5},{2,6},{3,7},{4,8},{5,9},{6,10},{7,11},{8,12},{9,13},{1... | collective-permute-start | bytes 1966088 | tf_op jit(solution)/shard_map/ppermute | solution.py:431
  9.9 2.0 %send_c.1.refs_2_ = bf16[640,640]{1,0:T(8,128)(2,1)} custom-call(s32[1]{0:T(128)} %bitcast.1.place_ref, bf16[256,5120]{1,0:T(8,128)(2,1)} %refs_0_.6, bf16[64,5120]{1,0:T(8,128)(2,1)S(1)} %bitcast.10, bf16[512,640]{1,0:T(8,128)(2,1)} %send_b.1.refs_2_), custom_call_target="tpu_custom_call" | custom-call | bytes 2000000 | tf_op jit(solution)/shard_map/send_c/pallas_call | solution.py:395
  11.9 4.7 %collective-permute-start.2 = (bf16[640,640]{1,0:T(8,128)(2,1)}, bf16[640,640]{1,0:T(8,128)(2,1)}, u32[]{:S(2)}, u32[]{:S(2)}) collective-permute-start(bf16[640,640]{1,0:T(8,128)(2,1)} %send_c.1.refs_2_), channel_id=1, source_target_pairs={{0,4},{1,5},{2,6},{3,7},{4,8},{5,9},{6,10},{7,11},{16,20},{17,21},... | collective-permute-start | bytes 2457608 | tf_op jit(solution)/shard_map/ppermute | solution.py:431
  19.9 6.8 %home.1.refs_3_ = bf16[272,2560]{1,0:T(8,128)(2,1)} custom-call(bf16[256,2560]{1,0:T(8,128)(2,1)S(1)} %copy-done.5, bf16[256,5120]{1,0:T(8,128)(2,1)} %refs_0_.6, bf16[256,5120]{1,0:T(8,128)(2,1)} %refs_0_.6, bf16[64,5120]{1,0:T(8,128)(2,1)S(1)} %bitcast.12, bf16[64,5120]{1,0:T(8,128)(2,1)S(1)} %bitcast.13, bf16[512,640]{1,0:T(8,128)(2,1)S(1)} %copy-done.2), custom_call_target="tpu_custom_call" | custom-call | flops 838860800 | bytes 6000000 | tf_op jit(solution)/shard_map/home/pallas_call | solution.py:202
  26.7 2.1 %send_e.1.refs_2_ = bf16[640,640]{1,0:T(8,128)(2,1)} custom-call(s32[1]{0:T(128)} %bitcast.1.place_ref, bf16[256,5120]{1,0:T(8,128)(2,1)} %refs_0_.6, bf16[64,5120]{1,0:T(8,128)(2,1)S(1)} %bitcast.14, bf16[512,640]{1,0:T(8,128)(2,1)} %collective-permute-done.3.refs_2_.refs_1_, bf16[272,2560]{1,0:T(8,128)(2,1)} %home.1.refs_3_), custom_call_target="tpu_custom_call" | custom-call | bytes 2000000 | tf_op jit(solution)/shard_map/send_e/pallas_call | solution.py:395
  31.8 6.9 %collective-permute-start.5 = (bf16[640,640]{1,0:T(8,128)(2,1)}, bf16[640,640]{1,0:T(8,128)(2,1)}, u32[]{:S(2)}, u32[]{:S(2)}) collective-permute-start(bf16[640,640]{1,0:T(8,128)(2,1)} %send_e.1.refs_2_), channel_id=1, source_target_pairs={{0,4},{1,5},{2,6},{3,7},{4,8},{5,9},{6,10},{7,11},{8,12},{9,13},{1... | collective-permute-start | bytes 2457608 | tf_op jit(solution)/shard_map/ppermute | solution.py:431
  38.7 2.1 %second_shard.1.refs_3_.refs_4_ = bf16[512,640]{1,0:T(8,128)(2,1)} custom-call(s32[1]{0:T(128)} %bitcast.1.place_ref, bf16[512,640]{1,0:T(8,128)(2,1)} %collective-permute-done.1.refs_0_.refs_2_, bf16[512,640]{1,0:T(8,128)(2,1)} %collective-permute-done.3.refs_2_.refs_1_, bf16[512,640]{1,0:T(8,128)(2,1)} %send_f.1.refs_2_), custom_call_target="tpu_custom_call" | custom-call | bytes 2000000 | tf_op jit(solution)/shard_map/second_shard/pallas_call | solution.py:395
  40.9 2.0 %send_g.1.refs_2_ = bf16[640,640]{1,0:T(8,128)(2,1)} custom-call(s32[1]{0:T(128)} %bitcast.1.place_ref, bf16[256,5120]{1,0:T(8,128)(2,1)} %refs_0_.6, bf16[64,5120]{1,0:T(8,128)(2,1)S(1)} %bitcast.15, bf16[640,640]{1,0:T(8,128)(2,1)} %collective-permute-done.2.refs_2_, bf16[512,640]{1,0:T(8,128)(2,1)} %second_shard.1.refs_3_.refs_4_), custom_call_target="tpu_custom_call" | custom-call | bytes 2000000 | tf_op jit(solution)/shard_map/send_g/pallas_call | solution.py:395
  47.0 21.4 %collective-permute-start.12 = (bf16[640,640]{1,0:T(8,128)(2,1)}, bf16[640,640]{1,0:T(8,128)(2,1)}, u32[]{:S(2)}, u32[]{:S(2)}) collective-permute-start(bf16[640,640]{1,0:T(8,128)(2,1)} %send_g.1.refs_2_), channel_id=1, source_target_pairs={{0,4},{1,5},{2,6},{3,7},{4,8},{5,9},{6,10},{7,11},{16,20},{17,21},... | collective-permute-start | bytes 2457608 | tf_op jit(solution)/shard_map/ppermute | solution.py:431
  72.8 11.1 %collective-permute-start.13 = (bf16[640,640]{1,0:T(8,128)(2,1)}, bf16[640,640]{1,0:T(8,128)(2,1)}, u32[]{:S(2)}, u32[]{:S(2)}) collective-permute-start(bf16[640,640]{1,0:T(8,128)(2,1)} %copy-done.8), channel_id=1, source_target_pairs={{0,4},{1,5},{2,6},{3,7},{4,8},{5,9},{6,10},{7,11},{8,12},{9,13},{1... | collective-permute-start | bytes 2457608 | tf_op jit(solution)/shard_map/ppermute | solution.py:431
  86.7 1.5 collective-permute-start.21
  88.2 2.0 %third_shard.1.refs_8_ = bf16[512,640]{1,0:T(8,128)(2,1)} custom-call(s32[1]{0:T(128)} %bitcast.1.place_ref, bf16[512,640]{1,0:T(8,128)(2,1)} %collective-permute-done.9.refs_0_, bf16[512,640]{1,0:T(8,128)(2,1)} %copy-done.7, bf16[512,640]{1,0:T(8,128)(2,1)} %collective-permute-done.1.refs_0_.refs_2_, ...), custom_call_target="tpu_custom_call" | custom-call | bytes 2000000 | tf_op jit(solution)/shard_map/third_shard/pallas_call | solution.py:395
  90.3 1.5 collective-permute-start.14
  91.9 12.3 %collective-permute-done.7.refs_0_ = bf16[512,640]{1,0:T(8,128)(2,1)} collective-permute-done((bf16[512,640]{1,0:T(8,128)(2,1)}, bf16[512,640]{1,0:T(8,128)(2,1)}, u32[]{:S(2)}, u32[]{:S(2)}) %collective-permute-start.7) | collective-permute-done | bytes 655392 | tf_op jit(solution)/shard_map/ppermute | solution.py:431
  104.2 1.6 collective-permute-start.10
  105.7 2.1 %last_shard.1.refs_12_ = bf16[512,640]{1,0:T(8,128)(2,1)} custom-call(s32[1]{0:T(128)} %bitcast.1.place_ref, bf16[512,640]{1,0:T(8,128)(2,1)} %collective-permute-done.7.refs_0_, bf16[512,640]{1,0:T(8,128)(2,1)} %collective-permute-done.4.refs_0_.refs_1_, bf16[640,640]{1,0:T(8,128)(2,1)} %collective-permute-done.5.refs_3_.refs_2_, ...), custom_call_target="tpu_custom_call" | custom-call | bytes 2000000 | tf_op jit(solution)/shard_map/last_shard/pallas_call | solution.py:395
  107.8 1.5 collective-permute-start.15
  115.5 11.7 %collective-permute-done.24.refs_9_ = bf16[512,640]{1,0:T(8,128)(2,1)} collective-permute-done((bf16[512,640]{1,0:T(8,128)(2,1)}, bf16[512,640]{1,0:T(8,128)(2,1)}, u32[]{:S(2)}, u32[]{:S(2)}) %collective-permute-start.24) | collective-permute-done | bytes 655392 | tf_op jit(solution)/shard_map/ppermute | solution.py:435
  128.6 12.5 %collective-permute-done.8 = bf16[512,640]{1,0:T(8,128)(2,1)} collective-permute-done((bf16[512,640]{1,0:T(8,128)(2,1)}, bf16[512,640]{1,0:T(8,128)(2,1)}, u32[]{:S(2)}, u32[]{:S(2)}) %collective-permute-start.8) | collective-permute-done | bytes 655392 | tf_op jit(solution)/shard_map/ppermute | solution.py:431
  141.7 12.4 %collective-permute-done.11 = bf16[512,640]{1,0:T(8,128)(2,1)} collective-permute-done((bf16[512,640]{1,0:T(8,128)(2,1)}, bf16[512,640]{1,0:T(8,128)(2,1)}, u32[]{:S(2)}, u32[]{:S(2)}) %collective-permute-start.11) | collective-permute-done | bytes 655392 | tf_op jit(solution)/shard_map/ppermute | solution.py:431
  156.0 10.3 %conditional.11 = (bf16[256,2560]{1,0:T(8,128)(2,1)}) conditional(s32[]{:T(128)} %clamp.2, (bf16[256,2560]{1,0:T(8,128)(2,1)}, bf16[272,2560]{1,0:T(8,128)(2,1)}, bf16[512,640]{1,0:T(8,128)(2,1)}, bf16[512,640]{1,0:T(8,128)(2,1)}, bf16[512,640]{1,0:T(8,128)(2,1)}) %tuple.82, (bf16[256,2560]{1,0:T(8,128)(2,1)}, ...), branch_computations={%region_20.21_spmd, %region_21.22_spmd, %region_22.23_spmd, %regio... | conditional | bytes 8 | solution.py:438
  156.0 10.1 %finish.4 = bf16[256,2560]{1,0:T(8,128)(2,1)} custom-call(bf16[256,2560]{1,0:T(8,128)(2,1)} %get-tuple-element.195.refs_0_, bf16[272,2560]{1,0:T(8,128)(2,1)} %get-tuple-element.196.refs_1_, bf16[512,640]{1,0:T(8,128)(2,1)} %get-tuple-element.197.refs_2_.refs_3_, bf16[512,640]{1,0:T(8,128)(2,1)} %get-tuple-element.197.refs_2_.refs_3_, ...), custom_call_target="tpu_custom_call" | custom-call | tf_op jit(solution)/shard_map/cond/branch_0_fun/finish/pallas_call | solution.py:317
  166.4 9.0 %cross.1 = bf16[256,2560]{1,0:T(8,128)(2,1)} custom-call(s32[1]{0:T(128)} %bitcast.3.pick_ref, bf16[256,2560]{1,0:T(8,128)(2,1)} %query.3, bf16[512,640]{1,0:T(8,128)(2,1)S(1)} %copy-done, bf16[512,640]{1,0:T(8,128)(2,1)S(1)} %collective-permute-done.18.refs_1_, bf16[512,640]{1,0:T(8,128)(2,1)S(1)} %collective-permute-done.19.refs_2_, ...), custom_call_target="tpu_custom_call" | custom-call | flops 1342177280 | bytes 12000000 | tf_op jit(solution)/shard_map/cross/pallas_call | solution.py:355
  (84 shorter events, 29.0 us)
Async XLA Ops:
  2.9 23.8 %collective-permute-start.3 = (bf16[512,640]{1,0:T(8,128)(2,1)}, bf16[512,640]{1,0:T(8,128)(2,1)}, u32[]{:S(2)}, u32[]{:S(2)}) collective-permute-start(bf16[512,640]{1,0:T(8,128)(2,1)} %prompt.1.refs_0_), channel_id=1, source_target_pairs={{0,4},{1,5},{2,6},{3,7},{4,8},{5,9},{6,10},{7,11},{8,12},{9,13},{1... | collective-permute-start | bytes 1966088 | tf_op jit(solution)/shard_map/ppermute | solution.py:431
  11.9 29.1 %collective-permute-start.2 = (bf16[640,640]{1,0:T(8,128)(2,1)}, bf16[640,640]{1,0:T(8,128)(2,1)}, u32[]{:S(2)}, u32[]{:S(2)}) collective-permute-start(bf16[640,640]{1,0:T(8,128)(2,1)} %send_c.1.refs_2_), channel_id=1, source_target_pairs={{0,4},{1,5},{2,6},{3,7},{4,8},{5,9},{6,10},{7,11},{16,20},{17,21},... | collective-permute-start | bytes 2457608 | tf_op jit(solution)/shard_map/ppermute | solution.py:431
  16.6 22.1 %collective-permute-start.1 = (bf16[512,640]{1,0:T(8,128)(2,1)}, bf16[512,640]{1,0:T(8,128)(2,1)}, u32[]{:S(2)}, u32[]{:S(2)}) collective-permute-start(bf16[512,640]{1,0:T(8,128)(2,1)} %send_b.1.refs_2_), channel_id=1, source_target_pairs={{12,8},{13,9},{14,10},{15,11},{8,4},{9,5},{10,6},{11,7},{4,0},{5,1... | collective-permute-start | bytes 1966088 | tf_op jit(solution)/shard_map/ppermute | solution.py:431
  29.8 17.2 %collective-permute-start.6 = (bf16[512,640]{1,0:T(8,128)(2,1)}, bf16[512,640]{1,0:T(8,128)(2,1)S(1)}, u32[]{:S(2)}, u32[]{:S(2)}) collective-permute-start(bf16[512,640]{1,0:T(8,128)(2,1)} %send_f.1.refs_2_), channel_id=1, source_target_pairs={{12,8},{13,9},{14,10},{15,11},{8,4},{9,5},{10,6},{11,7},{28,24},{2... | collective-permute-start | bytes 1966088 | tf_op jit(solution)/shard_map/ppermute | solution.py:431
  30.5 38.9 %collective-permute-start = (bf16[512,640]{1,0:T(8,128)(2,1)S(1)}, bf16[512,640]{1,0:T(8,128)(2,1)}, u32[]{:S(2)}, u32[]{:S(2)}) collective-permute-start(bf16[512,640]{1,0:T(8,128)(2,1)S(1)} %copy-done.3), channel_id=1, source_target_pairs={{12,4},{13,5},{14,6},{15,7},{4,0},{5,1},{6,2},{7,3},{28,20},{29,21... | collective-permute-start | bytes 1966088 | tf_op jit(solution)/shard_map/ppermute | solution.py:431
  31.8 38.9 %collective-permute-start.5 = (bf16[640,640]{1,0:T(8,128)(2,1)}, bf16[640,640]{1,0:T(8,128)(2,1)}, u32[]{:S(2)}, u32[]{:S(2)}) collective-permute-start(bf16[640,640]{1,0:T(8,128)(2,1)} %send_e.1.refs_2_), channel_id=1, source_target_pairs={{0,4},{1,5},{2,6},{3,7},{4,8},{5,9},{6,10},{7,11},{8,12},{9,13},{1... | collective-permute-start | bytes 2457608 | tf_op jit(solution)/shard_map/ppermute | solution.py:431
  43.9 39.9 %collective-permute-start.4 = (bf16[512,640]{1,0:T(8,128)(2,1)}, bf16[512,640]{1,0:T(8,128)(2,1)}, u32[]{:S(2)}, u32[]{:S(2)}) collective-permute-start(bf16[512,640]{1,0:T(8,128)(2,1)} %send_i.1.refs_3_), channel_id=1, source_target_pairs={{12,8},{13,9},{14,10},{15,11},{8,4},{9,5},{10,6},{11,7},{28,24},{2... | collective-permute-start | bytes 1966088 | tf_op jit(solution)/shard_map/ppermute | solution.py:431
  45.5 39.3 %collective-permute-start.18 = (bf16[512,640]{1,0:T(8,128)(2,1)S(1)}, bf16[512,640]{1,0:T(8,128)(2,1)S(1)}, u32[]{:S(2)}, u32[]{:S(2)}) collective-permute-start(bf16[512,640]{1,0:T(8,128)(2,1)S(1)} %copy-done), channel_id=1, source_target_pairs={{0,2},{1,3},{2,0},{3,1},{4,6},{5,7},{6,4},{7,5},{8,10},{9,11},{10,... | collective-permute-start | bytes 1966088 | tf_op jit(solution)/shard_map/ppermute | solution.py:435
  47.0 39.1 %collective-permute-start.12 = (bf16[640,640]{1,0:T(8,128)(2,1)}, bf16[640,640]{1,0:T(8,128)(2,1)}, u32[]{:S(2)}, u32[]{:S(2)}) collective-permute-start(bf16[640,640]{1,0:T(8,128)(2,1)} %send_g.1.refs_2_), channel_id=1, source_target_pairs={{0,4},{1,5},{2,6},{3,7},{4,8},{5,9},{6,10},{7,11},{16,20},{17,21},... | collective-permute-start | bytes 2457608 | tf_op jit(solution)/shard_map/ppermute | solution.py:431
  69.4 17.3 %collective-permute-start.9 = (bf16[512,640]{1,0:T(8,128)(2,1)}, bf16[512,640]{1,0:T(8,128)(2,1)}, u32[]{:S(2)}, u32[]{:S(2)}) collective-permute-start(bf16[512,640]{1,0:T(8,128)(2,1)} %send_k.1), channel_id=1, source_target_pairs={{12,8},{13,9},{14,10},{15,11},{8,4},{9,5},{10,6},{11,7},{4,0},{5,1... | collective-permute-start | bytes 1966088 | tf_op jit(solution)/shard_map/ppermute | solution.py:431
  72.8 31.4 %collective-permute-start.13 = (bf16[640,640]{1,0:T(8,128)(2,1)}, bf16[640,640]{1,0:T(8,128)(2,1)}, u32[]{:S(2)}, u32[]{:S(2)}) collective-permute-start(bf16[640,640]{1,0:T(8,128)(2,1)} %copy-done.8), channel_id=1, source_target_pairs={{0,4},{1,5},{2,6},{3,7},{4,8},{5,9},{6,10},{7,11},{8,12},{9,13},{1... | collective-permute-start | bytes 2457608 | tf_op jit(solution)/shard_map/ppermute | solution.py:431
  84.8 19.4 %collective-permute-start.7 = (bf16[512,640]{1,0:T(8,128)(2,1)}, bf16[512,640]{1,0:T(8,128)(2,1)}, u32[]{:S(2)}, u32[]{:S(2)}) collective-permute-start(bf16[512,640]{1,0:T(8,128)(2,1)} %send_l.1.refs_4_), channel_id=1, source_target_pairs={{8,4},{9,5},{10,6},{11,7},{4,0},{5,1},{6,2},{7,3},{24,20},{25,21},... | collective-permute-start | bytes 1966088 | tf_op jit(solution)/shard_map/ppermute | solution.py:431
  86.1 21.7 %collective-permute-start.20 = (bf16[512,640]{1,0:T(8,128)(2,1)S(1)}, bf16[512,640]{1,0:T(8,128)(2,1)S(1)}, u32[]{:S(2)}, u32[]{:S(2)}) collective-permute-start(bf16[512,640]{1,0:T(8,128)(2,1)S(1)} %collective-permute-done.18.refs_1_), channel_id=1, source_target_pairs={{0,1},{1,0},{2,3},{3,2},{4,5},{5,4},{6,7},{7,6},{8,9},{9,8},{10,11... | collective-permute-start | bytes 1966088 | tf_op jit(solution)/shard_map/ppermute | solution.py:435
  86.7 22.7 %collective-permute-start.21 = (bf16[512,640]{1,0:T(8,128)(2,1)S(1)}, bf16[512,640]{1,0:T(8,128)(2,1)}, u32[]{:S(2)}, u32[]{:S(2)}) collective-permute-start(bf16[512,640]{1,0:T(8,128)(2,1)S(1)} %copy-done.1), channel_id=1, source_target_pairs={{0,2},{1,3},{2,0},{3,1},{4,6},{5,7},{6,4},{7,5},{8,10},{9,11},{10,... | collective-permute-start | bytes 1966088 | tf_op jit(solution)/shard_map/ppermute | solution.py:435
  90.3 22.5 %collective-permute-start.14 = (bf16[544,640]{1,0:T(8,128)(2,1)}, bf16[544,640]{1,0:T(8,128)(2,1)}, u32[]{:S(2)}, u32[]{:S(2)}) collective-permute-start(bf16[544,640]{1,0:T(8,128)(2,1)} %get-tuple-element.225.refs_4_), channel_id=1, source_target_pairs={{4,8},{5,9},{6,10},{7,11},{8,12},{9,13},{10,14},{11,15},{20,24},{2... | collective-permute-start | bytes 2088968 | tf_op jit(solution)/shard_map/ppermute | solution.py:431
  109.4 17.8 %collective-permute-start.24 = (bf16[512,640]{1,0:T(8,128)(2,1)}, bf16[512,640]{1,0:T(8,128)(2,1)}, u32[]{:S(2)}, u32[]{:S(2)}) collective-permute-start(bf16[512,640]{1,0:T(8,128)(2,1)} %third_shard.1.refs_8_), channel_id=1, source_target_pairs={{0,2},{1,3},{2,0},{3,1},{4,6},{5,7},{6,4},{7,5},{8,10},{9,11},{10,... | collective-permute-start | bytes 1966088 | tf_op jit(solution)/shard_map/ppermute | solution.py:435
  110.9 30.2 %collective-permute-start.8 = (bf16[512,640]{1,0:T(8,128)(2,1)}, bf16[512,640]{1,0:T(8,128)(2,1)}, u32[]{:S(2)}, u32[]{:S(2)}) collective-permute-start(bf16[512,640]{1,0:T(8,128)(2,1)} %collective-permute-done.7.refs_0_), channel_id=1, source_target_pairs={{4,0},{5,1},{6,2},{7,3},{20,16},{21,17},{22,18},{23,19}} | collective-permute-start | bytes 1966088 | tf_op jit(solution)/shard_map/ppermute | solution.py:431
  112.2 28.9 %collective-permute-start.27 = (bf16[512,640]{1,0:T(8,128)(2,1)}, bf16[512,640]{1,0:T(8,128)(2,1)}, u32[]{:S(2)}, u32[]{:S(2)}) collective-permute-start(bf16[512,640]{1,0:T(8,128)(2,1)} %last_shard.1.refs_12_), channel_id=1, source_target_pairs={{0,2},{1,3},{2,0},{3,1},{4,6},{5,7},{6,4},{7,5},{8,10},{9,11},{10,... | collective-permute-start | bytes 1966088 | tf_op jit(solution)/shard_map/ppermute | solution.py:435
  112.8 41.4 %collective-permute-start.11 = (bf16[512,640]{1,0:T(8,128)(2,1)}, bf16[512,640]{1,0:T(8,128)(2,1)}, u32[]{:S(2)}, u32[]{:S(2)}) collective-permute-start(bf16[512,640]{1,0:T(8,128)(2,1)} %collective-permute-done.10), channel_id=1, source_target_pairs={{4,0},{5,1},{6,2},{7,3},{20,16},{21,17},{22,18},{23,19}} | collective-permute-start | bytes 1966088 | tf_op jit(solution)/shard_map/ppermute | solution.py:431
  114.1 27.5 %collective-permute-start.16 = (bf16[272,640]{1,0:T(8,128)(2,1)}, bf16[272,640]{1,0:T(8,128)(2,1)}, u32[]{:S(2)}, u32[]{:S(2)}) collective-permute-start(bf16[272,640]{1,0:T(8,128)(2,1)} %get-tuple-element.227), channel_id=1, source_target_pairs={{8,12},{9,13},{10,14},{11,15},{24,28},{25,29},{26,30},{27,31}} | collective-permute-start | bytes 1044488 | tf_op jit(solution)/shard_map/ppermute | solution.py:431
  127.2 26.9 %collective-permute-start.17 = (bf16[272,640]{1,0:T(8,128)(2,1)}, bf16[272,640]{1,0:T(8,128)(2,1)}, u32[]{:S(2)}, u32[]{:S(2)}) collective-permute-start(bf16[272,640]{1,0:T(8,128)(2,1)} %get-tuple-element.228.refs_16_), channel_id=1, source_target_pairs={{8,12},{9,13},{10,14},{11,15},{24,28},{25,29},{26,30},{27,31}} | collective-permute-start | bytes 1044488 | tf_op jit(solution)/shard_map/ppermute | solution.py:431
  141.1 25.2 %collective-permute-start.23 = (bf16[512,640]{1,0:T(8,128)(2,1)}, bf16[512,640]{1,0:T(8,128)(2,1)}, u32[]{:S(2)}, u32[]{:S(2)}) collective-permute-start(bf16[512,640]{1,0:T(8,128)(2,1)} %collective-permute-done.21.refs_5_), channel_id=1, source_target_pairs={{0,1},{1,0},{2,3},{3,2},{4,5},{5,4},{6,7},{7,6},{8,9},{9,8},{10,11... | collective-permute-start | bytes 1966088 | tf_op jit(solution)/shard_map/ppermute | solution.py:435
  141.2 25.2 %collective-permute-start.25 = (bf16[512,640]{1,0:T(8,128)(2,1)}, bf16[512,640]{1,0:T(8,128)(2,1)}, u32[]{:S(2)}, u32[]{:S(2)}) collective-permute-start(bf16[512,640]{1,0:T(8,128)(2,1)} %third_shard.1.refs_8_), channel_id=1, source_target_pairs={{0,1},{1,0},{2,3},{3,2},{4,5},{5,4},{6,7},{7,6},{8,9},{9,8},{10,11... | collective-permute-start | bytes 1966088 | tf_op jit(solution)/shard_map/ppermute | solution.py:435
  141.7 24.7 %collective-permute-start.28 = (bf16[512,640]{1,0:T(8,128)(2,1)}, bf16[512,640]{1,0:T(8,128)(2,1)}, u32[]{:S(2)}, u32[]{:S(2)}) collective-permute-start(bf16[512,640]{1,0:T(8,128)(2,1)} %last_shard.1.refs_12_), channel_id=1, source_target_pairs={{0,1},{1,0},{2,3},{3,2},{4,5},{5,4},{6,7},{7,6},{8,9},{9,8},{10,11... | collective-permute-start | bytes 1966088 | tf_op jit(solution)/shard_map/ppermute | solution.py:435
  (16 other events, 150.9 us)
where the time goes:
time: 176 us; the launch traced here: 175 us
  starting transfers between devices  74.3 us (42%)
  waiting for transfers between devices  49.1 us (28%)
  Pallas kernels  47.3 us (27%)
  local copies, waits for them, and re-layouts  2 us (1%)
    ppermute x18, starting transfers between devices, move(): return lax.ppermute(value, 'span', both)  67.5 us
    ppermute x18, waiting for transfers between devices, move(): return lax.ppermute(value, 'span', both)  37.4 us
    pallas_call x14, Pallas kernels, pack(): pl.pallas_call(kernel, out_shape=jax.ShapeDtypeStruct((rows, CW), jnp.bfl...  21.3 us
    ppermute x12, waiting for transfers between devices, across(): return lax.ppermute(value, 'span', pairs)  11.7 us
    pallas_call x1, Pallas kernels, finish(): pl.pallas_call(kernel, out_shape=jax.ShapeDtypeStruct(queries.shape, jnp....  10.1 us
    pallas_call x1, Pallas kernels, cross(): pl.pallas_call(kernel, out_shape=jax.ShapeDtypeStruct(queries.shape, jnp....  9.01 us
    pallas_call x1, Pallas kernels, home(): pl.pallas_call(kernel, out_shape=jax.ShapeDtypeStruct((frame + STAT, WIDT...  6.83 us
    ppermute x12, starting transfers between devices, across(): return lax.ppermute(value, 'span', pairs)  6.82 us
  transfers between devices with their start and end apart: 30, of which 5 were waited for; matrix products, arithmetic and copies ran while one was open for 0% of the time, Pallas kernels for 21%

commit v1 on v0

--- a/solution.py
+++ b/solution.py
@@ -329,29 +329,35 @@
 def cross(queries, shards, pick, prompt_rows, after):
     frame = queries.shape[0]
     step = 2 * prompt_rows
+    size = 2 * CHUNKS * step
+    count = sum(each.shape[0] for each in shards) // size
 
     def kernel(pick_ref, query, *refs):
         out = refs[-1]
         picked = pick_ref[0] * prompt_rows
 
         def chunk(at, carry):
-            def rows(ref, which):
-                start = pl.multiple_of(which * step + picked, 8)
-                return ref.at[pl.ds(start, prompt_rows)]
-
-            first = pl.multiple_of(at * CW, HDIM)
+            def pieces(which, cols):
+                return stacked(
+                    [
+                        ref[pl.ds(pl.multiple_of(first + which * step + picked, 8), prompt_rows), cols]
+                        for ref in refs[: len(shards)]
+                        for first in range(0, ref.shape[0], size)
+                    ]
+                )
+
+            left = pl.multiple_of(at * CW, HDIM)
             for head in range(PER):
                 cols = pl.ds(head * HDIM, HDIM)
-                keys = stacked([rows(ref, at)[:, cols] for ref in refs[:-2]])
-                values = stacked([rows(ref, CHUNKS + at)[:, cols] for ref in refs[:-2]])
-                here = pl.ds(first + head * HDIM, HDIM)
+                keys, values = pieces(at, cols), pieces(CHUNKS + at, cols)
+                here = pl.ds(left + head * HDIM, HDIM)
                 _, total, blended = fresh_state(query[:, here], keys, values)
                 out[:, here] = (blended / total).astype(jnp.bfloat16)
             return carry
 
         lax.fori_loop(0, CHUNKS, chunk, 0)
 
-    work = HEADS * frame * prompt_rows * len(shards)
+    work = HEADS * frame * prompt_rows * count
     return pl.pallas_call(
         kernel,
         out_shape=jax.ShapeDtypeStruct(queries.shape, jnp.bfloat16),
@@ -498,6 +504,11 @@
             held = held + [across(each, flip) for each in held]
             flip //= 2
         return held
+
+    planes = [[at * streams + s for s in range(streams)] for at in range(WIN)]
+
+    def gathered(shard):
+        return [lax.all_gather(shard, "span", axis_index_groups=planes, axis=0, tiled=True)]
 
     stream_ids = jnp.arange(switch.shape[0], dtype=jnp.int32)
     switch_at = jnp.sum(jnp.where(stream_ids == stream, switch, 0))
@@ -642,19 +653,6 @@
         after=(send_h,),
     )
     down_l = move(send_l, (2, 1), (1, 0))
-    third = pack(
-        place_ref,
-        prompt_size,
-        {
-            0: whole(down_k, prompt_size),
-            1: whole(down_f, prompt_size),
-            2: whole(down_b, prompt_size),
-            3: whole(up_e, prompt_size),
-        },
-        name="third_shard",
-        after=(send_l,),
-    )
-    stages += spread(third)
     send_j = choose(
         [
             lambda t, f, s, c, g, b, d, fd: unused(two, t),
@@ -668,7 +666,7 @@
             ),
             lambda t, f, s, c, g, b, d, fd: unused(two, t),
         ],
-        third,
+        send_l,
         frame_kv,
         sink,
         up_c,
@@ -678,20 +676,20 @@
         down_f,
     )
     up_j = move(send_j, (1, 2), (2, 3))
-    down_m = move(down_k, (2, 1))
-    last = pack(
+    third = pack(
         place_ref,
         prompt_size,
         {
-            0: whole(down_l, prompt_size),
-            1: whole(down_i, prompt_size),
-            2: whole(up_e, prompt_size),
-            3: whole(up_h, prompt_size),
+            0: whole(down_k, prompt_size),
+            1: whole(down_f, prompt_size),
+            2: whole(down_b, prompt_size),
+            3: whole(up_e, prompt_size),
         },
-        name="last_shard",
+        name="third_shard",
         after=(send_j,),
     )
-    stages += spread(last)
+    stages += spread(third)
+    down_m = move(down_k, (2, 1))
     down_o = move(down_l, (1, 0))
     send_n = choose(
         [
@@ -702,7 +700,7 @@
             lambda t, f, s, h, k, i: join(Block(i, 0, frame), h, f, s, 0, two),
             lambda t, f, s, h, k, i: unused(two, t),
         ],
-        last,
+        third,
         frame_kv,
         sink,
         up_h,
@@ -710,6 +708,19 @@
         down_i,
     )
     up_n = move(send_n, (1, 2), (2, 3))
+    last = pack(
+        place_ref,
+        prompt_size,
+        {
+            0: whole(down_l, prompt_size),
+            1: whole(down_i, prompt_size),
+            2: whole(up_e, prompt_size),
+            3: whole(up_h, prompt_size),
+        },
+        name="last_shard",
+        after=(send_n,),
+    )
+    stages += spread(last)
     send_o = choose(
         [
             lambda t, f, s, j, i: unused(part_rows, t),
@@ -717,7 +728,7 @@
             lambda t, f, s, j, i: join(Block(i, frame, frame), j, f, s, 1, part_rows),
             lambda t, f, s, j, i: unused(part_rows, t),
         ],
-        send_n,
+        last,
         frame_kv,
         sink,
         up_j,
@@ -725,6 +736,7 @@
     )
     up_o = move(send_o, (2, 3))
     down_r = move(down_m, (1, 0))
+    cross_out = cross(cross_queries, stages, pick, prompt_rows, send_o)
     send_q = choose(
         [
             lambda t, f, s, n, d: unused(part_rows, t),
@@ -740,7 +752,6 @@
     )
     up_q = move(send_q, (2, 3))
 
-    cross_out = cross(cross_queries, stages, pick, prompt_rows, send_q)
 
     def finish0(q, h, x, u, d):
         return finish(q, h, [d["d"], d["o"], d["r"]], [], [], sink_rows)

time: 176 us -> 170 us (0.966)
  starting transfers between devices: 74.3 us -> 63.8 us
  waiting for transfers between devices: 49.1 us -> 55 us
    ppermute x18, starting transfers between devices: 67.5 us -> 58.1 us  [move(): return lax.ppermute(value, 'span', both)]
    ppermute x12, waiting for transfers between devices: 11.7 us -> 15.1 us  [across(): return lax.ppermute(value, 'span', pairs)]
    ppermute x18, waiting for transfers between devices: 37.4 us -> 39.9 us  [move(): return lax.ppermute(value, 'span', both)]
  transfers between devices with their start and end apart: 30 -> 30, of which waited for: 5 -> 8; matrix products, arithmetic and copies ran while one was open for 0% -> 0% of each run, Pallas kernels for 21% -> 21%
where the time goes in v1:
time: 170 us
  starting transfers between devices  63.8 us (38%)
  waiting for transfers between devices  55 us (32%)
  Pallas kernels  46.9 us (28%)
  between operations  1.71 us (1%)
    ppermute x18, starting transfers between devices, move(): return lax.ppermute(value, 'span', both)  58.1 us
    ppermute x18, waiting for transfers between devices, move(): return lax.ppermute(value, 'span', both)  39.9 us
    pallas_call x14, Pallas kernels, pack(): pl.pallas_call(kernel, out_shape=jax.ShapeDtypeStruct((rows, CW), jnp.bfl...  20.9 us
    ppermute x12, waiting for transfers between devices, across(): return lax.ppermute(value, 'span', pairs)  15.1 us
    pallas_call x1, Pallas kernels, finish(): pl.pallas_call(kernel, out_shape=jax.ShapeDtypeStruct(queries.shape, jnp....  10.1 us
    pallas_call x1, Pallas kernels, cross(): pl.pallas_call(kernel, out_shape=jax.ShapeDtypeStruct(queries.shape, jnp....  9.06 us
    pallas_call x1, Pallas kernels, home(): pl.pallas_call(kernel, out_shape=jax.ShapeDtypeStruct((frame + STAT, WIDT...  6.83 us
    ppermute x12, starting transfers between devices, across(): return lax.ppermute(value, 'span', pairs)  5.74 us
  transfers between devices with their start and end apart: 30, of which 8 were waited for; matrix products, arithmetic and copies ran while one was open for 0% of the time, Pallas kernels for 21%

profile of v1, /device:TPU:0, one launch (start us, length us, event | category | flops | bytes accessed | tf_op | source)
XLA Modules:
  0.0 169.6 jit_solution(5896302422628698971)
XLA Ops:
  0.7 2.2 %prompt.1.refs_0_ = bf16[512,640]{1,0:T(8,128)(2,1)} custom-call(s32[1]{0:T(128)} %bitcast.1.place_ref, bf16[64,5120]{1,0:T(8,128)(2,1)} %bitcast.20), custom_call_target="tpu_custom_call" | custom-call | bytes 2000000 | tf_op jit(solution)/shard_map/prompt/pallas_call | solution.py:401
  2.8 6.1 %collective-permute-start.3 = (bf16[512,640]{1,0:T(8,128)(2,1)}, bf16[512,640]{1,0:T(8,128)(2,1)}, u32[]{:S(2)}, u32[]{:S(2)}) collective-permute-start(bf16[512,640]{1,0:T(8,128)(2,1)} %prompt.1.refs_0_), channel_id=1, source_target_pairs={{0,4},{1,5},{2,6},{3,7},{4,8},{5,9},{6,10},{7,11},{8,12},{9,13},{1... | collective-permute-start | bytes 1966088 | tf_op jit(solution)/shard_map/ppermute | solution.py:437
  11.0 4.9 %collective-permute-start.2 = (bf16[640,640]{1,0:T(8,128)(2,1)}, bf16[640,640]{1,0:T(8,128)(2,1)}, u32[]{:S(2)}, u32[]{:S(2)}) collective-permute-start(bf16[640,640]{1,0:T(8,128)(2,1)} %send_c.1.refs_2_), channel_id=1, source_target_pairs={{0,4},{1,5},{2,6},{3,7},{4,8},{5,9},{6,10},{7,11},{16,20},{17,21},... | collective-permute-start | bytes 2457608 | tf_op jit(solution)/shard_map/ppermute | solution.py:437
  20.5 6.8 %home.1.refs_3_ = bf16[272,2560]{1,0:T(8,128)(2,1)} custom-call(bf16[256,2560]{1,0:T(8,128)(2,1)S(1)} %copy-done.5, bf16[256,5120]{1,0:T(8,128)(2,1)} %refs_0_.6, bf16[256,5120]{1,0:T(8,128)(2,1)} %refs_0_.6, bf16[64,5120]{1,0:T(8,128)(2,1)S(1)} %bitcast.13, bf16[64,5120]{1,0:T(8,128)(2,1)S(1)} %bitcast.14, bf16[512,640]{1,0:T(8,128)(2,1)S(1)} %copy-done.2), custom_call_target="tpu_custom_call" | custom-call | flops 838860800 | bytes 6000000 | tf_op jit(solution)/shard_map/home/pallas_call | solution.py:202
  27.3 2.0 %send_e.1.refs_2_ = bf16[640,640]{1,0:T(8,128)(2,1)} custom-call(s32[1]{0:T(128)} %bitcast.1.place_ref, bf16[256,5120]{1,0:T(8,128)(2,1)} %refs_0_.6, bf16[64,5120]{1,0:T(8,128)(2,1)S(1)} %bitcast.15, bf16[512,640]{1,0:T(8,128)(2,1)} %collective-permute-done.3.refs_2_.refs_1_, bf16[272,2560]{1,0:T(8,128)(2,1)} %home.1.refs_3_), custom_call_target="tpu_custom_call" | custom-call | bytes 2000000 | tf_op jit(solution)/shard_map/send_e/pallas_call | solution.py:401
  31.9 6.0 %collective-permute-start.5 = (bf16[640,640]{1,0:T(8,128)(2,1)}, bf16[640,640]{1,0:T(8,128)(2,1)}, u32[]{:S(2)}, u32[]{:S(2)}) collective-permute-start(bf16[640,640]{1,0:T(8,128)(2,1)} %send_e.1.refs_2_), channel_id=1, source_target_pairs={{0,4},{1,5},{2,6},{3,7},{4,8},{5,9},{6,10},{7,11},{8,12},{9,13},{1... | collective-permute-start | bytes 2457608 | tf_op jit(solution)/shard_map/ppermute | solution.py:437
  41.1 1.8 %second_shard.1.refs_3_.refs_4_ = bf16[512,640]{1,0:T(8,128)(2,1)} custom-call(s32[1]{0:T(128)} %bitcast.1.place_ref, bf16[512,640]{1,0:T(8,128)(2,1)S(1)} %collective-permute-done.1.refs_0_.refs_2_, bf16[512,640]{1,0:T(8,128)(2,1)} %collective-permute-done.3.refs_2_.refs_1_, bf16[512,640]{1,0:T(8,128)(2,1)} %send_f.1.refs_2_), custom_call_target="tpu_custom_call" | custom-call | bytes 2000000 | tf_op jit(solution)/shard_map/second_shard/pallas_call | solution.py:401
  42.8 2.0 %send_g.1.refs_2_ = bf16[640,640]{1,0:T(8,128)(2,1)} custom-call(s32[1]{0:T(128)} %bitcast.1.place_ref, bf16[256,5120]{1,0:T(8,128)(2,1)} %refs_0_.6, bf16[64,5120]{1,0:T(8,128)(2,1)S(1)} %bitcast.16, bf16[640,640]{1,0:T(8,128)(2,1)} %collective-permute-done.2.refs_2_, bf16[512,640]{1,0:T(8,128)(2,1)} %second_shard.1.refs_3_.refs_4_), custom_call_target="tpu_custom_call" | custom-call | bytes 2000000 | tf_op jit(solution)/shard_map/send_g/pallas_call | solution.py:401
  44.8 3.2 %collective-permute-done = bf16[512,640]{1,0:T(8,128)(2,1)} collective-permute-done((bf16[512,640]{1,0:T(8,128)(2,1)}, bf16[512,640]{1,0:T(8,128)(2,1)}, u32[]{:S(2)}, u32[]{:S(2)}) %collective-permute-start) | collective-permute-done | bytes 655392 | tf_op jit(solution)/shard_map/ppermute | solution.py:437
  48.0 9.9 %collective-permute-start.12 = (bf16[640,640]{1,0:T(8,128)(2,1)}, bf16[640,640]{1,0:T(8,128)(2,1)}, u32[]{:S(2)}, u32[]{:S(2)}) collective-permute-start(bf16[640,640]{1,0:T(8,128)(2,1)} %send_g.1.refs_2_), channel_id=1, source_target_pairs={{0,4},{1,5},{2,6},{3,7},{4,8},{5,9},{6,10},{7,11},{16,20},{17,21},... | collective-permute-start | bytes 2457608 | tf_op jit(solution)/shard_map/ppermute | solution.py:437
  61.3 2.1 %conditional.6 = (bf16[640,640]{1,0:T(8,128)(2,1)}) conditional(s32[]{:T(128)} %clamp.2, (bf16[256,5120]{1,0:T(8,128)(2,1)}, bf16[64,5120]{1,0:T(8,128)(2,1)S(1)}) %tuple.123, (bf16[512,640]{1,0:T(8,128)(2,1)}, bf16[512,640]{1,0:T(8,128)(2,1)}, bf16[256,5120]{1,0:T(8,128)(2,1)}, bf16[64,5120]{1,0:T(8,128)(2,1)S(1)}, ...), branch_computations={%region_0.1_spmd, %region_1.2_spmd, %region_2.3_spmd, %region_3.4_... | conditional | flops 838860800 | bytes 4000008 | solution.py:444
  61.3 2.1 %branch.2 = bf16[640,640]{1,0:T(8,128)(2,1)} custom-call(s32[1]{0:T(128)} %constant.27.clone.place_ref, bf16[256,5120]{1,0:T(8,128)(2,1)} %get-tuple-element.155.refs_0_, bf16[64,5120]{1,0:T(8,128)(2,1)S(1)} %get-tuple-element.156.refs_1_), custom_call_target="tpu_custom_call" | custom-call | bytes 2000000 | tf_op jit(solution)/shard_map/cond/branch_0_fun/branch/pallas_call | solution.py:401
  63.4 13.1 %collective-permute-start.13 = (bf16[640,640]{1,0:T(8,128)(2,1)}, bf16[640,640]{1,0:T(8,128)(2,1)}, u32[]{:S(2)}, u32[]{:S(2)}) collective-permute-start(bf16[640,640]{1,0:T(8,128)(2,1)} %get-tuple-element.224.refs_2_), channel_id=1, source_target_pairs={{0,4},{1,5},{2,6},{3,7},{4,8},{5,9},{6,10},{7,11},{8,12},{9,13},{1... | collective-permute-start | bytes 2457608 | tf_op jit(solution)/shard_map/ppermute | solution.py:437
  83.3 13.0 %collective-permute-done.9.refs_0_ = bf16[512,640]{1,0:T(8,128)(2,1)} collective-permute-done((bf16[512,640]{1,0:T(8,128)(2,1)}, bf16[512,640]{1,0:T(8,128)(2,1)}, u32[]{:S(2)}, u32[]{:S(2)}) %collective-permute-start.9) | collective-permute-done | bytes 655392 | tf_op jit(solution)/shard_map/ppermute | solution.py:437
  97.7 2.1 %third_shard.1.refs_8_ = bf16[512,640]{1,0:T(8,128)(2,1)} custom-call(s32[1]{0:T(128)} %bitcast.1.place_ref, bf16[512,640]{1,0:T(8,128)(2,1)} %collective-permute-done.9.refs_0_, bf16[512,640]{1,0:T(8,128)(2,1)} %collective-permute-done.6.refs_0_.refs_1_, bf16[512,640]{1,0:T(8,128)(2,1)} %copy-done.6, ...), custom_call_target="tpu_custom_call" | custom-call | bytes 2000000 | tf_op jit(solution)/shard_map/third_shard/pallas_call | solution.py:401
  101.4 8.5 %collective-permute-done.7.refs_0_ = bf16[512,640]{1,0:T(8,128)(2,1)} collective-permute-done((bf16[512,640]{1,0:T(8,128)(2,1)}, bf16[512,640]{1,0:T(8,128)(2,1)}, u32[]{:S(2)}, u32[]{:S(2)}) %collective-permute-start.7) | collective-permute-done | bytes 655392 | tf_op jit(solution)/shard_map/ppermute | solution.py:437
  111.4 2.0 %last_shard.1.refs_12_ = bf16[512,640]{1,0:T(8,128)(2,1)} custom-call(s32[1]{0:T(128)} %bitcast.1.place_ref, bf16[512,640]{1,0:T(8,128)(2,1)} %collective-permute-done.7.refs_0_, bf16[512,640]{1,0:T(8,128)(2,1)} %collective-permute-done.4.refs_0_.refs_1_, bf16[640,640]{1,0:T(8,128)(2,1)} %collective-permute-done.5.refs_3_.refs_2_, ...), custom_call_target="tpu_custom_call" | custom-call | bytes 2000000 | tf_op jit(solution)/shard_map/last_shard/pallas_call | solution.py:401
  118.1 9.7 %collective-permute-done.24.refs_9_ = bf16[512,640]{1,0:T(8,128)(2,1)} collective-permute-done((bf16[512,640]{1,0:T(8,128)(2,1)}, bf16[512,640]{1,0:T(8,128)(2,1)}, u32[]{:S(2)}, u32[]{:S(2)}) %collective-permute-start.24) | collective-permute-done | bytes 655392 | tf_op jit(solution)/shard_map/ppermute | solution.py:441
  129.3 6.0 %collective-permute-done.8 = bf16[512,640]{1,0:T(8,128)(2,1)} collective-permute-done((bf16[512,640]{1,0:T(8,128)(2,1)}, bf16[512,640]{1,0:T(8,128)(2,1)}, u32[]{:S(2)}, u32[]{:S(2)}) %collective-permute-start.8) | collective-permute-done | bytes 655392 | tf_op jit(solution)/shard_map/ppermute | solution.py:437
  135.3 5.3 %collective-permute-done.27.refs_13_ = bf16[512,640]{1,0:T(8,128)(2,1)} collective-permute-done((bf16[512,640]{1,0:T(8,128)(2,1)}, bf16[512,640]{1,0:T(8,128)(2,1)}, u32[]{:S(2)}, u32[]{:S(2)}) %collective-permute-start.27) | collective-permute-done | bytes 655392 | tf_op jit(solution)/shard_map/ppermute | solution.py:441
  140.6 7.7 %collective-permute-done.11 = bf16[512,640]{1,0:T(8,128)(2,1)} collective-permute-done((bf16[512,640]{1,0:T(8,128)(2,1)}, bf16[512,640]{1,0:T(8,128)(2,1)}, u32[]{:S(2)}, u32[]{:S(2)}) %collective-permute-start.11) | collective-permute-done | bytes 655392 | tf_op jit(solution)/shard_map/ppermute | solution.py:437
  150.1 10.3 %conditional.11 = (bf16[256,2560]{1,0:T(8,128)(2,1)}) conditional(s32[]{:T(128)} %clamp.2, (bf16[256,2560]{1,0:T(8,128)(2,1)}, bf16[272,2560]{1,0:T(8,128)(2,1)}, bf16[512,640]{1,0:T(8,128)(2,1)}, bf16[512,640]{1,0:T(8,128)(2,1)}, bf16[512,640]{1,0:T(8,128)(2,1)}) %tuple.82, (bf16[256,2560]{1,0:T(8,128)(2,1)}, ...), branch_computations={%region_20.21_spmd, %region_21.22_spmd, %region_22.23_spmd, %regio... | conditional | bytes 8 | solution.py:444
  150.1 10.1 %finish.4 = bf16[256,2560]{1,0:T(8,128)(2,1)} custom-call(bf16[256,2560]{1,0:T(8,128)(2,1)} %get-tuple-element.195.refs_0_, bf16[272,2560]{1,0:T(8,128)(2,1)} %get-tuple-element.196.refs_1_, bf16[512,640]{1,0:T(8,128)(2,1)} %get-tuple-element.197.refs_2_.refs_3_, bf16[512,640]{1,0:T(8,128)(2,1)} %get-tuple-element.197.refs_2_.refs_3_, ...), custom_call_target="tpu_custom_call" | custom-call | tf_op jit(solution)/shard_map/cond/branch_0_fun/finish/pallas_call | solution.py:317
  160.5 9.1 %cross.1 = bf16[256,2560]{1,0:T(8,128)(2,1)} custom-call(s32[1]{0:T(128)} %bitcast.3.pick_ref, bf16[256,2560]{1,0:T(8,128)(2,1)} %query.3, bf16[512,640]{1,0:T(8,128)(2,1)S(1)} %copy-done, bf16[512,640]{1,0:T(8,128)(2,1)S(1)} %collective-permute-done.18.refs_1_, bf16[512,640]{1,0:T(8,128)(2,1)S(1)} %collective-permute-done.19.refs_2_, ...), custom_call_target="tpu_custom_call" | custom-call | flops 1342177280 | bytes 12000000 | tf_op jit(solution)/shard_map/cross/pallas_call | solution.py:361
  (80 shorter events, 34.2 us)
Async XLA Ops:
  2.8 24.5 %collective-permute-start.3 = (bf16[512,640]{1,0:T(8,128)(2,1)}, bf16[512,640]{1,0:T(8,128)(2,1)}, u32[]{:S(2)}, u32[]{:S(2)}) collective-permute-start(bf16[512,640]{1,0:T(8,128)(2,1)} %prompt.1.refs_0_), channel_id=1, source_target_pairs={{0,4},{1,5},{2,6},{3,7},{4,8},{5,9},{6,10},{7,11},{8,12},{9,13},{1... | collective-permute-start | bytes 1966088 | tf_op jit(solution)/shard_map/ppermute | solution.py:437
  11.0 30.1 %collective-permute-start.2 = (bf16[640,640]{1,0:T(8,128)(2,1)}, bf16[640,640]{1,0:T(8,128)(2,1)}, u32[]{:S(2)}, u32[]{:S(2)}) collective-permute-start(bf16[640,640]{1,0:T(8,128)(2,1)} %send_c.1.refs_2_), channel_id=1, source_target_pairs={{0,4},{1,5},{2,6},{3,7},{4,8},{5,9},{6,10},{7,11},{16,20},{17,21},... | collective-permute-start | bytes 2457608 | tf_op jit(solution)/shard_map/ppermute | solution.py:437
  15.8 22.1 %collective-permute-start.1 = (bf16[512,640]{1,0:T(8,128)(2,1)}, bf16[512,640]{1,0:T(8,128)(2,1)S(1)}, u32[]{:S(2)}, u32[]{:S(2)}) collective-permute-start(bf16[512,640]{1,0:T(8,128)(2,1)} %send_b.1.refs_2_), channel_id=1, source_target_pairs={{12,8},{13,9},{14,10},{15,11},{8,4},{9,5},{10,6},{11,7},{4,0},{5,1... | collective-permute-start | bytes 1966088 | tf_op jit(solution)/shard_map/ppermute | solution.py:437
  18.1 29.9 %collective-permute-start = (bf16[512,640]{1,0:T(8,128)(2,1)}, bf16[512,640]{1,0:T(8,128)(2,1)}, u32[]{:S(2)}, u32[]{:S(2)}) collective-permute-start(bf16[512,640]{1,0:T(8,128)(2,1)} %send_d.1._), channel_id=1, source_target_pairs={{12,4},{13,5},{14,6},{15,7},{4,0},{5,1},{6,2},{7,3},{28,20},{29,21... | collective-permute-start | bytes 1966088 | tf_op jit(solution)/shard_map/ppermute | solution.py:437
  30.3 28.5 %collective-permute-start.6 = (bf16[512,640]{1,0:T(8,128)(2,1)}, bf16[512,640]{1,0:T(8,128)(2,1)}, u32[]{:S(2)}, u32[]{:S(2)}) collective-permute-start(bf16[512,640]{1,0:T(8,128)(2,1)} %send_f.1.refs_2_), channel_id=1, source_target_pairs={{12,8},{13,9},{14,10},{15,11},{8,4},{9,5},{10,6},{11,7},{28,24},{2... | collective-permute-start | bytes 1966088 | tf_op jit(solution)/shard_map/ppermute | solution.py:437
  31.9 29.4 %collective-permute-start.5 = (bf16[640,640]{1,0:T(8,128)(2,1)}, bf16[640,640]{1,0:T(8,128)(2,1)}, u32[]{:S(2)}, u32[]{:S(2)}) collective-permute-start(bf16[640,640]{1,0:T(8,128)(2,1)} %send_e.1.refs_2_), channel_id=1, source_target_pairs={{0,4},{1,5},{2,6},{3,7},{4,8},{5,9},{6,10},{7,11},{8,12},{9,13},{1... | collective-permute-start | bytes 2457608 | tf_op jit(solution)/shard_map/ppermute | solution.py:437
  37.9 38.6 %collective-permute-start.18 = (bf16[512,640]{1,0:T(8,128)(2,1)S(1)}, bf16[512,640]{1,0:T(8,128)(2,1)S(1)}, u32[]{:S(2)}, u32[]{:S(2)}) collective-permute-start(bf16[512,640]{1,0:T(8,128)(2,1)S(1)} %copy-done), channel_id=1, source_target_pairs={{0,2},{1,3},{2,0},{3,1},{4,6},{5,7},{6,4},{7,5},{8,10},{9,11},{10,... | collective-permute-start | bytes 1966088 | tf_op jit(solution)/shard_map/ppermute | solution.py:441
  41.0 35.5 %collective-permute-start.19 = (bf16[512,640]{1,0:T(8,128)(2,1)S(1)}, bf16[512,640]{1,0:T(8,128)(2,1)S(1)}, u32[]{:S(2)}, u32[]{:S(2)}) collective-permute-start(bf16[512,640]{1,0:T(8,128)(2,1)S(1)} %copy-done), channel_id=1, source_target_pairs={{0,1},{1,0},{2,3},{3,2},{4,5},{5,4},{6,7},{7,6},{8,9},{9,8},{10,11... | collective-permute-start | bytes 1966088 | tf_op jit(solution)/shard_map/ppermute | solution.py:441
  48.0 32.4 %collective-permute-start.12 = (bf16[640,640]{1,0:T(8,128)(2,1)}, bf16[640,640]{1,0:T(8,128)(2,1)}, u32[]{:S(2)}, u32[]{:S(2)}) collective-permute-start(bf16[640,640]{1,0:T(8,128)(2,1)} %send_g.1.refs_2_), channel_id=1, source_target_pairs={{0,4},{1,5},{2,6},{3,7},{4,8},{5,9},{6,10},{7,11},{16,20},{17,21},... | collective-permute-start | bytes 2457608 | tf_op jit(solution)/shard_map/ppermute | solution.py:437
  58.8 19.0 %collective-permute-start.4 = (bf16[512,640]{1,0:T(8,128)(2,1)}, bf16[512,640]{1,0:T(8,128)(2,1)}, u32[]{:S(2)}, u32[]{:S(2)}) collective-permute-start(bf16[512,640]{1,0:T(8,128)(2,1)} %send_i.1.refs_3_), channel_id=1, source_target_pairs={{12,8},{13,9},{14,10},{15,11},{8,4},{9,5},{10,6},{11,7},{28,24},{2... | collective-permute-start | bytes 1966088 | tf_op jit(solution)/shard_map/ppermute | solution.py:437
  63.4 32.8 %collective-permute-start.13 = (bf16[640,640]{1,0:T(8,128)(2,1)}, bf16[640,640]{1,0:T(8,128)(2,1)}, u32[]{:S(2)}, u32[]{:S(2)}) collective-permute-start(bf16[640,640]{1,0:T(8,128)(2,1)} %get-tuple-element.224.refs_2_), channel_id=1, source_target_pairs={{0,4},{1,5},{2,6},{3,7},{4,8},{5,9},{6,10},{7,11},{8,12},{9,13},{1... | collective-permute-start | bytes 2457608 | tf_op jit(solution)/shard_map/ppermute | solution.py:437
  76.5 19.7 %collective-permute-start.9 = (bf16[512,640]{1,0:T(8,128)(2,1)}, bf16[512,640]{1,0:T(8,128)(2,1)}, u32[]{:S(2)}, u32[]{:S(2)}) collective-permute-start(bf16[512,640]{1,0:T(8,128)(2,1)} %send_k.1), channel_id=1, source_target_pairs={{12,8},{13,9},{14,10},{15,11},{8,4},{9,5},{10,6},{11,7},{4,0},{5,1... | collective-permute-start | bytes 1966088 | tf_op jit(solution)/shard_map/ppermute | solution.py:437
  77.8 22.1 %collective-permute-start.21 = (bf16[512,640]{1,0:T(8,128)(2,1)S(1)}, bf16[512,640]{1,0:T(8,128)(2,1)}, u32[]{:S(2)}, u32[]{:S(2)}) collective-permute-start(bf16[512,640]{1,0:T(8,128)(2,1)S(1)} %copy-done.1), channel_id=1, source_target_pairs={{0,2},{1,3},{2,0},{3,1},{4,6},{5,7},{6,4},{7,5},{8,10},{9,11},{10,... | collective-permute-start | bytes 1966088 | tf_op jit(solution)/shard_map/ppermute | solution.py:441
  80.4 29.5 %collective-permute-start.7 = (bf16[512,640]{1,0:T(8,128)(2,1)}, bf16[512,640]{1,0:T(8,128)(2,1)}, u32[]{:S(2)}, u32[]{:S(2)}) collective-permute-start(bf16[512,640]{1,0:T(8,128)(2,1)} %send_l.1), channel_id=1, source_target_pairs={{8,4},{9,5},{10,6},{11,7},{4,0},{5,1},{6,2},{7,3},{24,20},{25,21},... | collective-permute-start | bytes 1966088 | tf_op jit(solution)/shard_map/ppermute | solution.py:437
  81.7 33.1 %collective-permute-start.14 = (bf16[544,640]{1,0:T(8,128)(2,1)}, bf16[544,640]{1,0:T(8,128)(2,1)}, u32[]{:S(2)}, u32[]{:S(2)}) collective-permute-start(bf16[544,640]{1,0:T(8,128)(2,1)} %get-tuple-element.225.refs_4_), channel_id=1, source_target_pairs={{4,8},{5,9},{6,10},{7,11},{8,12},{9,13},{10,14},{11,15},{20,24},{2... | collective-permute-start | bytes 2088968 | tf_op jit(solution)/shard_map/ppermute | solution.py:437
  96.3 19.1 %collective-permute-start.10 = (bf16[512,640]{1,0:T(8,128)(2,1)}, bf16[512,640]{1,0:T(8,128)(2,1)}, u32[]{:S(2)}, u32[]{:S(2)}) collective-permute-start(bf16[512,640]{1,0:T(8,128)(2,1)} %collective-permute-done.9.refs_0_), channel_id=1, source_target_pairs={{8,4},{9,5},{10,6},{11,7},{24,20},{25,21},{26,22},{27,23}} | collective-permute-start | bytes 1966088 | tf_op jit(solution)/shard_map/ppermute | solution.py:437
  109.9 18.0 %collective-permute-start.24 = (bf16[512,640]{1,0:T(8,128)(2,1)}, bf16[512,640]{1,0:T(8,128)(2,1)}, u32[]{:S(2)}, u32[]{:S(2)}) collective-permute-start(bf16[512,640]{1,0:T(8,128)(2,1)} %third_shard.1.refs_8_), channel_id=1, source_target_pairs={{0,2},{1,3},{2,0},{3,1},{4,6},{5,7},{6,4},{7,5},{8,10},{9,11},{10,... | collective-permute-start | bytes 1966088 | tf_op jit(solution)/shard_map/ppermute | solution.py:441
  113.5 21.8 %collective-permute-start.8 = (bf16[512,640]{1,0:T(8,128)(2,1)}, bf16[512,640]{1,0:T(8,128)(2,1)}, u32[]{:S(2)}, u32[]{:S(2)}) collective-permute-start(bf16[512,640]{1,0:T(8,128)(2,1)} %collective-permute-done.7.refs_0_), channel_id=1, source_target_pairs={{4,0},{5,1},{6,2},{7,3},{20,16},{21,17},{22,18},{23,19}} | collective-permute-start | bytes 1966088 | tf_op jit(solution)/shard_map/ppermute | solution.py:437
  114.8 25.8 %collective-permute-start.27 = (bf16[512,640]{1,0:T(8,128)(2,1)}, bf16[512,640]{1,0:T(8,128)(2,1)}, u32[]{:S(2)}, u32[]{:S(2)}) collective-permute-start(bf16[512,640]{1,0:T(8,128)(2,1)} %last_shard.1.refs_12_), channel_id=1, source_target_pairs={{0,2},{1,3},{2,0},{3,1},{4,6},{5,7},{6,4},{7,5},{8,10},{9,11},{10,... | collective-permute-start | bytes 1966088 | tf_op jit(solution)/shard_map/ppermute | solution.py:441
  115.4 32.9 %collective-permute-start.11 = (bf16[512,640]{1,0:T(8,128)(2,1)}, bf16[512,640]{1,0:T(8,128)(2,1)}, u32[]{:S(2)}, u32[]{:S(2)}) collective-permute-start(bf16[512,640]{1,0:T(8,128)(2,1)} %collective-permute-done.10), channel_id=1, source_target_pairs={{4,0},{5,1},{6,2},{7,3},{20,16},{21,17},{22,18},{23,19}} | collective-permute-start | bytes 1966088 | tf_op jit(solution)/shard_map/ppermute | solution.py:437
  127.9 20.4 %collective-permute-start.17 = (bf16[272,640]{1,0:T(8,128)(2,1)}, bf16[272,640]{1,0:T(8,128)(2,1)}, u32[]{:S(2)}, u32[]{:S(2)}) collective-permute-start(bf16[272,640]{1,0:T(8,128)(2,1)} %get-tuple-element.228), channel_id=1, source_target_pairs={{8,12},{9,13},{10,14},{11,15},{24,28},{25,29},{26,30},{27,31}} | collective-permute-start | bytes 1044488 | tf_op jit(solution)/shard_map/ppermute | solution.py:437
  129.2 31.2 %collective-permute-start.23 = (bf16[512,640]{1,0:T(8,128)(2,1)}, bf16[512,640]{1,0:T(8,128)(2,1)}, u32[]{:S(2)}, u32[]{:S(2)}) collective-permute-start(bf16[512,640]{1,0:T(8,128)(2,1)} %collective-permute-done.21.refs_5_), channel_id=1, source_target_pairs={{0,1},{1,0},{2,3},{3,2},{4,5},{5,4},{6,7},{7,6},{8,9},{9,8},{10,11... | collective-permute-start | bytes 1966088 | tf_op jit(solution)/shard_map/ppermute | solution.py:441
  135.3 25.2 %collective-permute-start.25 = (bf16[512,640]{1,0:T(8,128)(2,1)}, bf16[512,640]{1,0:T(8,128)(2,1)}, u32[]{:S(2)}, u32[]{:S(2)}) collective-permute-start(bf16[512,640]{1,0:T(8,128)(2,1)} %third_shard.1.refs_8_), channel_id=1, source_target_pairs={{0,1},{1,0},{2,3},{3,2},{4,5},{5,4},{6,7},{7,6},{8,9},{9,8},{10,11... | collective-permute-start | bytes 1966088 | tf_op jit(solution)/shard_map/ppermute | solution.py:441
  140.6 19.9 %collective-permute-start.28 = (bf16[512,640]{1,0:T(8,128)(2,1)}, bf16[512,640]{1,0:T(8,128)(2,1)}, u32[]{:S(2)}, u32[]{:S(2)}) collective-permute-start(bf16[512,640]{1,0:T(8,128)(2,1)} %last_shard.1.refs_12_), channel_id=1, source_target_pairs={{0,1},{1,0},{2,3},{3,2},{4,5},{5,4},{6,7},{7,6},{8,9},{9,8},{10,11... | collective-permute-start | bytes 1966088 | tf_op jit(solution)/shard_map/ppermute | solution.py:441
  (14 other events, 177.7 us)

commit v2 on v1

--- a/solution.py
+++ b/solution.py
@@ -68,6 +68,33 @@
     beside = jnp.concatenate([values, jnp.ones_like(values)], axis=1)
     both = jnp.dot(weights, beside, preferred_element_type=jnp.float32)
     return top * LOG_SCALE, both[:, HDIM:], both[:, :HDIM]
+
+
+def merge_rows(parts, frame):
+    eye = diagonal()
+    groups = frame // HDIM
+    logs = []
+    for part in parts:
+        tile = part[frame : frame + 3 * groups].astype(jnp.float32)
+        logs.append(
+            tile[:groups] + tile[groups : 2 * groups] + tile[2 * groups : 3 * groups]
+        )
+    top = logs[0]
+    for each in logs[1:]:
+        top = jnp.maximum(top, each)
+    shares = [jnp.exp2(each - top) for each in logs]
+    total = shares[0]
+    for each in shares[1:]:
+        total = total + each
+    merged = []
+    for group in range(groups):
+        rows = 0.0
+        for part, share in zip(parts, shares):
+            row = (share / total)[group : group + 1]
+            column = jnp.sum(jnp.where(eye, row, 0.0), axis=1, keepdims=True)
+            rows = rows + column * part[group * HDIM : (group + 1) * HDIM].astype(jnp.float32)
+        merged.append(rows)
+    return jnp.concatenate(merged, axis=0)
 
 
 def merge_states(states):
@@ -222,19 +249,20 @@
     )(queries, frame_kv, frame_kv, sink, sink, after)
 
 
-def finish(queries, at_home, sinks, came, extra, sink_rows):
+def finish(queries, at_home, sinks, came, extra, sink_rows, own=None):
     frame = queries.shape[0]
     as_keys = bool(came) and len(came) == CHUNKS and bool(sinks)
     rows = 2 * frame + 2 * sink_rows
     came_rows = rows if as_keys else frame + STAT
     moved = [(each, came_rows) for each in came] + [(each, rows) for each in extra]
+    pairs = 2 * len(sinks) + (4 if own else 0)
 
     def kernel(*refs):
         query, home_ref = refs[:2]
-        sink_refs = refs[2 : 2 + 2 * len(sinks)]
-        sources = refs[2 + 2 * len(sinks) : 2 + 2 * len(sinks) + len(moved)]
-        out = refs[2 + 2 * len(sinks) + len(moved)]
-        held = refs[3 + 2 * len(sinks) + len(moved) : -1]
+        sink_refs = refs[2 : 2 + pairs]
+        sources = refs[2 + pairs : 2 + pairs + len(moved)]
+        out = refs[2 + pairs + len(moved)]
+        held = refs[3 + pairs + len(moved) : -1]
         sems = refs[-1]
         step = pl.program_id(0)
 
@@ -266,10 +294,13 @@
                 for buffer, which in key_places:
                     keys += [buffer[which, :frame, cols], buffer[which, 2 * frame : 2 * frame + sink_rows, cols]]
                     values += [buffer[which, frame : 2 * frame, cols], buffer[which, 2 * frame + sink_rows :, cols]]
-                parts = [home_ref[:, cols]]
+                parts = [] if own else [home_ref[:, cols]]
                 if part_place is not None:
                     parts.append(part_place[0][part_place[1], :, cols])
-                states = [fresh_state(query[:, cols], stacked(keys), stacked(values))] if keys else []
+                if not keys:
+                    out[:, cols] = merge_rows(parts, frame).astype(jnp.bfloat16)
+                    continue
+                states = [fresh_state(query[:, cols], stacked(keys), stacked(values))]
                 for part in parts:
                     states.append(
                         (
@@ -309,6 +340,14 @@
             pl.BlockSpec((sink_rows, CW), lambda at: (at, 0)),
             pl.BlockSpec((sink_rows, CW), lambda at: (CHUNKS + at, 0)),
         ]
+    own_arrays = []
+    if own:
+        for array in own:
+            for first in (0, CHUNKS):
+                own_arrays.append(array)
+                in_specs.append(
+                    pl.BlockSpec((array.shape[0], CW), lambda at, first=first: (0, first + at))
+                )
     scratch = []
     if came:
         scratch.append(pltpu.VMEM((len(came), came_rows, CW), jnp.bfloat16))
@@ -323,52 +362,69 @@
         scratch_shapes=scratch + [pltpu.SemaphoreType.DMA((max(len(moved), 1),))],
         compiler_params=pltpu.CompilerParams(vmem_limit_bytes=VMEM),
         name="finish",
-    )(queries, at_home, *[each for sink in sinks for each in (sink, sink)], *[each for each, _ in moved])
+    )(
+        queries,
+        at_home,
+        *[each for sink in sinks for each in (sink, sink)],
+        *own_arrays,
+        *[each for each, _ in moved],
+    )
 
 
 def cross(queries, shards, pick, prompt_rows, after):
     frame = queries.shape[0]
-    step = 2 * prompt_rows
-    size = 2 * CHUNKS * step
-    count = sum(each.shape[0] for each in shards) // size
+    blocks = 2 * CHUNKS
+    parts = [each.reshape(blocks, 2, prompt_rows, CW) for each in shards]
+    while parts[0].shape[2] % 16:
+        half = len(parts) // 2
+        parts = [
+            jnp.concatenate([one, other], axis=2) for one, other in zip(parts[:half], parts[half:])
+        ]
+    rows = parts[0].shape[2]
+    tokens = rows * len(parts)
 
     def kernel(pick_ref, query, *refs):
-        out = refs[-1]
-        picked = pick_ref[0] * prompt_rows
+        out, held, sems = refs[-3:]
+        copies = [
+            pltpu.make_async_copy(
+                refs[n].at[:, pick_ref[0]], held.at[:, pl.ds(n * rows, rows)], sems.at[n]
+            )
+            for n in range(len(parts))
+        ]
+        for copy in copies:
+            copy.start()
+        for copy in copies:
+            copy.wait()
 
         def chunk(at, carry):
-            def pieces(which, cols):
-                return stacked(
-                    [
-                        ref[pl.ds(pl.multiple_of(first + which * step + picked, 8), prompt_rows), cols]
-                        for ref in refs[: len(shards)]
-                        for first in range(0, ref.shape[0], size)
-                    ]
-                )
-
             left = pl.multiple_of(at * CW, HDIM)
             for head in range(PER):
                 cols = pl.ds(head * HDIM, HDIM)
-                keys, values = pieces(at, cols), pieces(CHUNKS + at, cols)
                 here = pl.ds(left + head * HDIM, HDIM)
-                _, total, blended = fresh_state(query[:, here], keys, values)
+                _, total, blended = fresh_state(
+                    query[:, here], held[at, :, cols], held[CHUNKS + at, :, cols]
+                )
                 out[:, here] = (blended / total).astype(jnp.bfloat16)
             return carry
 
         lax.fori_loop(0, CHUNKS, chunk, 0)
 
-    work = HEADS * frame * prompt_rows * count
+    work = HEADS * frame * tokens
     return pl.pallas_call(
         kernel,
         out_shape=jax.ShapeDtypeStruct(queries.shape, jnp.bfloat16),
-        in_specs=[SCALAR] + [INSIDE] * (1 + len(shards)) + [ANYWHERE],
+        in_specs=[SCALAR, INSIDE] + [ANYWHERE] * (len(parts) + 1),
         out_specs=INSIDE,
+        scratch_shapes=[
+            pltpu.VMEM((blocks, tokens, CW), jnp.bfloat16),
+            pltpu.SemaphoreType.DMA((len(parts),)),
+        ],
         compiler_params=pltpu.CompilerParams(vmem_limit_bytes=VMEM),
         cost_estimate=pl.CostEstimate(
             flops=4 * work * HDIM, bytes_accessed=12_000_000, transcendentals=work
         ),
         name="cross",
-    )(pick, queries, *shards, after)
+    )(pick, queries, *parts, after)
 
 
 def pack(place, rows, plans, name="pack", after=()):
@@ -504,11 +560,6 @@
             held = held + [across(each, flip) for each in held]
             flip //= 2
         return held
-
-    planes = [[at * streams + s for s in range(streams)] for at in range(WIN)]
-
-    def gathered(shard):
-        return [lax.all_gather(shard, "span", axis_index_groups=planes, axis=0, tiled=True)]
 
     stream_ids = jnp.arange(switch.shape[0], dtype=jnp.int32)
     switch_at = jnp.sum(jnp.where(stream_ids == stream, switch, 0))
@@ -718,7 +769,7 @@
             3: whole(up_h, prompt_size),
         },
         name="last_shard",
-        after=(send_n,),
+        after=(stages[6], send_n,),
     )
     stages += spread(last)
     send_o = choose(
@@ -753,22 +804,22 @@
     up_q = move(send_q, (2, 3))
 
 
-    def finish0(q, h, x, u, d):
-        return finish(q, h, [d["d"], d["o"], d["r"]], [], [], sink_rows)
-
-    def finish1(q, h, x, u, d):
+    def finish0(q, h, f, s, x, u, d):
+        return finish(q, h, [d["d"], d["o"], d["r"]], [], [], sink_rows, (f, s))
+
+    def finish1(q, h, f, s, x, u, d):
         return finish(q, h, [d["l"], d["m"]], [u["e"], u["g"], u["h"], u["c"]], [], sink_rows)
 
-    def finish2(q, h, x, u, d):
+    def finish2(q, h, f, s, x, u, d):
         return finish(q, h, [d["k"]], [u["h"], u["j"], u["n"]], [u["c"], u["g"]], sink_rows)
 
-    def finish3(q, h, x, u, d):
+    def finish3(q, h, f, s, x, u, d):
         return finish(q, h, [], [u["n"], u["o"], u["q"], u["j"]], [], sink_rows)
 
     ups = {"c": up_c, "e": up_e, "g": up_g, "h": up_h, "j": up_j, "n": up_n, "o": up_o, "q": up_q}
     downs = {"d": down_d, "k": down_k, "l": down_l, "m": down_m, "o": down_o, "r": down_r}
     self_out = choose(
-        [finish0, finish1, finish2, finish3], queries, at_home, cross_out, ups, downs
+        [finish0, finish1, finish2, finish3], queries, at_home, frame_kv, sink, cross_out, ups, downs
     )
     return (self_out, cross_out)
 

time: 170 us -> 167 us (0.982)
  Pallas kernels: 46.9 us -> 44.2 us
  waiting for transfers between devices: 55 us -> 52.8 us
    pallas_call x1, Pallas kernels: 10.1 us -> 7.48 us  [finish(): pl.pallas_call(kernel, out_shape=jax.ShapeDtypeStruct(queries.shape, jnp....]
    ppermute x18, waiting for transfers between devices: 39.9 us -> 37.7 us  [move(): return lax.ppermute(value, 'span', both)]
  transfers between devices with their start and end apart: 30 -> 30, of which waited for: 8 -> 8; matrix products, arithmetic and copies ran while one was open for 0% -> 0% of each run, Pallas kernels for 21% -> 20%
where the time goes in v2:
time: 167 us; the launch traced here: 166 us
  starting transfers between devices  64.4 us (39%)
  waiting for transfers between devices  52.8 us (32%)
  Pallas kernels  44.2 us (26%)
  local copies, waits for them, and re-layouts  1.97 us (1%)
  between operations  1.91 us (1%)
    ppermute x18, starting transfers between devices, move(): return lax.ppermute(value, 'span', both)  58.2 us
    ppermute x18, waiting for transfers between devices, move(): return lax.ppermute(value, 'span', both)  37.7 us
    pallas_call x14, Pallas kernels, pack(): pl.pallas_call(kernel, out_shape=jax.ShapeDtypeStruct((rows, CW), jnp.bfl...  20.8 us
    ppermute x12, waiting for transfers between devices, across(): return lax.ppermute(value, 'span', pairs)  15.1 us
    pallas_call x1, Pallas kernels, cross(): pl.pallas_call(kernel, out_shape=jax.ShapeDtypeStruct(queries.shape, jnp....  9.12 us
    pallas_call x1, Pallas kernels, finish(): pl.pallas_call(kernel, out_shape=jax.ShapeDtypeStruct(queries.shape, jnp....  7.48 us
    pallas_call x1, Pallas kernels, home(): pl.pallas_call(kernel, out_shape=jax.ShapeDtypeStruct((frame + STAT, WIDT...  6.84 us
    ppermute x12, starting transfers between devices, across(): return lax.ppermute(value, 'span', pairs)  6.2 us
  transfers between devices with their start and end apart: 30, of which 8 were waited for; matrix products, arithmetic and copies ran while one was open for 0% of the time, Pallas kernels for 20%

profile of v2, /device:TPU:0, one launch (start us, length us, event | category | flops | bytes accessed | tf_op | source)
XLA Modules:
  0.0 166.2 jit_solution(15459226610964883834)
XLA Ops:
  0.7 2.2 %prompt.1.refs_0_ = bf16[512,640]{1,0:T(8,128)(2,1)} custom-call(s32[1]{0:T(128)} %bitcast.1.place_ref, bf16[64,5120]{1,0:T(8,128)(2,1)} %bitcast.44), custom_call_target="tpu_custom_call" | custom-call | bytes 2000000 | tf_op jit(solution)/shard_map/prompt/pallas_call | solution.py:457
  2.8 6.0 %collective-permute-start.3 = (bf16[512,640]{1,0:T(8,128)(2,1)}, bf16[512,640]{1,0:T(8,128)(2,1)}, u32[]{:S(2)}, u32[]{:S(2)}) collective-permute-start(bf16[512,640]{1,0:T(8,128)(2,1)} %prompt.1.refs_0_), channel_id=1, source_target_pairs={{0,4},{1,5},{2,6},{3,7},{4,8},{5,9},{6,10},{7,11},{8,12},{9,13},{1... | collective-permute-start | bytes 1966088 | tf_op jit(solution)/shard_map/ppermute | solution.py:493
  10.9 4.9 %collective-permute-start.2 = (bf16[640,640]{1,0:T(8,128)(2,1)}, bf16[640,640]{1,0:T(8,128)(2,1)}, u32[]{:S(2)}, u32[]{:S(2)}) collective-permute-start(bf16[640,640]{1,0:T(8,128)(2,1)} %send_c.1.refs_2_), channel_id=1, source_target_pairs={{0,4},{1,5},{2,6},{3,7},{4,8},{5,9},{6,10},{7,11},{16,20},{17,21},... | collective-permute-start | bytes 2457608 | tf_op jit(solution)/shard_map/ppermute | solution.py:493
  20.5 6.8 %home.1.refs_3_ = bf16[272,2560]{1,0:T(8,128)(2,1)} custom-call(bf16[256,2560]{1,0:T(8,128)(2,1)S(1)} %copy-done.8, bf16[256,5120]{1,0:T(8,128)(2,1)} %refs_0_.6, bf16[256,5120]{1,0:T(8,128)(2,1)} %refs_0_.6, bf16[64,5120]{1,0:T(8,128)(2,1)S(1)} %bitcast.33, bf16[64,5120]{1,0:T(8,128)(2,1)S(1)} %bitcast.34, bf16[512,640]{1,0:T(8,128)(2,1)S(1)} %copy-done.4), custom_call_target="tpu_custom_call" | custom-call | flops 838860800 | bytes 6000000 | tf_op jit(solution)/shard_map/home/pallas_call | solution.py:229
  27.3 2.0 %send_e.1.refs_2_ = bf16[640,640]{1,0:T(8,128)(2,1)} custom-call(s32[1]{0:T(128)} %bitcast.1.place_ref, bf16[256,5120]{1,0:T(8,128)(2,1)} %refs_0_.6, bf16[64,5120]{1,0:T(8,128)(2,1)S(1)} %bitcast.35, bf16[512,640]{1,0:T(8,128)(2,1)} %collective-permute-done.3.refs_2_.refs_1_, bf16[272,2560]{1,0:T(8,128)(2,1)} %home.1.refs_3_), custom_call_target="tpu_custom_call" | custom-call | bytes 2000000 | tf_op jit(solution)/shard_map/send_e/pallas_call | solution.py:457
  31.8 6.0 %collective-permute-start.5 = (bf16[640,640]{1,0:T(8,128)(2,1)}, bf16[640,640]{1,0:T(8,128)(2,1)}, u32[]{:S(2)}, u32[]{:S(2)}) collective-permute-start(bf16[640,640]{1,0:T(8,128)(2,1)} %send_e.1.refs_2_), channel_id=1, source_target_pairs={{0,4},{1,5},{2,6},{3,7},{4,8},{5,9},{6,10},{7,11},{8,12},{9,13},{1... | collective-permute-start | bytes 2457608 | tf_op jit(solution)/shard_map/ppermute | solution.py:493
  41.0 1.8 %second_shard.1.refs_3_ = bf16[512,640]{1,0:T(8,128)(2,1)} custom-call(s32[1]{0:T(128)} %bitcast.1.place_ref, bf16[512,640]{1,0:T(8,128)(2,1)S(1)} %collective-permute-done.1.refs_0_.refs_2_, bf16[512,640]{1,0:T(8,128)(2,1)} %collective-permute-done.3.refs_2_.refs_1_, bf16[512,640]{1,0:T(8,128)(2,1)} %send_f.1.refs_2_), custom_call_target="tpu_custom_call" | custom-call | bytes 2000000 | tf_op jit(solution)/shard_map/second_shard/pallas_call | solution.py:457
  42.8 2.0 %send_g.1.refs_2_ = bf16[640,640]{1,0:T(8,128)(2,1)} custom-call(s32[1]{0:T(128)} %bitcast.1.place_ref, bf16[256,5120]{1,0:T(8,128)(2,1)} %refs_0_.6, bf16[64,5120]{1,0:T(8,128)(2,1)S(1)} %bitcast.36, bf16[640,640]{1,0:T(8,128)(2,1)} %collective-permute-done.2.refs_2_, bf16[512,640]{1,0:T(8,128)(2,1)} %second_shard.1.refs_3_), custom_call_target="tpu_custom_call" | custom-call | bytes 2000000 | tf_op jit(solution)/shard_map/send_g/pallas_call | solution.py:457
  44.9 3.1 %collective-permute-done = bf16[512,640]{1,0:T(8,128)(2,1)} collective-permute-done((bf16[512,640]{1,0:T(8,128)(2,1)}, bf16[512,640]{1,0:T(8,128)(2,1)}, u32[]{:S(2)}, u32[]{:S(2)}) %collective-permute-start) | collective-permute-done | bytes 655392 | tf_op jit(solution)/shard_map/ppermute | solution.py:493
  48.0 9.9 %collective-permute-start.12 = (bf16[640,640]{1,0:T(8,128)(2,1)}, bf16[640,640]{1,0:T(8,128)(2,1)}, u32[]{:S(2)}, u32[]{:S(2)}) collective-permute-start(bf16[640,640]{1,0:T(8,128)(2,1)} %send_g.1.refs_2_), channel_id=1, source_target_pairs={{0,4},{1,5},{2,6},{3,7},{4,8},{5,9},{6,10},{7,11},{16,20},{17,21},... | collective-permute-start | bytes 2457608 | tf_op jit(solution)/shard_map/ppermute | solution.py:493
  61.3 2.1 %conditional.6 = (bf16[640,640]{1,0:T(8,128)(2,1)}) conditional(s32[]{:T(128)} %clamp.2, (bf16[256,5120]{1,0:T(8,128)(2,1)}, bf16[64,5120]{1,0:T(8,128)(2,1)S(1)}) %tuple.122, (bf16[512,640]{1,0:T(8,128)(2,1)}, bf16[512,640]{1,0:T(8,128)(2,1)}, bf16[256,5120]{1,0:T(8,128)(2,1)}, bf16[64,5120]{1,0:T(8,128)(2,1)S(1)}, ...), branch_computations={%region_0.1_spmd, %region_1.2_spmd, %region_2.3_spmd, %region_3.4_... | conditional | flops 838860800 | bytes 4000008 | solution.py:500
  61.3 2.1 %branch.2 = bf16[640,640]{1,0:T(8,128)(2,1)} custom-call(s32[1]{0:T(128)} %constant.27.clone.place_ref, bf16[256,5120]{1,0:T(8,128)(2,1)} %get-tuple-element.159.refs_0_, bf16[64,5120]{1,0:T(8,128)(2,1)S(1)} %get-tuple-element.160.refs_1_), custom_call_target="tpu_custom_call" | custom-call | bytes 2000000 | tf_op jit(solution)/shard_map/cond/branch_0_fun/branch/pallas_call | solution.py:457
  63.4 13.1 %collective-permute-start.13 = (bf16[640,640]{1,0:T(8,128)(2,1)}, bf16[640,640]{1,0:T(8,128)(2,1)}, u32[]{:S(2)}, u32[]{:S(2)}) collective-permute-start(bf16[640,640]{1,0:T(8,128)(2,1)} %get-tuple-element.230.refs_2_), channel_id=1, source_target_pairs={{0,4},{1,5},{2,6},{3,7},{4,8},{5,9},{6,10},{7,11},{8,12},{9,13},{1... | collective-permute-start | bytes 2457608 | tf_op jit(solution)/shard_map/ppermute | solution.py:493
  82.2 14.0 %collective-permute-done.9.refs_0_ = bf16[512,640]{1,0:T(8,128)(2,1)} collective-permute-done((bf16[512,640]{1,0:T(8,128)(2,1)}, bf16[512,640]{1,0:T(8,128)(2,1)}, u32[]{:S(2)}, u32[]{:S(2)}) %collective-permute-start.9) | collective-permute-done | bytes 655392 | tf_op jit(solution)/shard_map/ppermute | solution.py:493
  99.2 2.0 %third_shard.1 = bf16[512,640]{1,0:T(8,128)(2,1)} custom-call(s32[1]{0:T(128)} %bitcast.1.place_ref, bf16[512,640]{1,0:T(8,128)(2,1)} %collective-permute-done.9.refs_0_, bf16[512,640]{1,0:T(8,128)(2,1)} %collective-permute-done.6.refs_0_.refs_1_, bf16[512,640]{1,0:T(8,128)(2,1)} %copy-done.9, bf16[640,640]{1,0:T(8,128)(2,1)} %collective-permute-done.5.refs_3_.refs_2_, ...), custom_call_target="tpu_custom_call" | custom-call | bytes 2000000 | tf_op jit(solution)/shard_map/third_shard/pallas_call | solution.py:457
  103.8 6.1 %collective-permute-done.7.refs_0_ = bf16[512,640]{1,0:T(8,128)(2,1)} collective-permute-done((bf16[512,640]{1,0:T(8,128)(2,1)}, bf16[512,640]{1,0:T(8,128)(2,1)}, u32[]{:S(2)}, u32[]{:S(2)}) %collective-permute-start.7) | collective-permute-done | bytes 655392 | tf_op jit(solution)/shard_map/ppermute | solution.py:493
  111.4 2.0 %last_shard.1 = bf16[512,640]{1,0:T(8,128)(2,1)} custom-call(s32[1]{0:T(128)} %bitcast.1.place_ref, bf16[512,640]{1,0:T(8,128)(2,1)} %collective-permute-done.7.refs_0_, bf16[512,640]{1,0:T(8,128)(2,1)} %collective-permute-done.4.refs_0_.refs_1_, bf16[640,640]{1,0:T(8,128)(2,1)} %collective-permute-done.5.refs_3_.refs_2_, ...), custom_call_target="tpu_custom_call" | custom-call | bytes 2000000 | tf_op jit(solution)/shard_map/last_shard/pallas_call | solution.py:457
  118.1 9.7 %collective-permute-done.24 = bf16[512,640]{1,0:T(8,128)(2,1)} collective-permute-done((bf16[512,640]{1,0:T(8,128)(2,1)}, bf16[512,640]{1,0:T(8,128)(2,1)}, u32[]{:S(2)}, u32[]{:S(2)}) %collective-permute-start.24) | collective-permute-done | bytes 655392 | tf_op jit(solution)/shard_map/ppermute | solution.py:497
  129.2 6.0 %collective-permute-done.8 = bf16[512,640]{1,0:T(8,128)(2,1)} collective-permute-done((bf16[512,640]{1,0:T(8,128)(2,1)}, bf16[512,640]{1,0:T(8,128)(2,1)}, u32[]{:S(2)}, u32[]{:S(2)}) %collective-permute-start.8) | collective-permute-done | bytes 655392 | tf_op jit(solution)/shard_map/ppermute | solution.py:493
  135.3 5.3 %collective-permute-done.27 = bf16[512,640]{1,0:T(8,128)(2,1)} collective-permute-done((bf16[512,640]{1,0:T(8,128)(2,1)}, bf16[512,640]{1,0:T(8,128)(2,1)}, u32[]{:S(2)}, u32[]{:S(2)}) %collective-permute-start.27) | collective-permute-done | bytes 655392 | tf_op jit(solution)/shard_map/ppermute | solution.py:497
  140.6 6.8 %collective-permute-done.11 = bf16[512,640]{1,0:T(8,128)(2,1)} collective-permute-done((bf16[512,640]{1,0:T(8,128)(2,1)}, bf16[512,640]{1,0:T(8,128)(2,1)}, u32[]{:S(2)}, u32[]{:S(2)}) %collective-permute-start.11) | collective-permute-done | bytes 655392 | tf_op jit(solution)/shard_map/ppermute | solution.py:493
  149.2 7.7 %conditional.11 = (bf16[256,2560]{1,0:T(8,128)(2,1)}) conditional(s32[]{:T(128)} %clamp.2, (bf16[256,2560]{1,0:T(8,128)(2,1)}, bf16[272,2560]{1,0:T(8,128)(2,1)}, bf16[512,640]{1,0:T(8,128)(2,1)}, bf16[512,640]{1,0:T(8,128)(2,1)}, bf16[512,640]{1,0:T(8,128)(2,1)}, /*index=5*/bf16[256,5120]{1,0:T(8,128)(2,1)}, ...), branch_computations={%region_20.21_spmd, %region_21.22_spmd, %region_22.23_spmd, %regio... | conditional | bytes 8 | solution.py:500
  149.2 7.5 %finish.4 = bf16[256,2560]{1,0:T(8,128)(2,1)} custom-call(bf16[256,2560]{1,0:T(8,128)(2,1)} %get-tuple-element.199.refs_0_, bf16[272,2560]{1,0:T(8,128)(2,1)} %get-tuple-element.200.refs_1_, bf16[512,640]{1,0:T(8,128)(2,1)} %get-tuple-element.201.refs_2_.refs_3_, bf16[512,640]{1,0:T(8,128)(2,1)} %get-tuple-element.201.refs_2_.refs_3_, ...), custom_call_target="tpu_custom_call" | custom-call | tf_op jit(solution)/shard_map/cond/branch_0_fun/finish/pallas_call | solution.py:356
  156.9 9.1 %cross.1 = bf16[256,2560]{1,0:T(8,128)(2,1)} custom-call(s32[1]{0:T(128)} %bitcast.3.pick_ref, bf16[256,2560]{1,0:T(8,128)(2,1)} %query.3, bf16[8,2,32,640]{3,2,1,0:T(8,128)(2,1)S(1)} %bitcast.20, bf16[8,2,32,640]{3,2,1,0:T(8,128)(2,1)S(1)} %bitcast.23, bf16[8,2,32,640]{3,2,1,0:T(8,128)(2,1)S(1)} %bitcast.24, bf16[8,2,32,640]{3,2,1,0:T(8,128)(2,1)} %bitcast.7.refs_3_, ...), custom_call_target="tpu_custom_call" | custom-call | flops 1342177280 | bytes 12000000 | tf_op jit(solution)/shard_map/cross/pallas_call | solution.py:413
  (88 shorter events, 35.6 us)
Async XLA Ops:
  2.8 24.5 %collective-permute-start.3 = (bf16[512,640]{1,0:T(8,128)(2,1)}, bf16[512,640]{1,0:T(8,128)(2,1)}, u32[]{:S(2)}, u32[]{:S(2)}) collective-permute-start(bf16[512,640]{1,0:T(8,128)(2,1)} %prompt.1.refs_0_), channel_id=1, source_target_pairs={{0,4},{1,5},{2,6},{3,7},{4,8},{5,9},{6,10},{7,11},{8,12},{9,13},{1... | collective-permute-start | bytes 1966088 | tf_op jit(solution)/shard_map/ppermute | solution.py:493
  10.9 30.1 %collective-permute-start.2 = (bf16[640,640]{1,0:T(8,128)(2,1)}, bf16[640,640]{1,0:T(8,128)(2,1)}, u32[]{:S(2)}, u32[]{:S(2)}) collective-permute-start(bf16[640,640]{1,0:T(8,128)(2,1)} %send_c.1.refs_2_), channel_id=1, source_target_pairs={{0,4},{1,5},{2,6},{3,7},{4,8},{5,9},{6,10},{7,11},{16,20},{17,21},... | collective-permute-start | bytes 2457608 | tf_op jit(solution)/shard_map/ppermute | solution.py:493
  15.8 22.1 %collective-permute-start.1 = (bf16[512,640]{1,0:T(8,128)(2,1)}, bf16[512,640]{1,0:T(8,128)(2,1)S(1)}, u32[]{:S(2)}, u32[]{:S(2)}) collective-permute-start(bf16[512,640]{1,0:T(8,128)(2,1)} %send_b.1.refs_2_), channel_id=1, source_target_pairs={{12,8},{13,9},{14,10},{15,11},{8,4},{9,5},{10,6},{11,7},{4,0},{5,1... | collective-permute-start | bytes 1966088 | tf_op jit(solution)/shard_map/ppermute | solution.py:493
  18.1 29.9 %collective-permute-start = (bf16[512,640]{1,0:T(8,128)(2,1)}, bf16[512,640]{1,0:T(8,128)(2,1)}, u32[]{:S(2)}, u32[]{:S(2)}) collective-permute-start(bf16[512,640]{1,0:T(8,128)(2,1)} %send_d.1._), channel_id=1, source_target_pairs={{12,4},{13,5},{14,6},{15,7},{4,0},{5,1},{6,2},{7,3},{28,20},{29,21... | collective-permute-start | bytes 1966088 | tf_op jit(solution)/shard_map/ppermute | solution.py:493
  30.3 28.5 %collective-permute-start.6 = (bf16[512,640]{1,0:T(8,128)(2,1)}, bf16[512,640]{1,0:T(8,128)(2,1)}, u32[]{:S(2)}, u32[]{:S(2)}) collective-permute-start(bf16[512,640]{1,0:T(8,128)(2,1)} %send_f.1.refs_2_), channel_id=1, source_target_pairs={{12,8},{13,9},{14,10},{15,11},{8,4},{9,5},{10,6},{11,7},{28,24},{2... | collective-permute-start | bytes 1966088 | tf_op jit(solution)/shard_map/ppermute | solution.py:493
  31.8 29.4 %collective-permute-start.5 = (bf16[640,640]{1,0:T(8,128)(2,1)}, bf16[640,640]{1,0:T(8,128)(2,1)}, u32[]{:S(2)}, u32[]{:S(2)}) collective-permute-start(bf16[640,640]{1,0:T(8,128)(2,1)} %send_e.1.refs_2_), channel_id=1, source_target_pairs={{0,4},{1,5},{2,6},{3,7},{4,8},{5,9},{6,10},{7,11},{8,12},{9,13},{1... | collective-permute-start | bytes 2457608 | tf_op jit(solution)/shard_map/ppermute | solution.py:493
  37.9 38.6 %collective-permute-start.19 = (bf16[512,640]{1,0:T(8,128)(2,1)S(1)}, bf16[512,640]{1,0:T(8,128)(2,1)S(1)}, u32[]{:S(2)}, u32[]{:S(2)}) collective-permute-start(bf16[512,640]{1,0:T(8,128)(2,1)S(1)} %copy-done), channel_id=1, source_target_pairs={{0,2},{1,3},{2,0},{3,1},{4,6},{5,7},{6,4},{7,5},{8,10},{9,11},{10,... | collective-permute-start | bytes 1966088 | tf_op jit(solution)/shard_map/ppermute | solution.py:497
  41.0 35.4 %collective-permute-start.20 = (bf16[512,640]{1,0:T(8,128)(2,1)S(1)}, bf16[512,640]{1,0:T(8,128)(2,1)S(1)}, u32[]{:S(2)}, u32[]{:S(2)}) collective-permute-start(bf16[512,640]{1,0:T(8,128)(2,1)S(1)} %copy-done), channel_id=1, source_target_pairs={{0,1},{1,0},{2,3},{3,2},{4,5},{5,4},{6,7},{7,6},{8,9},{9,8},{10,11... | collective-permute-start | bytes 1966088 | tf_op jit(solution)/shard_map/ppermute | solution.py:497
  48.0 31.3 %collective-permute-start.12 = (bf16[640,640]{1,0:T(8,128)(2,1)}, bf16[640,640]{1,0:T(8,128)(2,1)}, u32[]{:S(2)}, u32[]{:S(2)}) collective-permute-start(bf16[640,640]{1,0:T(8,128)(2,1)} %send_g.1.refs_2_), channel_id=1, source_target_pairs={{0,4},{1,5},{2,6},{3,7},{4,8},{5,9},{6,10},{7,11},{16,20},{17,21},... | collective-permute-start | bytes 2457608 | tf_op jit(solution)/shard_map/ppermute | solution.py:493
  58.8 19.0 %collective-permute-start.4 = (bf16[512,640]{1,0:T(8,128)(2,1)}, bf16[512,640]{1,0:T(8,128)(2,1)}, u32[]{:S(2)}, u32[]{:S(2)}) collective-permute-start(bf16[512,640]{1,0:T(8,128)(2,1)} %send_i.1.refs_3_), channel_id=1, source_target_pairs={{12,8},{13,9},{14,10},{15,11},{8,4},{9,5},{10,6},{11,7},{28,24},{2... | collective-permute-start | bytes 1966088 | tf_op jit(solution)/shard_map/ppermute | solution.py:493
  63.4 34.4 %collective-permute-start.13 = (bf16[640,640]{1,0:T(8,128)(2,1)}, bf16[640,640]{1,0:T(8,128)(2,1)}, u32[]{:S(2)}, u32[]{:S(2)}) collective-permute-start(bf16[640,640]{1,0:T(8,128)(2,1)} %get-tuple-element.230.refs_2_), channel_id=1, source_target_pairs={{0,4},{1,5},{2,6},{3,7},{4,8},{5,9},{6,10},{7,11},{8,12},{9,13},{1... | collective-permute-start | bytes 2457608 | tf_op jit(solution)/shard_map/ppermute | solution.py:493
  76.5 19.7 %collective-permute-start.9 = (bf16[512,640]{1,0:T(8,128)(2,1)}, bf16[512,640]{1,0:T(8,128)(2,1)}, u32[]{:S(2)}, u32[]{:S(2)}) collective-permute-start(bf16[512,640]{1,0:T(8,128)(2,1)} %send_k.1), channel_id=1, source_target_pairs={{12,8},{13,9},{14,10},{15,11},{8,4},{9,5},{10,6},{11,7},{4,0},{5,1... | collective-permute-start | bytes 1966088 | tf_op jit(solution)/shard_map/ppermute | solution.py:493
  77.8 24.4 %collective-permute-start.21 = (bf16[512,640]{1,0:T(8,128)(2,1)S(1)}, bf16[512,640]{1,0:T(8,128)(2,1)}, u32[]{:S(2)}, u32[]{:S(2)}) collective-permute-start(bf16[512,640]{1,0:T(8,128)(2,1)S(1)} %collective-permute-done.19), channel_id=1, source_target_pairs={{0,1},{1,0},{2,3},{3,2},{4,5},{5,4},{6,7},{7,6},{8,9},{9,8},{10,11... | collective-permute-start | bytes 1966088 | tf_op jit(solution)/shard_map/ppermute | solution.py:497
  79.3 30.6 %collective-permute-start.7 = (bf16[512,640]{1,0:T(8,128)(2,1)}, bf16[512,640]{1,0:T(8,128)(2,1)}, u32[]{:S(2)}, u32[]{:S(2)}) collective-permute-start(bf16[512,640]{1,0:T(8,128)(2,1)} %send_l.1), channel_id=1, source_target_pairs={{8,4},{9,5},{10,6},{11,7},{4,0},{5,1},{6,2},{7,3},{24,20},{25,21},... | collective-permute-start | bytes 1966088 | tf_op jit(solution)/shard_map/ppermute | solution.py:493
  80.7 34.1 %collective-permute-start.14 = (bf16[544,640]{1,0:T(8,128)(2,1)}, bf16[544,640]{1,0:T(8,128)(2,1)}, u32[]{:S(2)}, u32[]{:S(2)}) collective-permute-start(bf16[544,640]{1,0:T(8,128)(2,1)} %get-tuple-element.231.refs_4_), channel_id=1, source_target_pairs={{4,8},{5,9},{6,10},{7,11},{8,12},{9,13},{10,14},{11,15},{20,24},{2... | collective-permute-start | bytes 2088968 | tf_op jit(solution)/shard_map/ppermute | solution.py:493
  96.2 17.2 %collective-permute-start.22 = (bf16[512,640]{1,0:T(8,128)(2,1)S(1)}, bf16[512,640]{1,0:T(8,128)(2,1)}, u32[]{:S(2)}, u32[]{:S(2)}) collective-permute-start(bf16[512,640]{1,0:T(8,128)(2,1)S(1)} %copy-done.1), channel_id=1, source_target_pairs={{0,2},{1,3},{2,0},{3,1},{4,6},{5,7},{6,4},{7,5},{8,10},{9,11},{10,... | collective-permute-start | bytes 1966088 | tf_op jit(solution)/shard_map/ppermute | solution.py:497
  97.7 17.6 %collective-permute-start.10 = (bf16[512,640]{1,0:T(8,128)(2,1)}, bf16[512,640]{1,0:T(8,128)(2,1)}, u32[]{:S(2)}, u32[]{:S(2)}) collective-permute-start(bf16[512,640]{1,0:T(8,128)(2,1)} %collective-permute-done.9.refs_0_), channel_id=1, source_target_pairs={{8,4},{9,5},{10,6},{11,7},{24,20},{25,21},{26,22},{27,23}} | collective-permute-start | bytes 1966088 | tf_op jit(solution)/shard_map/ppermute | solution.py:493
  109.9 18.0 %collective-permute-start.24 = (bf16[512,640]{1,0:T(8,128)(2,1)}, bf16[512,640]{1,0:T(8,128)(2,1)}, u32[]{:S(2)}, u32[]{:S(2)}) collective-permute-start(bf16[512,640]{1,0:T(8,128)(2,1)} %third_shard.1), channel_id=1, source_target_pairs={{0,2},{1,3},{2,0},{3,1},{4,6},{5,7},{6,4},{7,5},{8,10},{9,11},{10,... | collective-permute-start | bytes 1966088 | tf_op jit(solution)/shard_map/ppermute | solution.py:497
  113.4 21.8 %collective-permute-start.8 = (bf16[512,640]{1,0:T(8,128)(2,1)}, bf16[512,640]{1,0:T(8,128)(2,1)}, u32[]{:S(2)}, u32[]{:S(2)}) collective-permute-start(bf16[512,640]{1,0:T(8,128)(2,1)} %collective-permute-done.7.refs_0_), channel_id=1, source_target_pairs={{4,0},{5,1},{6,2},{7,3},{20,16},{21,17},{22,18},{23,19}} | collective-permute-start | bytes 1966088 | tf_op jit(solution)/shard_map/ppermute | solution.py:493
  114.7 25.8 %collective-permute-start.27 = (bf16[512,640]{1,0:T(8,128)(2,1)}, bf16[512,640]{1,0:T(8,128)(2,1)}, u32[]{:S(2)}, u32[]{:S(2)}) collective-permute-start(bf16[512,640]{1,0:T(8,128)(2,1)} %last_shard.1), channel_id=1, source_target_pairs={{0,2},{1,3},{2,0},{3,1},{4,6},{5,7},{6,4},{7,5},{8,10},{9,11},{10,... | collective-permute-start | bytes 1966088 | tf_op jit(solution)/shard_map/ppermute | solution.py:497
  115.3 32.0 %collective-permute-start.11 = (bf16[512,640]{1,0:T(8,128)(2,1)}, bf16[512,640]{1,0:T(8,128)(2,1)}, u32[]{:S(2)}, u32[]{:S(2)}) collective-permute-start(bf16[512,640]{1,0:T(8,128)(2,1)} %collective-permute-done.10), channel_id=1, source_target_pairs={{4,0},{5,1},{6,2},{7,3},{20,16},{21,17},{22,18},{23,19}} | collective-permute-start | bytes 1966088 | tf_op jit(solution)/shard_map/ppermute | solution.py:493
  127.8 19.5 %collective-permute-start.18 = (bf16[272,640]{1,0:T(8,128)(2,1)}, bf16[272,640]{1,0:T(8,128)(2,1)}, u32[]{:S(2)}, u32[]{:S(2)}) collective-permute-start(bf16[272,640]{1,0:T(8,128)(2,1)} %get-tuple-element.234), channel_id=1, source_target_pairs={{8,12},{9,13},{10,14},{11,15},{24,28},{25,29},{26,30},{27,31}} | collective-permute-start | bytes 1044488 | tf_op jit(solution)/shard_map/ppermute | solution.py:493
  129.2 27.7 %collective-permute-start.23 = (bf16[512,640]{1,0:T(8,128)(2,1)}, bf16[512,640]{1,0:T(8,128)(2,1)}, u32[]{:S(2)}, u32[]{:S(2)}) collective-permute-start(bf16[512,640]{1,0:T(8,128)(2,1)} %collective-permute-done.22), channel_id=1, source_target_pairs={{0,1},{1,0},{2,3},{3,2},{4,5},{5,4},{6,7},{7,6},{8,9},{9,8},{10,11... | collective-permute-start | bytes 1966088 | tf_op jit(solution)/shard_map/ppermute | solution.py:497
  135.2 21.6 %collective-permute-start.25 = (bf16[512,640]{1,0:T(8,128)(2,1)}, bf16[512,640]{1,0:T(8,128)(2,1)}, u32[]{:S(2)}, u32[]{:S(2)}) collective-permute-start(bf16[512,640]{1,0:T(8,128)(2,1)} %third_shard.1), channel_id=1, source_target_pairs={{0,1},{1,0},{2,3},{3,2},{4,5},{5,4},{6,7},{7,6},{8,9},{9,8},{10,11... | collective-permute-start | bytes 1966088 | tf_op jit(solution)/shard_map/ppermute | solution.py:497
  (18 other events, 209.6 us)

commit v3 on v2

--- a/solution.py
+++ b/solution.py
@@ -396,18 +396,19 @@
         for copy in copies:
             copy.wait()
 
-        def chunk(at, carry):
-            left = pl.multiple_of(at * CW, HDIM)
-            for head in range(PER):
-                cols = pl.ds(head * HDIM, HDIM)
-                here = pl.ds(left + head * HDIM, HDIM)
-                _, total, blended = fresh_state(
-                    query[:, here], held[at, :, cols], held[CHUNKS + at, :, cols]
-                )
-                out[:, here] = (blended / total).astype(jnp.bfloat16)
+        def chunk(step, carry):
+            for head in range(2 * PER):
+                at = 2 * step + head // PER
+                cols = pl.ds(head % PER * HDIM, HDIM)
+                here = pl.ds(pl.multiple_of(2 * step * CW, HDIM) + head * HDIM, HDIM)
+                keys, values = held[at, :, cols], held[CHUNKS + at, :, cols]
+                for row in range(0, frame, frame // 2):
+                    some = pl.ds(row, frame // 2)
+                    _, total, blended = fresh_state(query[some, here], keys, values)
+                    out[some, here] = (blended / total).astype(jnp.bfloat16)
             return carry
 
-        lax.fori_loop(0, CHUNKS, chunk, 0)
+        lax.fori_loop(0, CHUNKS // 2, chunk, 0)
 
     work = HEADS * frame * tokens
     return pl.pallas_call(

time: 167 us -> 166 us (level)
  no operation moved by 1% of the time
where the time goes in v3:
time: 166 us; the launch traced here: 165 us
  starting transfers between devices  64.4 us (39%)
  waiting for transfers between devices  52.8 us (32%)
  Pallas kernels  43.3 us (26%)
  local copies, waits for them, and re-layouts  1.97 us (1%)
  between operations  1.91 us (1%)
    ppermute x18, starting transfers between devices, move(): return lax.ppermute(value, 'span', both)  58.2 us
    ppermute x18, waiting for transfers between devices, move(): return lax.ppermute(value, 'span', both)  37.7 us
    pallas_call x14, Pallas kernels, pack(): pl.pallas_call(kernel, out_shape=jax.ShapeDtypeStruct((rows, CW), jnp.bfl...  20.8 us
    ppermute x12, waiting for transfers between devices, across(): return lax.ppermute(value, 'span', pairs)  15.1 us
    pallas_call x1, Pallas kernels, cross(): pl.pallas_call(kernel, out_shape=jax.ShapeDtypeStruct(queries.shape, jnp....  8.19 us
    pallas_call x1, Pallas kernels, finish(): pl.pallas_call(kernel, out_shape=jax.ShapeDtypeStruct(queries.shape, jnp....  7.48 us
    pallas_call x1, Pallas kernels, home(): pl.pallas_call(kernel, out_shape=jax.ShapeDtypeStruct((frame + STAT, WIDT...  6.84 us
    ppermute x12, starting transfers between devices, across(): return lax.ppermute(value, 'span', pairs)  6.2 us
  transfers between devices with their start and end apart: 30, of which 8 were waited for; matrix products, arithmetic and copies ran while one was open for 0% of the time, Pallas kernels for 20%

profile of v3, /device:TPU:0, one launch (start us, length us, event | category | flops | bytes accessed | tf_op | source)
XLA Modules:
  0.0 165.3 jit_solution(9257353457242683784)
XLA Ops:
  0.7 2.2 %prompt.1.refs_0_ = bf16[512,640]{1,0:T(8,128)(2,1)} custom-call(s32[1]{0:T(128)} %bitcast.1.place_ref, bf16[64,5120]{1,0:T(8,128)(2,1)} %bitcast.44), custom_call_target="tpu_custom_call" | custom-call | bytes 2000000 | tf_op jit(solution)/shard_map/prompt/pallas_call | solution.py:458
  2.8 6.0 %collective-permute-start.3 = (bf16[512,640]{1,0:T(8,128)(2,1)}, bf16[512,640]{1,0:T(8,128)(2,1)}, u32[]{:S(2)}, u32[]{:S(2)}) collective-permute-start(bf16[512,640]{1,0:T(8,128)(2,1)} %prompt.1.refs_0_), channel_id=1, source_target_pairs={{0,4},{1,5},{2,6},{3,7},{4,8},{5,9},{6,10},{7,11},{8,12},{9,13},{1... | collective-permute-start | bytes 1966088 | tf_op jit(solution)/shard_map/ppermute | solution.py:494
  10.9 4.9 %collective-permute-start.2 = (bf16[640,640]{1,0:T(8,128)(2,1)}, bf16[640,640]{1,0:T(8,128)(2,1)}, u32[]{:S(2)}, u32[]{:S(2)}) collective-permute-start(bf16[640,640]{1,0:T(8,128)(2,1)} %send_c.1.refs_2_), channel_id=1, source_target_pairs={{0,4},{1,5},{2,6},{3,7},{4,8},{5,9},{6,10},{7,11},{16,20},{17,21},... | collective-permute-start | bytes 2457608 | tf_op jit(solution)/shard_map/ppermute | solution.py:494
  20.5 6.8 %home.1.refs_3_ = bf16[272,2560]{1,0:T(8,128)(2,1)} custom-call(bf16[256,2560]{1,0:T(8,128)(2,1)S(1)} %copy-done.8, bf16[256,5120]{1,0:T(8,128)(2,1)} %refs_0_.6, bf16[256,5120]{1,0:T(8,128)(2,1)} %refs_0_.6, bf16[64,5120]{1,0:T(8,128)(2,1)S(1)} %bitcast.33, bf16[64,5120]{1,0:T(8,128)(2,1)S(1)} %bitcast.34, bf16[512,640]{1,0:T(8,128)(2,1)S(1)} %copy-done.4), custom_call_target="tpu_custom_call" | custom-call | flops 838860800 | bytes 6000000 | tf_op jit(solution)/shard_map/home/pallas_call | solution.py:229
  27.3 2.0 %send_e.1.refs_2_ = bf16[640,640]{1,0:T(8,128)(2,1)} custom-call(s32[1]{0:T(128)} %bitcast.1.place_ref, bf16[256,5120]{1,0:T(8,128)(2,1)} %refs_0_.6, bf16[64,5120]{1,0:T(8,128)(2,1)S(1)} %bitcast.35, bf16[512,640]{1,0:T(8,128)(2,1)} %collective-permute-done.3.refs_2_.refs_1_, bf16[272,2560]{1,0:T(8,128)(2,1)} %home.1.refs_3_), custom_call_target="tpu_custom_call" | custom-call | bytes 2000000 | tf_op jit(solution)/shard_map/send_e/pallas_call | solution.py:458
  31.8 6.0 %collective-permute-start.5 = (bf16[640,640]{1,0:T(8,128)(2,1)}, bf16[640,640]{1,0:T(8,128)(2,1)}, u32[]{:S(2)}, u32[]{:S(2)}) collective-permute-start(bf16[640,640]{1,0:T(8,128)(2,1)} %send_e.1.refs_2_), channel_id=1, source_target_pairs={{0,4},{1,5},{2,6},{3,7},{4,8},{5,9},{6,10},{7,11},{8,12},{9,13},{1... | collective-permute-start | bytes 2457608 | tf_op jit(solution)/shard_map/ppermute | solution.py:494
  41.0 1.8 %second_shard.1.refs_3_ = bf16[512,640]{1,0:T(8,128)(2,1)} custom-call(s32[1]{0:T(128)} %bitcast.1.place_ref, bf16[512,640]{1,0:T(8,128)(2,1)S(1)} %collective-permute-done.1.refs_0_.refs_2_, bf16[512,640]{1,0:T(8,128)(2,1)} %collective-permute-done.3.refs_2_.refs_1_, bf16[512,640]{1,0:T(8,128)(2,1)} %send_f.1.refs_2_), custom_call_target="tpu_custom_call" | custom-call | bytes 2000000 | tf_op jit(solution)/shard_map/second_shard/pallas_call | solution.py:458
  42.8 2.0 %send_g.1.refs_2_ = bf16[640,640]{1,0:T(8,128)(2,1)} custom-call(s32[1]{0:T(128)} %bitcast.1.place_ref, bf16[256,5120]{1,0:T(8,128)(2,1)} %refs_0_.6, bf16[64,5120]{1,0:T(8,128)(2,1)S(1)} %bitcast.36, bf16[640,640]{1,0:T(8,128)(2,1)} %collective-permute-done.2.refs_2_, bf16[512,640]{1,0:T(8,128)(2,1)} %second_shard.1.refs_3_), custom_call_target="tpu_custom_call" | custom-call | bytes 2000000 | tf_op jit(solution)/shard_map/send_g/pallas_call | solution.py:458
  44.9 3.1 %collective-permute-done = bf16[512,640]{1,0:T(8,128)(2,1)} collective-permute-done((bf16[512,640]{1,0:T(8,128)(2,1)}, bf16[512,640]{1,0:T(8,128)(2,1)}, u32[]{:S(2)}, u32[]{:S(2)}) %collective-permute-start) | collective-permute-done | bytes 655392 | tf_op jit(solution)/shard_map/ppermute | solution.py:494
  48.0 9.9 %collective-permute-start.12 = (bf16[640,640]{1,0:T(8,128)(2,1)}, bf16[640,640]{1,0:T(8,128)(2,1)}, u32[]{:S(2)}, u32[]{:S(2)}) collective-permute-start(bf16[640,640]{1,0:T(8,128)(2,1)} %send_g.1.refs_2_), channel_id=1, source_target_pairs={{0,4},{1,5},{2,6},{3,7},{4,8},{5,9},{6,10},{7,11},{16,20},{17,21},... | collective-permute-start | bytes 2457608 | tf_op jit(solution)/shard_map/ppermute | solution.py:494
  61.3 2.1 %conditional.6 = (bf16[640,640]{1,0:T(8,128)(2,1)}) conditional(s32[]{:T(128)} %clamp.2, (bf16[256,5120]{1,0:T(8,128)(2,1)}, bf16[64,5120]{1,0:T(8,128)(2,1)S(1)}) %tuple.122, (bf16[512,640]{1,0:T(8,128)(2,1)}, bf16[512,640]{1,0:T(8,128)(2,1)}, bf16[256,5120]{1,0:T(8,128)(2,1)}, bf16[64,5120]{1,0:T(8,128)(2,1)S(1)}, ...), branch_computations={%region_0.1_spmd, %region_1.2_spmd, %region_2.3_spmd, %region_3.4_... | conditional | flops 838860800 | bytes 4000008 | solution.py:501
  61.3 2.1 %branch.2 = bf16[640,640]{1,0:T(8,128)(2,1)} custom-call(s32[1]{0:T(128)} %constant.27.clone.place_ref, bf16[256,5120]{1,0:T(8,128)(2,1)} %get-tuple-element.159.refs_0_, bf16[64,5120]{1,0:T(8,128)(2,1)S(1)} %get-tuple-element.160.refs_1_), custom_call_target="tpu_custom_call" | custom-call | bytes 2000000 | tf_op jit(solution)/shard_map/cond/branch_0_fun/branch/pallas_call | solution.py:458
  63.4 13.1 %collective-permute-start.13 = (bf16[640,640]{1,0:T(8,128)(2,1)}, bf16[640,640]{1,0:T(8,128)(2,1)}, u32[]{:S(2)}, u32[]{:S(2)}) collective-permute-start(bf16[640,640]{1,0:T(8,128)(2,1)} %get-tuple-element.230.refs_2_), channel_id=1, source_target_pairs={{0,4},{1,5},{2,6},{3,7},{4,8},{5,9},{6,10},{7,11},{8,12},{9,13},{1... | collective-permute-start | bytes 2457608 | tf_op jit(solution)/shard_map/ppermute | solution.py:494
  82.2 14.0 %collective-permute-done.9.refs_0_ = bf16[512,640]{1,0:T(8,128)(2,1)} collective-permute-done((bf16[512,640]{1,0:T(8,128)(2,1)}, bf16[512,640]{1,0:T(8,128)(2,1)}, u32[]{:S(2)}, u32[]{:S(2)}) %collective-permute-start.9) | collective-permute-done | bytes 655392 | tf_op jit(solution)/shard_map/ppermute | solution.py:494
  99.2 2.0 %third_shard.1 = bf16[512,640]{1,0:T(8,128)(2,1)} custom-call(s32[1]{0:T(128)} %bitcast.1.place_ref, bf16[512,640]{1,0:T(8,128)(2,1)} %collective-permute-done.9.refs_0_, bf16[512,640]{1,0:T(8,128)(2,1)} %collective-permute-done.6.refs_0_.refs_1_, bf16[512,640]{1,0:T(8,128)(2,1)} %copy-done.9, bf16[640,640]{1,0:T(8,128)(2,1)} %collective-permute-done.5.refs_3_.refs_2_, ...), custom_call_target="tpu_custom_call" | custom-call | bytes 2000000 | tf_op jit(solution)/shard_map/third_shard/pallas_call | solution.py:458
  103.8 6.1 %collective-permute-done.7.refs_0_ = bf16[512,640]{1,0:T(8,128)(2,1)} collective-permute-done((bf16[512,640]{1,0:T(8,128)(2,1)}, bf16[512,640]{1,0:T(8,128)(2,1)}, u32[]{:S(2)}, u32[]{:S(2)}) %collective-permute-start.7) | collective-permute-done | bytes 655392 | tf_op jit(solution)/shard_map/ppermute | solution.py:494
  111.4 2.0 %last_shard.1 = bf16[512,640]{1,0:T(8,128)(2,1)} custom-call(s32[1]{0:T(128)} %bitcast.1.place_ref, bf16[512,640]{1,0:T(8,128)(2,1)} %collective-permute-done.7.refs_0_, bf16[512,640]{1,0:T(8,128)(2,1)} %collective-permute-done.4.refs_0_.refs_1_, bf16[640,640]{1,0:T(8,128)(2,1)} %collective-permute-done.5.refs_3_.refs_2_, ...), custom_call_target="tpu_custom_call" | custom-call | bytes 2000000 | tf_op jit(solution)/shard_map/last_shard/pallas_call | solution.py:458
  118.1 9.7 %collective-permute-done.24 = bf16[512,640]{1,0:T(8,128)(2,1)} collective-permute-done((bf16[512,640]{1,0:T(8,128)(2,1)}, bf16[512,640]{1,0:T(8,128)(2,1)}, u32[]{:S(2)}, u32[]{:S(2)}) %collective-permute-start.24) | collective-permute-done | bytes 655392 | tf_op jit(solution)/shard_map/ppermute | solution.py:498
  129.2 6.0 %collective-permute-done.8 = bf16[512,640]{1,0:T(8,128)(2,1)} collective-permute-done((bf16[512,640]{1,0:T(8,128)(2,1)}, bf16[512,640]{1,0:T(8,128)(2,1)}, u32[]{:S(2)}, u32[]{:S(2)}) %collective-permute-start.8) | collective-permute-done | bytes 655392 | tf_op jit(solution)/shard_map/ppermute | solution.py:494
  135.3 5.3 %collective-permute-done.27 = bf16[512,640]{1,0:T(8,128)(2,1)} collective-permute-done((bf16[512,640]{1,0:T(8,128)(2,1)}, bf16[512,640]{1,0:T(8,128)(2,1)}, u32[]{:S(2)}, u32[]{:S(2)}) %collective-permute-start.27) | collective-permute-done | bytes 655392 | tf_op jit(solution)/shard_map/ppermute | solution.py:498
  140.6 6.8 %collective-permute-done.11 = bf16[512,640]{1,0:T(8,128)(2,1)} collective-permute-done((bf16[512,640]{1,0:T(8,128)(2,1)}, bf16[512,640]{1,0:T(8,128)(2,1)}, u32[]{:S(2)}, u32[]{:S(2)}) %collective-permute-start.11) | collective-permute-done | bytes 655392 | tf_op jit(solution)/shard_map/ppermute | solution.py:494
  149.2 7.7 %conditional.11 = (bf16[256,2560]{1,0:T(8,128)(2,1)}) conditional(s32[]{:T(128)} %clamp.2, (bf16[256,2560]{1,0:T(8,128)(2,1)}, bf16[272,2560]{1,0:T(8,128)(2,1)}, bf16[512,640]{1,0:T(8,128)(2,1)}, bf16[512,640]{1,0:T(8,128)(2,1)}, bf16[512,640]{1,0:T(8,128)(2,1)}, /*index=5*/bf16[256,5120]{1,0:T(8,128)(2,1)}, ...), branch_computations={%region_20.21_spmd, %region_21.22_spmd, %region_22.23_spmd, %regio... | conditional | bytes 8 | solution.py:501
  149.2 7.5 %finish.4 = bf16[256,2560]{1,0:T(8,128)(2,1)} custom-call(bf16[256,2560]{1,0:T(8,128)(2,1)} %get-tuple-element.199.refs_0_, bf16[272,2560]{1,0:T(8,128)(2,1)} %get-tuple-element.200.refs_1_, bf16[512,640]{1,0:T(8,128)(2,1)} %get-tuple-element.201.refs_2_.refs_3_, bf16[512,640]{1,0:T(8,128)(2,1)} %get-tuple-element.201.refs_2_.refs_3_, ...), custom_call_target="tpu_custom_call" | custom-call | tf_op jit(solution)/shard_map/cond/branch_0_fun/finish/pallas_call | solution.py:356
  156.9 8.2 %cross.1 = bf16[256,2560]{1,0:T(8,128)(2,1)} custom-call(s32[1]{0:T(128)} %bitcast.3.pick_ref, bf16[256,2560]{1,0:T(8,128)(2,1)} %query.3, bf16[8,2,32,640]{3,2,1,0:T(8,128)(2,1)S(1)} %bitcast.20, bf16[8,2,32,640]{3,2,1,0:T(8,128)(2,1)S(1)} %bitcast.23, bf16[8,2,32,640]{3,2,1,0:T(8,128)(2,1)S(1)} %bitcast.24, bf16[8,2,32,640]{3,2,1,0:T(8,128)(2,1)} %bitcast.7.refs_3_, ...), custom_call_target="tpu_custom_call" | custom-call | flops 1342177280 | bytes 12000000 | tf_op jit(solution)/shard_map/cross/pallas_call | solution.py:414
  (88 shorter events, 35.6 us)
Async XLA Ops:
  2.8 24.5 %collective-permute-start.3 = (bf16[512,640]{1,0:T(8,128)(2,1)}, bf16[512,640]{1,0:T(8,128)(2,1)}, u32[]{:S(2)}, u32[]{:S(2)}) collective-permute-start(bf16[512,640]{1,0:T(8,128)(2,1)} %prompt.1.refs_0_), channel_id=1, source_target_pairs={{0,4},{1,5},{2,6},{3,7},{4,8},{5,9},{6,10},{7,11},{8,12},{9,13},{1... | collective-permute-start | bytes 1966088 | tf_op jit(solution)/shard_map/ppermute | solution.py:494
  10.9 30.1 %collective-permute-start.2 = (bf16[640,640]{1,0:T(8,128)(2,1)}, bf16[640,640]{1,0:T(8,128)(2,1)}, u32[]{:S(2)}, u32[]{:S(2)}) collective-permute-start(bf16[640,640]{1,0:T(8,128)(2,1)} %send_c.1.refs_2_), channel_id=1, source_target_pairs={{0,4},{1,5},{2,6},{3,7},{4,8},{5,9},{6,10},{7,11},{16,20},{17,21},... | collective-permute-start | bytes 2457608 | tf_op jit(solution)/shard_map/ppermute | solution.py:494
  15.8 22.1 %collective-permute-start.1 = (bf16[512,640]{1,0:T(8,128)(2,1)}, bf16[512,640]{1,0:T(8,128)(2,1)S(1)}, u32[]{:S(2)}, u32[]{:S(2)}) collective-permute-start(bf16[512,640]{1,0:T(8,128)(2,1)} %send_b.1.refs_2_), channel_id=1, source_target_pairs={{12,8},{13,9},{14,10},{15,11},{8,4},{9,5},{10,6},{11,7},{4,0},{5,1... | collective-permute-start | bytes 1966088 | tf_op jit(solution)/shard_map/ppermute | solution.py:494
  18.1 29.9 %collective-permute-start = (bf16[512,640]{1,0:T(8,128)(2,1)}, bf16[512,640]{1,0:T(8,128)(2,1)}, u32[]{:S(2)}, u32[]{:S(2)}) collective-permute-start(bf16[512,640]{1,0:T(8,128)(2,1)} %send_d.1._), channel_id=1, source_target_pairs={{12,4},{13,5},{14,6},{15,7},{4,0},{5,1},{6,2},{7,3},{28,20},{29,21... | collective-permute-start | bytes 1966088 | tf_op jit(solution)/shard_map/ppermute | solution.py:494
  30.3 28.5 %collective-permute-start.6 = (bf16[512,640]{1,0:T(8,128)(2,1)}, bf16[512,640]{1,0:T(8,128)(2,1)}, u32[]{:S(2)}, u32[]{:S(2)}) collective-permute-start(bf16[512,640]{1,0:T(8,128)(2,1)} %send_f.1.refs_2_), channel_id=1, source_target_pairs={{12,8},{13,9},{14,10},{15,11},{8,4},{9,5},{10,6},{11,7},{28,24},{2... | collective-permute-start | bytes 1966088 | tf_op jit(solution)/shard_map/ppermute | solution.py:494
  31.8 29.4 %collective-permute-start.5 = (bf16[640,640]{1,0:T(8,128)(2,1)}, bf16[640,640]{1,0:T(8,128)(2,1)}, u32[]{:S(2)}, u32[]{:S(2)}) collective-permute-start(bf16[640,640]{1,0:T(8,128)(2,1)} %send_e.1.refs_2_), channel_id=1, source_target_pairs={{0,4},{1,5},{2,6},{3,7},{4,8},{5,9},{6,10},{7,11},{8,12},{9,13},{1... | collective-permute-start | bytes 2457608 | tf_op jit(solution)/shard_map/ppermute | solution.py:494
  37.9 38.6 %collective-permute-start.19 = (bf16[512,640]{1,0:T(8,128)(2,1)S(1)}, bf16[512,640]{1,0:T(8,128)(2,1)S(1)}, u32[]{:S(2)}, u32[]{:S(2)}) collective-permute-start(bf16[512,640]{1,0:T(8,128)(2,1)S(1)} %copy-done), channel_id=1, source_target_pairs={{0,2},{1,3},{2,0},{3,1},{4,6},{5,7},{6,4},{7,5},{8,10},{9,11},{10,... | collective-permute-start | bytes 1966088 | tf_op jit(solution)/shard_map/ppermute | solution.py:498
  41.0 35.4 %collective-permute-start.20 = (bf16[512,640]{1,0:T(8,128)(2,1)S(1)}, bf16[512,640]{1,0:T(8,128)(2,1)S(1)}, u32[]{:S(2)}, u32[]{:S(2)}) collective-permute-start(bf16[512,640]{1,0:T(8,128)(2,1)S(1)} %copy-done), channel_id=1, source_target_pairs={{0,1},{1,0},{2,3},{3,2},{4,5},{5,4},{6,7},{7,6},{8,9},{9,8},{10,11... | collective-permute-start | bytes 1966088 | tf_op jit(solution)/shard_map/ppermute | solution.py:498
  48.0 31.3 %collective-permute-start.12 = (bf16[640,640]{1,0:T(8,128)(2,1)}, bf16[640,640]{1,0:T(8,128)(2,1)}, u32[]{:S(2)}, u32[]{:S(2)}) collective-permute-start(bf16[640,640]{1,0:T(8,128)(2,1)} %send_g.1.refs_2_), channel_id=1, source_target_pairs={{0,4},{1,5},{2,6},{3,7},{4,8},{5,9},{6,10},{7,11},{16,20},{17,21},... | collective-permute-start | bytes 2457608 | tf_op jit(solution)/shard_map/ppermute | solution.py:494
  58.8 19.0 %collective-permute-start.4 = (bf16[512,640]{1,0:T(8,128)(2,1)}, bf16[512,640]{1,0:T(8,128)(2,1)}, u32[]{:S(2)}, u32[]{:S(2)}) collective-permute-start(bf16[512,640]{1,0:T(8,128)(2,1)} %send_i.1.refs_3_), channel_id=1, source_target_pairs={{12,8},{13,9},{14,10},{15,11},{8,4},{9,5},{10,6},{11,7},{28,24},{2... | collective-permute-start | bytes 1966088 | tf_op jit(solution)/shard_map/ppermute | solution.py:494
  63.4 34.4 %collective-permute-start.13 = (bf16[640,640]{1,0:T(8,128)(2,1)}, bf16[640,640]{1,0:T(8,128)(2,1)}, u32[]{:S(2)}, u32[]{:S(2)}) collective-permute-start(bf16[640,640]{1,0:T(8,128)(2,1)} %get-tuple-element.230.refs_2_), channel_id=1, source_target_pairs={{0,4},{1,5},{2,6},{3,7},{4,8},{5,9},{6,10},{7,11},{8,12},{9,13},{1... | collective-permute-start | bytes 2457608 | tf_op jit(solution)/shard_map/ppermute | solution.py:494
  76.5 19.7 %collective-permute-start.9 = (bf16[512,640]{1,0:T(8,128)(2,1)}, bf16[512,640]{1,0:T(8,128)(2,1)}, u32[]{:S(2)}, u32[]{:S(2)}) collective-permute-start(bf16[512,640]{1,0:T(8,128)(2,1)} %send_k.1), channel_id=1, source_target_pairs={{12,8},{13,9},{14,10},{15,11},{8,4},{9,5},{10,6},{11,7},{4,0},{5,1... | collective-permute-start | bytes 1966088 | tf_op jit(solution)/shard_map/ppermute | solution.py:494
  77.8 24.4 %collective-permute-start.21 = (bf16[512,640]{1,0:T(8,128)(2,1)S(1)}, bf16[512,640]{1,0:T(8,128)(2,1)}, u32[]{:S(2)}, u32[]{:S(2)}) collective-permute-start(bf16[512,640]{1,0:T(8,128)(2,1)S(1)} %collective-permute-done.19), channel_id=1, source_target_pairs={{0,1},{1,0},{2,3},{3,2},{4,5},{5,4},{6,7},{7,6},{8,9},{9,8},{10,11... | collective-permute-start | bytes 1966088 | tf_op jit(solution)/shard_map/ppermute | solution.py:498
  79.3 30.6 %collective-permute-start.7 = (bf16[512,640]{1,0:T(8,128)(2,1)}, bf16[512,640]{1,0:T(8,128)(2,1)}, u32[]{:S(2)}, u32[]{:S(2)}) collective-permute-start(bf16[512,640]{1,0:T(8,128)(2,1)} %send_l.1), channel_id=1, source_target_pairs={{8,4},{9,5},{10,6},{11,7},{4,0},{5,1},{6,2},{7,3},{24,20},{25,21},... | collective-permute-start | bytes 1966088 | tf_op jit(solution)/shard_map/ppermute | solution.py:494
  80.7 34.1 %collective-permute-start.14 = (bf16[544,640]{1,0:T(8,128)(2,1)}, bf16[544,640]{1,0:T(8,128)(2,1)}, u32[]{:S(2)}, u32[]{:S(2)}) collective-permute-start(bf16[544,640]{1,0:T(8,128)(2,1)} %get-tuple-element.231.refs_4_), channel_id=1, source_target_pairs={{4,8},{5,9},{6,10},{7,11},{8,12},{9,13},{10,14},{11,15},{20,24},{2... | collective-permute-start | bytes 2088968 | tf_op jit(solution)/shard_map/ppermute | solution.py:494
  96.2 17.2 %collective-permute-start.22 = (bf16[512,640]{1,0:T(8,128)(2,1)S(1)}, bf16[512,640]{1,0:T(8,128)(2,1)}, u32[]{:S(2)}, u32[]{:S(2)}) collective-permute-start(bf16[512,640]{1,0:T(8,128)(2,1)S(1)} %copy-done.1), channel_id=1, source_target_pairs={{0,2},{1,3},{2,0},{3,1},{4,6},{5,7},{6,4},{7,5},{8,10},{9,11},{10,... | collective-permute-start | bytes 1966088 | tf_op jit(solution)/shard_map/ppermute | solution.py:498
  97.7 17.6 %collective-permute-start.10 = (bf16[512,640]{1,0:T(8,128)(2,1)}, bf16[512,640]{1,0:T(8,128)(2,1)}, u32[]{:S(2)}, u32[]{:S(2)}) collective-permute-start(bf16[512,640]{1,0:T(8,128)(2,1)} %collective-permute-done.9.refs_0_), channel_id=1, source_target_pairs={{8,4},{9,5},{10,6},{11,7},{24,20},{25,21},{26,22},{27,23}} | collective-permute-start | bytes 1966088 | tf_op jit(solution)/shard_map/ppermute | solution.py:494
  109.9 18.0 %collective-permute-start.24 = (bf16[512,640]{1,0:T(8,128)(2,1)}, bf16[512,640]{1,0:T(8,128)(2,1)}, u32[]{:S(2)}, u32[]{:S(2)}) collective-permute-start(bf16[512,640]{1,0:T(8,128)(2,1)} %third_shard.1), channel_id=1, source_target_pairs={{0,2},{1,3},{2,0},{3,1},{4,6},{5,7},{6,4},{7,5},{8,10},{9,11},{10,... | collective-permute-start | bytes 1966088 | tf_op jit(solution)/shard_map/ppermute | solution.py:498
  113.4 21.8 %collective-permute-start.8 = (bf16[512,640]{1,0:T(8,128)(2,1)}, bf16[512,640]{1,0:T(8,128)(2,1)}, u32[]{:S(2)}, u32[]{:S(2)}) collective-permute-start(bf16[512,640]{1,0:T(8,128)(2,1)} %collective-permute-done.7.refs_0_), channel_id=1, source_target_pairs={{4,0},{5,1},{6,2},{7,3},{20,16},{21,17},{22,18},{23,19}} | collective-permute-start | bytes 1966088 | tf_op jit(solution)/shard_map/ppermute | solution.py:494
  114.7 25.8 %collective-permute-start.27 = (bf16[512,640]{1,0:T(8,128)(2,1)}, bf16[512,640]{1,0:T(8,128)(2,1)}, u32[]{:S(2)}, u32[]{:S(2)}) collective-permute-start(bf16[512,640]{1,0:T(8,128)(2,1)} %last_shard.1), channel_id=1, source_target_pairs={{0,2},{1,3},{2,0},{3,1},{4,6},{5,7},{6,4},{7,5},{8,10},{9,11},{10,... | collective-permute-start | bytes 1966088 | tf_op jit(solution)/shard_map/ppermute | solution.py:498
  115.3 32.0 %collective-permute-start.11 = (bf16[512,640]{1,0:T(8,128)(2,1)}, bf16[512,640]{1,0:T(8,128)(2,1)}, u32[]{:S(2)}, u32[]{:S(2)}) collective-permute-start(bf16[512,640]{1,0:T(8,128)(2,1)} %collective-permute-done.10), channel_id=1, source_target_pairs={{4,0},{5,1},{6,2},{7,3},{20,16},{21,17},{22,18},{23,19}} | collective-permute-start | bytes 1966088 | tf_op jit(solution)/shard_map/ppermute | solution.py:494
  127.8 19.5 %collective-permute-start.18 = (bf16[272,640]{1,0:T(8,128)(2,1)}, bf16[272,640]{1,0:T(8,128)(2,1)}, u32[]{:S(2)}, u32[]{:S(2)}) collective-permute-start(bf16[272,640]{1,0:T(8,128)(2,1)} %get-tuple-element.234), channel_id=1, source_target_pairs={{8,12},{9,13},{10,14},{11,15},{24,28},{25,29},{26,30},{27,31}} | collective-permute-start | bytes 1044488 | tf_op jit(solution)/shard_map/ppermute | solution.py:494
  129.2 27.7 %collective-permute-start.23 = (bf16[512,640]{1,0:T(8,128)(2,1)}, bf16[512,640]{1,0:T(8,128)(2,1)}, u32[]{:S(2)}, u32[]{:S(2)}) collective-permute-start(bf16[512,640]{1,0:T(8,128)(2,1)} %collective-permute-done.22), channel_id=1, source_target_pairs={{0,1},{1,0},{2,3},{3,2},{4,5},{5,4},{6,7},{7,6},{8,9},{9,8},{10,11... | collective-permute-start | bytes 1966088 | tf_op jit(solution)/shard_map/ppermute | solution.py:498
  135.2 21.6 %collective-permute-start.25 = (bf16[512,640]{1,0:T(8,128)(2,1)}, bf16[512,640]{1,0:T(8,128)(2,1)}, u32[]{:S(2)}, u32[]{:S(2)}) collective-permute-start(bf16[512,640]{1,0:T(8,128)(2,1)} %third_shard.1), channel_id=1, source_target_pairs={{0,1},{1,0},{2,3},{3,2},{4,5},{5,4},{6,7},{7,6},{8,9},{9,8},{10,11... | collective-permute-start | bytes 1966088 | tf_op jit(solution)/shard_map/ppermute | solution.py:498
  (18 other events, 209.6 us)

commit v4 on v3

--- a/solution.py
+++ b/solution.py
@@ -300,7 +300,11 @@
                 if not keys:
                     out[:, cols] = merge_rows(parts, frame).astype(jnp.bfloat16)
                     continue
-                states = [fresh_state(query[:, cols], stacked(keys), stacked(values))]
+                both = [
+                    fresh_state(query[row : row + frame // 2, cols], stacked(keys), stacked(values))
+                    for row in (0, frame // 2)
+                ]
+                states = [tuple(jnp.concatenate(pair, axis=0) for pair in zip(*both))]
                 for part in parts:
                     states.append(
                         (

time: 166 us -> 171 us (1.030)
  the two profiles are of different devices: /device:TPU:0 before, /device:TPU:13 now
where the time goes in v4:
time: 171 us; the launch traced here: 170 us
  Pallas kernels  75.2 us (44%)
  starting transfers between devices  68.9 us (40%)
  waiting for transfers between devices  21 us (12%)
  local copies, waits for them, and re-layouts  1.97 us (1%)
  between operations  1.93 us (1%)
    ppermute x18, starting transfers between devices, move(): return lax.ppermute(value, 'span', both)  46.3 us
    pallas_call x13, Pallas kernels, pack(): pl.pallas_call(kernel, out_shape=jax.ShapeDtypeStruct((rows, CW), jnp.bfl...  22.9 us
    ppermute x12, starting transfers between devices, across(): return lax.ppermute(value, 'span', pairs)  22.6 us
    pallas_call x3, Pallas kernels, attend(): pl.pallas_call(kernel, out_shape=jax.ShapeDtypeStruct(out_shape, jnp.bflo...  21.9 us
    pallas_call x1, Pallas kernels, finish(): pl.pallas_call(kernel, out_shape=jax.ShapeDtypeStruct(queries.shape, jnp....  15.4 us
    ppermute x18, waiting for transfers between devices, move(): return lax.ppermute(value, 'span', both)  13 us
    pallas_call x1, Pallas kernels, cross(): pl.pallas_call(kernel, out_shape=jax.ShapeDtypeStruct(queries.shape, jnp....  8.22 us
    ppermute x12, waiting for transfers between devices, across(): return lax.ppermute(value, 'span', pairs)  7.96 us
  transfers between devices with their start and end apart: 30, of which 6 were waited for; matrix products, arithmetic and copies ran while one was open for 0% of the time, Pallas kernels for 38%

profile of v4, /device:TPU:13, one launch (start us, length us, event | category | flops | bytes accessed | tf_op | source)
XLA Modules:
  0.0 169.9 jit_solution(13563373842977028957)
XLA Ops:
  2.9 3.5 %collective-permute-start.3 = (bf16[512,640]{1,0:T(8,128)(2,1)}, bf16[512,640]{1,0:T(8,128)(2,1)}, u32[]{:S(2)}, u32[]{:S(2)}) collective-permute-start(bf16[512,640]{1,0:T(8,128)(2,1)} %prompt.1.refs_0_), channel_id=1, source_target_pairs={{0,4},{1,5},{2,6},{3,7},{4,8},{5,9},{6,10},{7,11},{8,12},{9,13},{1... | collective-permute-start | bytes 1966088 | tf_op jit(solution)/shard_map/ppermute | solution.py:498
  9.5 3.3 %collective-permute-start.2 = (bf16[640,640]{1,0:T(8,128)(2,1)}, bf16[640,640]{1,0:T(8,128)(2,1)}, u32[]{:S(2)}, u32[]{:S(2)}) collective-permute-start(bf16[640,640]{1,0:T(8,128)(2,1)} %send_c.1.refs_2_), channel_id=1, source_target_pairs={{0,4},{1,5},{2,6},{3,7},{4,8},{5,9},{6,10},{7,11},{16,20},{17,21},... | collective-permute-start | bytes 2457608 | tf_op jit(solution)/shard_map/ppermute | solution.py:498
  12.8 3.0 %collective-permute-start.1 = (bf16[512,640]{1,0:T(8,128)(2,1)}, bf16[512,640]{1,0:T(8,128)(2,1)S(1)}, u32[]{:S(2)}, u32[]{:S(2)}) collective-permute-start(bf16[512,640]{1,0:T(8,128)(2,1)} %send_b.1.refs_2_), channel_id=1, source_target_pairs={{12,8},{13,9},{14,10},{15,11},{8,4},{9,5},{10,6},{11,7},{4,0},{5,1... | collective-permute-start | bytes 1966088 | tf_op jit(solution)/shard_map/ppermute | solution.py:498
  20.0 6.8 %home.1.refs_3_ = bf16[272,2560]{1,0:T(8,128)(2,1)} custom-call(bf16[256,2560]{1,0:T(8,128)(2,1)S(1)} %copy-done.8, bf16[256,5120]{1,0:T(8,128)(2,1)} %refs_0_.6, bf16[256,5120]{1,0:T(8,128)(2,1)} %refs_0_.6, bf16[64,5120]{1,0:T(8,128)(2,1)S(1)} %bitcast.33, bf16[64,5120]{1,0:T(8,128)(2,1)S(1)} %bitcast.34, bf16[512,640]{1,0:T(8,128)(2,1)S(1)} %copy-done.4), custom_call_target="tpu_custom_call" | custom-call | flops 838860800 | bytes 6000000 | tf_op jit(solution)/shard_map/home/pallas_call | solution.py:229
  31.2 4.0 %collective-permute-start.5 = (bf16[640,640]{1,0:T(8,128)(2,1)}, bf16[640,640]{1,0:T(8,128)(2,1)}, u32[]{:S(2)}, u32[]{:S(2)}) collective-permute-start(bf16[640,640]{1,0:T(8,128)(2,1)} %send_e.1.refs_2_), channel_id=1, source_target_pairs={{0,4},{1,5},{2,6},{3,7},{4,8},{5,9},{6,10},{7,11},{8,12},{9,13},{1... | collective-permute-start | bytes 2457608 | tf_op jit(solution)/shard_map/ppermute | solution.py:498
  35.5 3.0 %collective-permute-done.2.refs_2_ = bf16[640,640]{1,0:T(8,128)(2,1)} collective-permute-done((bf16[640,640]{1,0:T(8,128)(2,1)}, bf16[640,640]{1,0:T(8,128)(2,1)}, u32[]{:S(2)}, u32[]{:S(2)}) %collective-permute-start.2) | collective-permute-done | bytes 819232 | tf_op jit(solution)/shard_map/ppermute | solution.py:498
  38.5 8.9 %collective-permute-start.20 = (bf16[512,640]{1,0:T(8,128)(2,1)S(1)}, bf16[512,640]{1,0:T(8,128)(2,1)S(1)}, u32[]{:S(2)}, u32[]{:S(2)}) collective-permute-start(bf16[512,640]{1,0:T(8,128)(2,1)S(1)} %copy-done), channel_id=1, source_target_pairs={{0,1},{1,0},{2,3},{3,2},{4,5},{5,4},{6,7},{7,6},{8,9},{9,8},{10,11... | collective-permute-start | bytes 1966088 | tf_op jit(solution)/shard_map/ppermute | solution.py:502
  54.5 4.6 %collective-permute-done.6.refs_0_.refs_1_ = bf16[512,640]{1,0:T(8,128)(2,1)} collective-permute-done((bf16[512,640]{1,0:T(8,128)(2,1)}, bf16[512,640]{1,0:T(8,128)(2,1)}, u32[]{:S(2)}, u32[]{:S(2)}) %collective-permute-start.6) | collective-permute-done | bytes 655392 | tf_op jit(solution)/shard_map/ppermute | solution.py:498
  62.6 7.6 %conditional.6 = (bf16[640,640]{1,0:T(8,128)(2,1)}) conditional(s32[]{:T(128)} %clamp.2, (bf16[256,5120]{1,0:T(8,128)(2,1)}, bf16[64,5120]{1,0:T(8,128)(2,1)S(1)}) %tuple.122, (bf16[512,640]{1,0:T(8,128)(2,1)}, bf16[512,640]{1,0:T(8,128)(2,1)}, bf16[256,5120]{1,0:T(8,128)(2,1)}, bf16[64,5120]{1,0:T(8,128)(2,1)S(1)}, ...), branch_computations={%region_0.1_spmd, %region_1.2_spmd, %region_2.3_spmd, %region_3.4_... | conditional | flops 838860800 | bytes 4000008 | solution.py:505
  62.6 7.6 %visit.3 = bf16[640,640]{1,0:T(8,128)(2,1)} custom-call(bf16[512,640]{1,0:T(8,128)(2,1)} %get-tuple-element.161.refs_0_, bf16[512,640]{1,0:T(8,128)(2,1)} %get-tuple-element.162.refs_1_, bf16[256,5120]{1,0:T(8,128)(2,1)} %get-tuple-element.163.refs_2_, bf16[64,5120]{1,0:T(8,128)(2,1)S(1)} %get-tuple-element.164.refs_3_, ...), custom_call_target="tpu_custom_call" | custom-call | flops 838860800 | bytes 4000000 | tf_op jit(solution)/shard_map/cond/branch_1_fun/visit/pallas_call | solution.py:201
  73.3 4.5 %collective-permute-start.9 = (bf16[512,640]{1,0:T(8,128)(2,1)}, bf16[512,640]{1,0:T(8,128)(2,1)}, u32[]{:S(2)}, u32[]{:S(2)}) collective-permute-start(bf16[512,640]{1,0:T(8,128)(2,1)} %send_k.1), channel_id=1, source_target_pairs={{12,8},{13,9},{14,10},{15,11},{8,4},{9,5},{10,6},{11,7},{4,0},{5,1... | collective-permute-start | bytes 1966088 | tf_op jit(solution)/shard_map/ppermute | solution.py:498
  82.5 7.7 %conditional.7 = (bf16[544,640]{1,0:T(8,128)(2,1)}) conditional(s32[]{:T(128)} %clamp.2, bf16[512,640]{1,0:T(8,128)(2,1)} %send_l.1, (bf16[512,640]{1,0:T(8,128)(2,1)}, bf16[512,640]{1,0:T(8,128)(2,1)}, bf16[256,5120]{1,0:T(8,128)(2,1)}, bf16[64,5120]{1,0:T(8,128)(2,1)}, bf16[640,640]{1,0:T(8,128)(2,1)}) %tuple.127, ...), branch_computations={%region_4.5_spmd, %region_5.6_spmd, %region_6.7_spmd, %region_7.8_... | conditional | flops 838860800 | bytes 4000008 | solution.py:505
  82.5 7.7 %visit.4 = bf16[544,640]{1,0:T(8,128)(2,1)} custom-call(bf16[512,640]{1,0:T(8,128)(2,1)} %get-tuple-element.173.refs_0_, bf16[512,640]{1,0:T(8,128)(2,1)} %get-tuple-element.174.refs_1_, bf16[256,5120]{1,0:T(8,128)(2,1)} %get-tuple-element.175.refs_2_, bf16[64,5120]{1,0:T(8,128)(2,1)} %get-tuple-element.176.refs_3_, bf16[640,640]{1,0:T(8,128)(2,1)} %get-tuple-element.177.refs_4_), custom_call_target="tpu_custom_call" | custom-call | flops 838860800 | bytes 4000000 | tf_op jit(solution)/shard_map/cond/branch_1_fun/visit/pallas_call | solution.py:201
  90.2 5.1 %collective-permute-start.14 = (bf16[544,640]{1,0:T(8,128)(2,1)}, bf16[544,640]{1,0:T(8,128)(2,1)}, u32[]{:S(2)}, u32[]{:S(2)}) collective-permute-start(bf16[544,640]{1,0:T(8,128)(2,1)} %get-tuple-element.231.refs_4_), channel_id=1, source_target_pairs={{4,8},{5,9},{6,10},{7,11},{8,12},{9,13},{10,14},{11,15},{20,24},{2... | collective-permute-start | bytes 2088968 | tf_op jit(solution)/shard_map/ppermute | solution.py:498
  98.9 6.7 %conditional.8 = (bf16[544,640]{1,0:T(8,128)(2,1)S(1)}) conditional(s32[]{:T(128)} %clamp.2, bf16[512,640]{1,0:T(8,128)(2,1)} %third_shard.1, (bf16[512,640]{1,0:T(8,128)(2,1)}, bf16[256,5120]{1,0:T(8,128)(2,1)}, bf16[64,5120]{1,0:T(8,128)(2,1)}, bf16[640,640]{1,0:T(8,128)(2,1)}) %tuple.119, ...), branch_computations={%region_8.9_spmd, %region_9.10_spmd, %region_10.11_spmd, %region_1... | conditional | flops 838860800 | bytes 4000008 | solution.py:505
  98.9 6.6 %visit.5 = bf16[544,640]{1,0:T(8,128)(2,1)S(1)} custom-call(bf16[512,640]{1,0:T(8,128)(2,1)} %get-tuple-element.183.refs_0_, bf16[256,5120]{1,0:T(8,128)(2,1)} %get-tuple-element.184.refs_1_, bf16[64,5120]{1,0:T(8,128)(2,1)} %get-tuple-element.185.refs_2_, bf16[640,640]{1,0:T(8,128)(2,1)} %get-tuple-element.186.refs_3_), custom_call_target="tpu_custom_call" | custom-call | flops 838860800 | bytes 4000000 | tf_op jit(solution)/shard_map/cond/branch_1_fun/visit/pallas_call | solution.py:201
  106.4 4.3 %collective-permute-start.15 = (bf16[544,640]{1,0:T(8,128)(2,1)}, bf16[544,640]{1,0:T(8,128)(2,1)}, u32[]{:S(2)}, u32[]{:S(2)}) collective-permute-start(bf16[544,640]{1,0:T(8,128)(2,1)} %copy-done.10), channel_id=1, source_target_pairs={{4,8},{5,9},{6,10},{7,11},{8,12},{9,13},{10,14},{11,15},{20,24},{2... | collective-permute-start | bytes 2088968 | tf_op jit(solution)/shard_map/ppermute | solution.py:498
  116.3 3.6 %collective-permute-done.10 = bf16[512,640]{1,0:T(8,128)(2,1)} collective-permute-done((bf16[512,640]{1,0:T(8,128)(2,1)}, bf16[512,640]{1,0:T(8,128)(2,1)}, u32[]{:S(2)}, u32[]{:S(2)}) %collective-permute-start.10) | collective-permute-done | bytes 655392 | tf_op jit(solution)/shard_map/ppermute | solution.py:498
  127.2 4.3 %collective-permute-start.23 = (bf16[512,640]{1,0:T(8,128)(2,1)}, bf16[512,640]{1,0:T(8,128)(2,1)}, u32[]{:S(2)}, u32[]{:S(2)}) collective-permute-start(bf16[512,640]{1,0:T(8,128)(2,1)} %collective-permute-done.22), channel_id=1, source_target_pairs={{0,1},{1,0},{2,3},{3,2},{4,5},{5,4},{6,7},{7,6},{8,9},{9,8},{10,11... | collective-permute-start | bytes 1966088 | tf_op jit(solution)/shard_map/ppermute | solution.py:502
  132.4 7.4 %collective-permute-done.27 = bf16[512,640]{1,0:T(8,128)(2,1)} collective-permute-done((bf16[512,640]{1,0:T(8,128)(2,1)}, bf16[512,640]{1,0:T(8,128)(2,1)}, u32[]{:S(2)}, u32[]{:S(2)}) %collective-permute-start.27) | collective-permute-done | bytes 655392 | tf_op jit(solution)/shard_map/ppermute | solution.py:502
  139.9 2.3 %collective-permute-start.28 = (bf16[512,640]{1,0:T(8,128)(2,1)}, bf16[512,640]{1,0:T(8,128)(2,1)}, u32[]{:S(2)}, u32[]{:S(2)}) collective-permute-start(bf16[512,640]{1,0:T(8,128)(2,1)} %last_shard.1), channel_id=1, source_target_pairs={{0,1},{1,0},{2,3},{3,2},{4,5},{5,4},{6,7},{7,6},{8,9},{9,8},{10,11... | collective-permute-start | bytes 1966088 | tf_op jit(solution)/shard_map/ppermute | solution.py:502
  145.9 15.6 %conditional.11 = (bf16[256,2560]{1,0:T(8,128)(2,1)}) conditional(s32[]{:T(128)} %clamp.2, (bf16[256,2560]{1,0:T(8,128)(2,1)}, bf16[272,2560]{1,0:T(8,128)(2,1)}, bf16[512,640]{1,0:T(8,128)(2,1)}, bf16[512,640]{1,0:T(8,128)(2,1)}, bf16[512,640]{1,0:T(8,128)(2,1)}, /*index=5*/bf16[256,5120]{1,0:T(8,128)(2,1)}, ...), branch_computations={%region_20.21_spmd, %region_21.22_spmd, %region_22.23_spmd, %regio... | conditional | bytes 8 | solution.py:505
  145.9 15.4 %finish.5 = bf16[256,2560]{1,0:T(8,128)(2,1)} custom-call(bf16[256,2560]{1,0:T(8,128)(2,1)} %get-tuple-element.206.refs_0_, bf16[272,2560]{1,0:T(8,128)(2,1)} %get-tuple-element.207.refs_1_, bf16[512,640]{1,0:T(8,128)(2,1)} %get-tuple-element.208.refs_2_.refs_3_, bf16[512,640]{1,0:T(8,128)(2,1)} %get-tuple-element.208.refs_2_.refs_3_, ...), custom_call_target="tpu_custom_call" | custom-call | tf_op jit(solution)/shard_map/cond/branch_1_fun/finish/pallas_call | solution.py:360
  161.5 8.2 %cross.1 = bf16[256,2560]{1,0:T(8,128)(2,1)} custom-call(s32[1]{0:T(128)} %bitcast.3.pick_ref, bf16[256,2560]{1,0:T(8,128)(2,1)} %query.3, bf16[8,2,32,640]{3,2,1,0:T(8,128)(2,1)S(1)} %bitcast.20, bf16[8,2,32,640]{3,2,1,0:T(8,128)(2,1)S(1)} %bitcast.23, bf16[8,2,32,640]{3,2,1,0:T(8,128)(2,1)S(1)} %bitcast.24, bf16[8,2,32,640]{3,2,1,0:T(8,128)(2,1)} %bitcast.7.refs_3_, ...), custom_call_target="tpu_custom_call" | custom-call | flops 1342177280 | bytes 12000000 | tf_op jit(solution)/shard_map/cross/pallas_call | solution.py:418
  (88 shorter events, 53.7 us)
Async XLA Ops:
  2.9 24.0 %collective-permute-start.3 = (bf16[512,640]{1,0:T(8,128)(2,1)}, bf16[512,640]{1,0:T(8,128)(2,1)}, u32[]{:S(2)}, u32[]{:S(2)}) collective-permute-start(bf16[512,640]{1,0:T(8,128)(2,1)} %prompt.1.refs_0_), channel_id=1, source_target_pairs={{0,4},{1,5},{2,6},{3,7},{4,8},{5,9},{6,10},{7,11},{8,12},{9,13},{1... | collective-permute-start | bytes 1966088 | tf_op jit(solution)/shard_map/ppermute | solution.py:498
  9.5 28.9 %collective-permute-start.2 = (bf16[640,640]{1,0:T(8,128)(2,1)}, bf16[640,640]{1,0:T(8,128)(2,1)}, u32[]{:S(2)}, u32[]{:S(2)}) collective-permute-start(bf16[640,640]{1,0:T(8,128)(2,1)} %send_c.1.refs_2_), channel_id=1, source_target_pairs={{0,4},{1,5},{2,6},{3,7},{4,8},{5,9},{6,10},{7,11},{16,20},{17,21},... | collective-permute-start | bytes 2457608 | tf_op jit(solution)/shard_map/ppermute | solution.py:498
  12.8 22.4 %collective-permute-start.1 = (bf16[512,640]{1,0:T(8,128)(2,1)}, bf16[512,640]{1,0:T(8,128)(2,1)S(1)}, u32[]{:S(2)}, u32[]{:S(2)}) collective-permute-start(bf16[512,640]{1,0:T(8,128)(2,1)} %send_b.1.refs_2_), channel_id=1, source_target_pairs={{12,8},{13,9},{14,10},{15,11},{8,4},{9,5},{10,6},{11,7},{4,0},{5,1... | collective-permute-start | bytes 1966088 | tf_op jit(solution)/shard_map/ppermute | solution.py:498
  17.0 34.7 %collective-permute-start = (bf16[512,640]{1,0:T(8,128)(2,1)}, bf16[512,640]{1,0:T(8,128)(2,1)}, u32[]{:S(2)}, u32[]{:S(2)}) collective-permute-start(bf16[512,640]{1,0:T(8,128)(2,1)} %send_d.1._), channel_id=1, source_target_pairs={{12,4},{13,5},{14,6},{15,7},{4,0},{5,1},{6,2},{7,3},{28,20},{29,21... | collective-permute-start | bytes 1966088 | tf_op jit(solution)/shard_map/ppermute | solution.py:498
  29.9 29.2 %collective-permute-start.6 = (bf16[512,640]{1,0:T(8,128)(2,1)}, bf16[512,640]{1,0:T(8,128)(2,1)}, u32[]{:S(2)}, u32[]{:S(2)}) collective-permute-start(bf16[512,640]{1,0:T(8,128)(2,1)} %send_f.1.refs_2_), channel_id=1, source_target_pairs={{12,8},{13,9},{14,10},{15,11},{8,4},{9,5},{10,6},{11,7},{28,24},{2... | collective-permute-start | bytes 1966088 | tf_op jit(solution)/shard_map/ppermute | solution.py:498
  31.2 31.4 %collective-permute-start.5 = (bf16[640,640]{1,0:T(8,128)(2,1)}, bf16[640,640]{1,0:T(8,128)(2,1)}, u32[]{:S(2)}, u32[]{:S(2)}) collective-permute-start(bf16[640,640]{1,0:T(8,128)(2,1)} %send_e.1.refs_2_), channel_id=1, source_target_pairs={{0,4},{1,5},{2,6},{3,7},{4,8},{5,9},{6,10},{7,11},{8,12},{9,13},{1... | collective-permute-start | bytes 2457608 | tf_op jit(solution)/shard_map/ppermute | solution.py:498
  35.2 36.9 %collective-permute-start.19 = (bf16[512,640]{1,0:T(8,128)(2,1)S(1)}, bf16[512,640]{1,0:T(8,128)(2,1)S(1)}, u32[]{:S(2)}, u32[]{:S(2)}) collective-permute-start(bf16[512,640]{1,0:T(8,128)(2,1)S(1)} %copy-done), channel_id=1, source_target_pairs={{0,2},{1,3},{2,0},{3,1},{4,6},{5,7},{6,4},{7,5},{8,10},{9,11},{10,... | collective-permute-start | bytes 1966088 | tf_op jit(solution)/shard_map/ppermute | solution.py:502
  38.5 34.8 %collective-permute-start.20 = (bf16[512,640]{1,0:T(8,128)(2,1)S(1)}, bf16[512,640]{1,0:T(8,128)(2,1)S(1)}, u32[]{:S(2)}, u32[]{:S(2)}) collective-permute-start(bf16[512,640]{1,0:T(8,128)(2,1)S(1)} %copy-done), channel_id=1, source_target_pairs={{0,1},{1,0},{2,3},{3,2},{4,5},{5,4},{6,7},{7,6},{8,9},{9,8},{10,11... | collective-permute-start | bytes 1966088 | tf_op jit(solution)/shard_map/ppermute | solution.py:502
  51.7 28.9 %collective-permute-start.12 = (bf16[640,640]{1,0:T(8,128)(2,1)}, bf16[640,640]{1,0:T(8,128)(2,1)}, u32[]{:S(2)}, u32[]{:S(2)}) collective-permute-start(bf16[640,640]{1,0:T(8,128)(2,1)} %send_g.1.refs_2_), channel_id=1, source_target_pairs={{0,4},{1,5},{2,6},{3,7},{4,8},{5,9},{6,10},{7,11},{16,20},{17,21},... | collective-permute-start | bytes 2457608 | tf_op jit(solution)/shard_map/ppermute | solution.py:498
  59.1 18.6 %collective-permute-start.4 = (bf16[512,640]{1,0:T(8,128)(2,1)}, bf16[512,640]{1,0:T(8,128)(2,1)}, u32[]{:S(2)}, u32[]{:S(2)}) collective-permute-start(bf16[512,640]{1,0:T(8,128)(2,1)} %send_i.1.refs_3_), channel_id=1, source_target_pairs={{12,8},{13,9},{14,10},{15,11},{8,4},{9,5},{10,6},{11,7},{28,24},{2... | collective-permute-start | bytes 1966088 | tf_op jit(solution)/shard_map/ppermute | solution.py:498
  70.2 25.4 %collective-permute-start.13 = (bf16[640,640]{1,0:T(8,128)(2,1)}, bf16[640,640]{1,0:T(8,128)(2,1)}, u32[]{:S(2)}, u32[]{:S(2)}) collective-permute-start(bf16[640,640]{1,0:T(8,128)(2,1)} %get-tuple-element.230.refs_2_), channel_id=1, source_target_pairs={{0,4},{1,5},{2,6},{3,7},{4,8},{5,9},{6,10},{7,11},{8,12},{9,13},{1... | collective-permute-start | bytes 2457608 | tf_op jit(solution)/shard_map/ppermute | solution.py:498
  73.3 22.0 %collective-permute-start.9 = (bf16[512,640]{1,0:T(8,128)(2,1)}, bf16[512,640]{1,0:T(8,128)(2,1)}, u32[]{:S(2)}, u32[]{:S(2)}) collective-permute-start(bf16[512,640]{1,0:T(8,128)(2,1)} %send_k.1), channel_id=1, source_target_pairs={{12,8},{13,9},{14,10},{15,11},{8,4},{9,5},{10,6},{11,7},{4,0},{5,1... | collective-permute-start | bytes 1966088 | tf_op jit(solution)/shard_map/ppermute | solution.py:498
  77.8 28.6 %collective-permute-start.21 = (bf16[512,640]{1,0:T(8,128)(2,1)S(1)}, bf16[512,640]{1,0:T(8,128)(2,1)}, u32[]{:S(2)}, u32[]{:S(2)}) collective-permute-start(bf16[512,640]{1,0:T(8,128)(2,1)S(1)} %collective-permute-done.19), channel_id=1, source_target_pairs={{0,1},{1,0},{2,3},{3,2},{4,5},{5,4},{6,7},{7,6},{8,9},{9,8},{10,11... | collective-permute-start | bytes 1966088 | tf_op jit(solution)/shard_map/ppermute | solution.py:502
  80.6 30.1 %collective-permute-start.7 = (bf16[512,640]{1,0:T(8,128)(2,1)}, bf16[512,640]{1,0:T(8,128)(2,1)}, u32[]{:S(2)}, u32[]{:S(2)}) collective-permute-start(bf16[512,640]{1,0:T(8,128)(2,1)} %send_l.1), channel_id=1, source_target_pairs={{8,4},{9,5},{10,6},{11,7},{4,0},{5,1},{6,2},{7,3},{24,20},{25,21},... | collective-permute-start | bytes 1966088 | tf_op jit(solution)/shard_map/ppermute | solution.py:498
  90.2 25.9 %collective-permute-start.14 = (bf16[544,640]{1,0:T(8,128)(2,1)}, bf16[544,640]{1,0:T(8,128)(2,1)}, u32[]{:S(2)}, u32[]{:S(2)}) collective-permute-start(bf16[544,640]{1,0:T(8,128)(2,1)} %get-tuple-element.231.refs_4_), channel_id=1, source_target_pairs={{4,8},{5,9},{6,10},{7,11},{8,12},{9,13},{10,14},{11,15},{20,24},{2... | collective-permute-start | bytes 2088968 | tf_op jit(solution)/shard_map/ppermute | solution.py:498
  95.3 18.7 %collective-permute-start.22 = (bf16[512,640]{1,0:T(8,128)(2,1)S(1)}, bf16[512,640]{1,0:T(8,128)(2,1)}, u32[]{:S(2)}, u32[]{:S(2)}) collective-permute-start(bf16[512,640]{1,0:T(8,128)(2,1)S(1)} %copy-done.1), channel_id=1, source_target_pairs={{0,2},{1,3},{2,0},{3,1},{4,6},{5,7},{6,4},{7,5},{8,10},{9,11},{10,... | collective-permute-start | bytes 1966088 | tf_op jit(solution)/shard_map/ppermute | solution.py:502
  95.5 24.4 %collective-permute-start.10 = (bf16[512,640]{1,0:T(8,128)(2,1)}, bf16[512,640]{1,0:T(8,128)(2,1)}, u32[]{:S(2)}, u32[]{:S(2)}) collective-permute-start(bf16[512,640]{1,0:T(8,128)(2,1)} %collective-permute-done.9.refs_0_), channel_id=1, source_target_pairs={{8,4},{9,5},{10,6},{11,7},{24,20},{25,21},{26,22},{27,23}} | collective-permute-start | bytes 1966088 | tf_op jit(solution)/shard_map/ppermute | solution.py:498
  116.1 23.7 %collective-permute-start.27 = (bf16[512,640]{1,0:T(8,128)(2,1)}, bf16[512,640]{1,0:T(8,128)(2,1)}, u32[]{:S(2)}, u32[]{:S(2)}) collective-permute-start(bf16[512,640]{1,0:T(8,128)(2,1)} %last_shard.1), channel_id=1, source_target_pairs={{0,2},{1,3},{2,0},{3,1},{4,6},{5,7},{6,4},{7,5},{8,10},{9,11},{10,... | collective-permute-start | bytes 1966088 | tf_op jit(solution)/shard_map/ppermute | solution.py:502
  119.9 22.3 %collective-permute-start.11 = (bf16[512,640]{1,0:T(8,128)(2,1)}, bf16[512,640]{1,0:T(8,128)(2,1)}, u32[]{:S(2)}, u32[]{:S(2)}) collective-permute-start(bf16[512,640]{1,0:T(8,128)(2,1)} %collective-permute-done.10), channel_id=1, source_target_pairs={{4,0},{5,1},{6,2},{7,3},{20,16},{21,17},{22,18},{23,19}} | collective-permute-start | bytes 1966088 | tf_op jit(solution)/shard_map/ppermute | solution.py:498
  125.8 18.7 %collective-permute-start.18 = (bf16[272,640]{1,0:T(8,128)(2,1)}, bf16[272,640]{1,0:T(8,128)(2,1)}, u32[]{:S(2)}, u32[]{:S(2)}) collective-permute-start(bf16[272,640]{1,0:T(8,128)(2,1)} %get-tuple-element.234), channel_id=1, source_target_pairs={{8,12},{9,13},{10,14},{11,15},{24,28},{25,29},{26,30},{27,31}} | collective-permute-start | bytes 1044488 | tf_op jit(solution)/shard_map/ppermute | solution.py:498
  127.2 34.2 %collective-permute-start.23 = (bf16[512,640]{1,0:T(8,128)(2,1)}, bf16[512,640]{1,0:T(8,128)(2,1)}, u32[]{:S(2)}, u32[]{:S(2)}) collective-permute-start(bf16[512,640]{1,0:T(8,128)(2,1)} %collective-permute-done.22), channel_id=1, source_target_pairs={{0,1},{1,0},{2,3},{3,2},{4,5},{5,4},{6,7},{7,6},{8,9},{9,8},{10,11... | collective-permute-start | bytes 1966088 | tf_op jit(solution)/shard_map/ppermute | solution.py:502
  131.5 30.0 %collective-permute-start.25 = (bf16[512,640]{1,0:T(8,128)(2,1)}, bf16[512,640]{1,0:T(8,128)(2,1)}, u32[]{:S(2)}, u32[]{:S(2)}) collective-permute-start(bf16[512,640]{1,0:T(8,128)(2,1)} %third_shard.1), channel_id=1, source_target_pairs={{0,1},{1,0},{2,3},{3,2},{4,5},{5,4},{6,7},{7,6},{8,9},{9,8},{10,11... | collective-permute-start | bytes 1966088 | tf_op jit(solution)/shard_map/ppermute | solution.py:502
  139.9 21.6 %collective-permute-start.28 = (bf16[512,640]{1,0:T(8,128)(2,1)}, bf16[512,640]{1,0:T(8,128)(2,1)}, u32[]{:S(2)}, u32[]{:S(2)}) collective-permute-start(bf16[512,640]{1,0:T(8,128)(2,1)} %last_shard.1), channel_id=1, source_target_pairs={{0,1},{1,0},{2,3},{3,2},{4,5},{5,4},{6,7},{7,6},{8,9},{9,8},{10,11... | collective-permute-start | bytes 1966088 | tf_op jit(solution)/shard_map/ppermute | solution.py:502
  142.2 19.3 %collective-permute-start.26 = (bf16[512,640]{1,0:T(8,128)(2,1)}, bf16[512,640]{1,0:T(8,128)(2,1)}, u32[]{:S(2)}, u32[]{:S(2)}) collective-permute-start(bf16[512,640]{1,0:T(8,128)(2,1)} %collective-permute-done.24), channel_id=1, source_target_pairs={{0,1},{1,0},{2,3},{3,2},{4,5},{5,4},{6,7},{7,6},{8,9},{9,8},{10,11... | collective-permute-start | bytes 1966088 | tf_op jit(solution)/shard_map/ppermute | solution.py:502
  (18 other events, 206.6 us)
